TPU v7x, 32 devices: a whole 2x2x4 slice. The times are simulated.
32 devices in a mesh: expert: 4 (over x, core), seq: 2 (over y), tensor: 4 (over z).
Axes of the slice: x: 2, y: 2, z: 4, core: 2. Of those that a mesh axis runs over, the one named last changes fastest.
Arguments:
- tokens_in: bfloat16 [128, 6144], P(('expert', 'seq'), 'tensor'), may hold values from -6 to 6
- out_grad: bfloat16 [128, 6144], P(('expert', 'seq'), 'tensor'), may hold values from -6 to 6
- route_ids: int32 [128, 2], P(('expert', 'seq')), may hold values from 0 to 3, all different within a row; in each aligned block of 16 rows (0 to 15, 16 to 31, ...) at most 16 rows name the same one
- route_weight: bfloat16 [128, 2], P(('expert', 'seq')), may hold values from 0.099609375 to 1
- gate_weight: bfloat16 [4, 6144, 8192], P('expert', None, ('seq', 'tensor')), may hold values from -0.078125 to 0.078125
- up_weight: bfloat16 [4, 6144, 8192], P('expert', None, ('seq', 'tensor')), may hold values from -0.078125 to 0.078125
- down_weight: bfloat16 [4, 8192, 6144], P('expert', ('seq', 'tensor')), may hold values from -0.0625 to 0.0625
Outputs:
- x_grad: bfloat16 [128, 6144], P(('expert', 'seq'), 'tensor')
- route_grad: bfloat16 [128, 2], P(('expert', 'seq'))
- gate_grad: bfloat16 [4, 6144, 8192], P('expert', None, ('seq', 'tensor'))
- up_grad: bfloat16 [4, 6144, 8192], P('expert', None, ('seq', 'tensor'))
- down_grad: bfloat16 [4, 8192, 6144], P('expert', ('seq', 'tensor'))
Inputs may be any that keep to these rules, and one draw needn't show every extreme that they name: `route_ids`: each token names two different experts, and every expert is named by some token.
All inputs are finite; a program needn't handle non-finite values.
Results may differ from a plain program's by a relative error of at most 0.0059.
Values may be sent and summed in bfloat16 or wider, within the bound.
No kernel may reach another device: no remote copies, remote signals or barrier semaphores. Data moves between devices by JAX's collectives and lax.ppermute only.
A program may use at most 192 MiB of HBM per device.

v0:
```python
import jax
import jax.numpy as jnp
from jax import lax
from jax.sharding import PartitionSpec as P


def per_device(tokens_in, out_grad, route_ids, route_weight, gate_weight, up_weight, down_weight):
    experts = lax.axis_size("expert")
    shard_rows = tokens_in.shape[0]
    feature_count = tokens_in.shape[1]
    slot_count = experts * shard_rows
    contract_rows = (((0,), (0,)), ((), ()))
    contract_cols = (((1,), (1,)), ((), ()))
    flat_ids = route_ids.reshape(-1)
    choose = (flat_ids[:, None] == jnp.arange(experts, dtype=jnp.int32)[None, :]).astype(jnp.int32)
    earlier = jnp.cumsum(choose, axis=0) - choose
    position = jnp.sum(earlier * choose, axis=1)
    target = flat_ids * shard_rows + position
    placed = (target[:, None] == jnp.arange(slot_count, dtype=jnp.int32)[None, :]).astype(
        jnp.float32
    )
    placed = placed.reshape(shard_rows, 2, slot_count)
    dispatch = jnp.sum(placed, axis=1).astype(jnp.bfloat16)
    send_rows = jnp.einsum("ts,td->sd", dispatch, tokens_in, preferred_element_type=jnp.float32)
    send_rows = send_rows.astype(jnp.bfloat16).reshape(experts, shard_rows, feature_count)
    send_grads = jnp.einsum("ts,td->sd", dispatch, out_grad, preferred_element_type=jnp.float32)
    send_grads = send_grads.astype(jnp.bfloat16).reshape(experts, shard_rows, feature_count)
    send_weight = jnp.einsum("tks,tk->s", placed, route_weight.astype(jnp.float32))
    send_weight = send_weight.astype(jnp.bfloat16).reshape(experts, shard_rows)
    recv_rows, recv_grads, recv_weight = (
        lax.all_to_all(send_rows, "expert", split_axis=0, concat_axis=0, tiled=True),
        lax.all_to_all(send_grads, "expert", split_axis=0, concat_axis=0, tiled=True),
        lax.all_to_all(send_weight, "expert", split_axis=0, concat_axis=0, tiled=True),
    )
    full_rows, full_grads = (
        lax.all_gather(recv_rows, "tensor", axis=2, tiled=True),
        lax.all_gather(recv_grads, "tensor", axis=2, tiled=True),
    )
    w_gate = gate_weight[0]
    w_up = up_weight[0]
    w_down = down_weight[0]
    model_width = w_gate.shape[0]
    hidden_count = w_gate.shape[1]
    rows_piece = lax.all_gather(full_rows, "seq", axis=0, tiled=True)
    grads_piece = lax.all_gather(full_grads, "seq", axis=0, tiled=True)
    weight_piece = lax.all_gather(recv_weight, "seq", axis=0, tiled=True)
    block_count = rows_piece.shape[0]
    row_block = rows_piece.reshape(-1, model_width)
    grad_block = grads_piece.reshape(-1, model_width)
    row_weight = weight_piece.reshape(-1).astype(jnp.float32)[:, None]
    gate_value = jnp.dot(row_block, w_gate, preferred_element_type=jnp.float32)
    up_value = jnp.dot(row_block, w_up, preferred_element_type=jnp.float32)
    sigmoid_gate = jax.nn.sigmoid(gate_value)
    activated = gate_value * sigmoid_gate
    hidden_value = activated * up_value
    hidden_scaled = (row_weight * hidden_value).astype(jnp.bfloat16)
    raw_grad = lax.dot_general(
        grad_block, w_down, contract_cols, preferred_element_type=jnp.float32
    )
    route_part = jnp.sum(hidden_value * raw_grad, axis=1)
    scaled = row_weight * raw_grad
    gate_delta = (
        scaled * up_value * sigmoid_gate * (1.0 + gate_value * (1.0 - sigmoid_gate))
    ).astype(jnp.bfloat16)
    up_delta = (scaled * activated).astype(jnp.bfloat16)
    new_gate = lax.dot_general(
        row_block, gate_delta, contract_rows, preferred_element_type=jnp.float32
    )
    new_up = lax.dot_general(row_block, up_delta, contract_rows, preferred_element_type=jnp.float32)
    new_down = lax.dot_general(
        hidden_scaled, grad_block, contract_rows, preferred_element_type=jnp.float32
    )
    gates_all = gate_delta.reshape(block_count, shard_rows, hidden_count)
    ups_all = up_delta.reshape(block_count, shard_rows, hidden_count)
    parts_all = route_part.reshape(block_count, shard_rows)
    sum_gate, sum_up, sum_down, gates_all, ups_all, parts_all = (
        new_gate,
        new_up,
        new_down,
        gates_all,
        ups_all,
        parts_all,
    )
    gate_grad = sum_gate.astype(jnp.bfloat16)[None]
    up_grad = sum_up.astype(jnp.bfloat16)[None]
    down_grad = sum_down.astype(jnp.bfloat16)[None]
    totals = lax.psum(parts_all, ("seq", "tensor"))
    own_routes = lax.dynamic_slice_in_dim(
        totals, lax.axis_index("seq") * experts, experts, 0
    ).astype(jnp.bfloat16)
    flat_gate = gates_all.reshape(-1, hidden_count)
    flat_up = ups_all.reshape(-1, hidden_count)
    result = lax.dot_general(flat_gate, w_gate, contract_cols, preferred_element_type=jnp.float32)
    shares = lax.psum_scatter(
        result + lax.dot_general(flat_up, w_up, contract_cols, preferred_element_type=jnp.float32),
        ("seq", "tensor"),
        scatter_dimension=0,
        tiled=True,
    )
    expert_delta = lax.all_to_all(
        shares.astype(jnp.bfloat16), "tensor", split_axis=1, concat_axis=0, tiled=True
    )
    expert_delta = expert_delta.reshape(experts, shard_rows, -1)
    back_delta, back_routes = (
        lax.all_to_all(expert_delta, "expert", split_axis=0, concat_axis=0, tiled=True),
        lax.all_to_all(own_routes, "expert", split_axis=0, concat_axis=0, tiled=True),
    )
    x_grad = jnp.einsum(
        "ts,sd->td",
        dispatch,
        back_delta.reshape(slot_count, -1),
        preferred_element_type=jnp.float32,
    )
    x_grad = x_grad.astype(jnp.bfloat16)
    route_grad = jnp.einsum(
        "tks,s->tk", placed, back_routes.reshape(-1).astype(jnp.float32)
    ).astype(jnp.bfloat16)
    return (x_grad, route_grad, gate_grad, up_grad, down_grad)


def solution(mesh):
    in_specs = (
        P(("expert", "seq"), "tensor"),
        P(("expert", "seq"), "tensor"),
        P(("expert", "seq"), None),
        P(("expert", "seq"), None),
        P("expert", None, ("seq", "tensor")),
        P("expert", None, ("seq", "tensor")),
        P("expert", ("seq", "tensor"), None),
    )
    out_specs = (
        P(("expert", "seq"), "tensor"),
        P(("expert", "seq"), None),
        P("expert", None, ("seq", "tensor")),
        P("expert", None, ("seq", "tensor")),
        P("expert", ("seq", "tensor"), None),
    )
    return jax.shard_map(
        per_device, mesh=mesh, in_specs=in_specs, out_specs=out_specs, check_vma=False
    )
```

profile of v0, /device:TPU:0, one launch (start us, length us, event | category | flops | bytes accessed | tf_op | source)
XLA Modules:
  0.0 234.7 jit_solution(13078340328715923610)
XLA Ops:
  9.6 9.3 %all_to_all.53 = bf16[4,16,1536]{2,1,0:T(8,128)(2,1)S(1)} all-to-all(bf16[4,16,1536]{2,1,0:T(8,128)(2,1)S(1)} %bitcast.72), channel_id=1, replica_groups=mesh['expert'=4,'seq'=2,'tensor'=4] {'expert'}, dimensions={0} | all-to-all | bytes 393216 | tf_op jit(solution)/shard_map/all_to_all | solution.py:31
  18.9 20.3 %all_gather.18 = bf16[4,16,6144]{2,1,0:T(8,128)(2,1)} all-gather(bf16[4,16,1536]{2,1,0:T(8,128)(2,1)S(1)} %all_to_all.53), channel_id=1, replica_groups=mesh['expert'=4,'seq'=2,'tensor'=4] {'tensor'}, dimensions={2}, use_global_device_ids=true | all-gather | bytes 983040 | tf_op jit(solution)/shard_map/all_gather | solution.py:36
  40.7 3.2 %all-to-all-start = ((bf16[4,1,16]{2,1,0:T(2,128)(2,1)}), bf16[4,1,16]{2,1,0:T(2,128)(2,1)S(1)}, u32[]{:S(2)}, u32[]{:S(2)}) async-start(bf16[4,1,16]{2,1,0:T(2,128)(2,1)} %all_to_all.46), calls=%async_computation | async-start | bytes 4096 | tf_op jit(solution)/shard_map/all_to_all | solution.py:33
  44.0 1.7 convolution_convert_fusion.1
  45.7 1.9 all-to-all-done
  47.6 3.4 %all-to-all-start.1 = ((bf16[4,16,1536]{2,1,0:T(8,128)(2,1)}), bf16[4,16,1536]{2,1,0:T(8,128)(2,1)S(1)}, u32[]{:S(2)}, u32[]{:S(2)}) async-start(bf16[4,16,1536]{2,1,0:T(8,128)(2,1)} %bitcast.2), calls=%async_computation.1 | async-start | bytes 393216 | tf_op jit(solution)/shard_map/all_to_all | solution.py:32
  51.0 4.4 %all-gather = bf16[8,1,16]{2,1,0:T(2,128)(2,1)S(1)} all-gather(bf16[4,1,16]{2,1,0:T(2,128)(2,1)S(1)} %all-to-all-done), channel_id=2, replica_groups=mesh['expert'=4,'seq'=2,'tensor'=4] {'seq'}, dimensions={0}, use_global_device_ids=true | all-gather | bytes 384 | tf_op jit(solution)/shard_map/all_gather | solution.py:46
  56.3 18.7 %all_gather.16 = bf16[4,16,6144]{2,1,0:T(8,128)(2,1)} all-gather(bf16[4,16,1536]{2,1,0:T(8,128)(2,1)S(1)} %all-to-all-done.1), channel_id=1, replica_groups=mesh['expert'=4,'seq'=2,'tensor'=4] {'tensor'}, dimensions={2}, use_global_device_ids=true | all-gather | bytes 983040 | tf_op jit(solution)/shard_map/all_gather | solution.py:37
  75.1 7.0 %fusion.2 = f32[128,1024]{1,0:T(8,128)S(1)} fusion(bf16[128,6144]{1,0:T(8,128)(2,1)} %bitcast.65, bf16[1,6144,1024]{2,1,0:T(8,128)(2,1)} %param.11), kind=kOutput, calls=%fused_computation.2 | convolution fusion | flops 1610612736 | bytes 14680064 | tf_op jit(solution)/shard_map/dot_general | solution.py:51
  82.1 6.7 %fusion.6 = f32[128,1024]{1,0:T(8,128)S(1)} fusion(bf16[128,6144]{1,0:T(8,128)(2,1)S(1)} %bitcast.67, bf16[1,6144,1024]{2,1,0:T(8,128)(2,1)} %param.12), kind=kOutput, calls=%fused_computation.6 | convolution fusion | flops 1610612736 | bytes 14680064 | tf_op jit(solution)/shard_map/dot_general | solution.py:52
  88.9 12.7 %all-gather.4.cloned.1.call-done = bf16[8,16,6144]{2,1,0:T(8,128)(2,1)} async-done(((bf16[4,16,6144]{2,1,0:T(8,128)(2,1)}), bf16[8,16,6144]{2,1,0:T(8,128)(2,1)}) %all-gather.4.cloned.1.call-update) | async-done | bytes 1572880 | tf_op jit(solution)/shard_map/all_gather | solution.py:45
  101.6 9.7 %multiply_reduce_fusion = (f32[128]{0:T(128)S(1)}, bf16[128,1024]{1,0:T(8,128)(2,1)S(1)}, bf16[128,1024]{1,0:T(8,128)(2,1)S(1)}) fusion(f32[128,1024]{1,0:T(8,128)S(1)} %fusion.6, f32[128,1024]{1,0:T(8,128)S(1)} %fusion.2, f32[128]{0:T(128)S(1)} %reshape.100, bf16[128,6144]{1,0:T(8,128)(2,1)} %bitcast.69, bf16[1,1024,6144]{2,1,0:T(8,128)(2,1)} %param.13), kind=kOutput, calls=%fused_computation.20 | convolution fusion | flops 1612840832 | bytes 15729664 | tf_op jit(solution)/shard_map/dot_general | solution.py:57
  111.3 10.6 %fusion = f32[128,6144]{1,0:T(8,128)} fusion(bf16[128,1024]{1,0:T(8,128)(2,1)S(1)} %get-tuple-element.6, bf16[1,6144,1024]{2,1,0:T(8,128)(2,1)} %param.11), kind=kOutput, calls=%fused_computation | convolution fusion | flops 1610612736 | bytes 15990784 | tf_op jit(solution)/shard_map/dot_general | solution.py:93
  121.9 7.9 %fusion.10 = f32[128,6144]{1,0:T(8,128)} fusion(f32[128,6144]{1,0:T(8,128)} %fusion, bf16[128,1024]{1,0:T(8,128)(2,1)S(1)} %get-tuple-element.7, bf16[1,6144,1024]{2,1,0:T(8,128)(2,1)S(1)} %bitcast.64), kind=kOutput, calls=%fused_computation.13 | convolution fusion | flops 1611399168 | bytes 19136512 | tf_op jit(solution)/shard_map/dot_general | solution.py:95
  129.9 21.0 %psum.7 = bf16[8,16]{1,0:T(8,128)(2,1)S(1)} all-reduce(f32[8,16]{1,0:T(8,128)S(1)} %reshape.98), channel_id=1, replica_groups=mesh['expert'=4,'seq'=2,'tensor'=4] {'seq','tensor'}, use_global_device_ids=true, to_apply=%region_5.6 | all-reduce | flops 128 | bytes 768 | tf_op jit(solution)/shard_map/psum | solution.py:87
  151.5 3.2 %all-to-all-start.5 = ((bf16[4,1,16]{2,1,0:T(2,128)(2,1)}), bf16[4,1,16]{2,1,0:T(2,128)(2,1)S(1)}, u32[]{:S(2)}, u32[]{:S(2)}) async-start(bf16[4,1,16]{2,1,0:T(2,128)(2,1)} %copy.46), calls=%async_computation.6 | async-start | bytes 4096 | tf_op jit(solution)/shard_map/all_to_all | solution.py:106
  154.8 8.1 %convert_bitcast_fusion.1 = bf16[1,6144,1024]{2,1,0:T(8,128)(2,1)} fusion(bf16[128,6144]{1,0:T(8,128)(2,1)} %bitcast.66, bf16[128,1024]{1,0:T(8,128)(2,1)S(1)} %get-tuple-element.7), kind=kOutput, calls=%fused_computation.11 | convolution fusion | flops 1616904192 | bytes 14417920 | tf_op jit(solution)/shard_map/dot_general | solution.py:69
  162.9 6.6 %convert_bitcast_fusion.2 = bf16[1,6144,1024]{2,1,0:T(8,128)(2,1)} fusion(bf16[128,6144]{1,0:T(8,128)(2,1)S(1)} %bitcast.68, bf16[128,1024]{1,0:T(8,128)(2,1)S(1)} %copy-done.9), kind=kOutput, calls=%fused_computation.12 | convolution fusion | flops 1616904192 | bytes 14417920 | tf_op jit(solution)/shard_map/dot_general | solution.py:66
  169.5 35.3 %reduce-scatter.2.cloned.1.call-done = f32[16,6144]{1,0:T(8,128)} async-done(((f32[128,6144]{1,0:T(8,128)}), f32[16,6144]{1,0:T(8,128)}) %reduce-scatter.2.cloned.1.call-update) | async-done | bytes 393232 | tf_op jit(solution)/shard_map/reduce_scatter | solution.py:94
  204.8 1.0 convert_element_type.71
  206.5 4.0 %all-to-all-start.3 = ((bf16[16,4,1536]{2,0,1:T(8,128)(2,1)}), bf16[16,4,1536]{2,0,1:T(8,128)(2,1)}, u32[]{:S(2)}, u32[]{:S(2)}) async-start(bf16[16,4,1536]{2,0,1:T(8,128)(2,1)} %bitcast.62), calls=%async_computation.4 | async-start | bytes 393216 | tf_op jit(solution)/shard_map/all_to_all | solution.py:100
  210.5 8.1 %convert_bitcast_fusion = bf16[1,1024,6144]{2,1,0:T(8,128)(2,1)} fusion(bf16[128,6144]{1,0:T(8,128)(2,1)} %bitcast.70, f32[128]{0:T(128)S(1)} %reshape.100, f32[128,1024]{1,0:T(8,128)S(1)} %copy-done.7, f32[128,1024]{1,0:T(8,128)S(1)} %copy-done.5), kind=kOutput, calls=%fused_computation.10 | convolution fusion | flops 1617821696 | bytes 15204864 | tf_op jit(solution)/shard_map/dot_general | solution.py:70
  218.7 3.4 %all-to-all-start.4 = ((bf16[4,16,1536]{2,1,0:T(8,128)(2,1)}), bf16[4,16,1536]{2,1,0:T(8,128)(2,1)S(1)}, u32[]{:S(2)}, u32[]{:S(2)}) async-start(bf16[4,16,1536]{2,1,0:T(8,128)(2,1)} %bitcast.9), calls=%async_computation.5 | async-start | bytes 393216 | tf_op jit(solution)/shard_map/all_to_all | solution.py:105
  222.8 4.6 %all-to-all-done.4 = bf16[4,16,1536]{2,1,0:T(8,128)(2,1)S(1)} async-done(((bf16[4,16,1536]{2,1,0:T(8,128)(2,1)}), bf16[4,16,1536]{2,1,0:T(8,128)(2,1)S(1)}, u32[]{:S(2)}, u32[]{:S(2)}) %all-to-all-start.4) | async-done | bytes 196640 | tf_op jit(solution)/shard_map/all_to_all | solution.py:105
  (60 shorter events, 8.0 us)
Async XLA Ops:
  7.2 2.2 copy-start
  7.2 67.9 %all-gather.6.cloned.1.call-start = ((), (), s32[]{:S(2)}) async-start(), calls=%async_computation.8 | async-start | bytes 2359296 | tf_op jit(solution)/shard_map/all_gather | solution.py:44
  40.7 6.9 %all-to-all-start = ((bf16[4,1,16]{2,1,0:T(2,128)(2,1)}), bf16[4,1,16]{2,1,0:T(2,128)(2,1)S(1)}, u32[]{:S(2)}, u32[]{:S(2)}) async-start(bf16[4,1,16]{2,1,0:T(2,128)(2,1)} %all_to_all.46), calls=%async_computation | async-start | bytes 4096 | tf_op jit(solution)/shard_map/all_to_all | solution.py:33
  47.6 8.7 %all-to-all-start.1 = ((bf16[4,16,1536]{2,1,0:T(8,128)(2,1)}), bf16[4,16,1536]{2,1,0:T(8,128)(2,1)S(1)}, u32[]{:S(2)}, u32[]{:S(2)}) async-start(bf16[4,16,1536]{2,1,0:T(8,128)(2,1)} %bitcast.2), calls=%async_computation.1 | async-start | bytes 393216 | tf_op jit(solution)/shard_map/all_to_all | solution.py:32
  51.0 50.6 %all-gather.4.cloned.1.call-start = ((), (), s32[]{:S(2)}) async-start(), calls=%async_computation.7 | async-start | bytes 2359296 | tf_op jit(solution)/shard_map/all_gather | solution.py:45
  75.0 129.7 %reduce-scatter.2.cloned.1.call-start = ((), (), s32[]{:S(2)}) async-start(), calls=%async_computation.9 | async-start | bytes 3538944 | tf_op jit(solution)/shard_map/reduce_scatter | solution.py:94
  75.1 7.0 %copy-start.2 = (bf16[8,16,6144]{2,1,0:T(8,128)(2,1)S(1)}, bf16[8,16,6144]{2,1,0:T(8,128)(2,1)}, u32[]{:S(2)}) copy-start(bf16[8,16,6144]{2,1,0:T(8,128)(2,1)} %all-gather.6.cloned.1.call-done) | copy-start | bytes 4718596
  82.1 29.1 %copy-start.4 = (f32[128,1024]{1,0:T(8,128)}, f32[128,1024]{1,0:T(8,128)S(1)}, u32[]{:S(2)}) copy-start(f32[128,1024]{1,0:T(8,128)S(1)} %fusion.2) | copy-start | bytes 1572868
  88.9 12.7 %copy-start.6 = (f32[128,1024]{1,0:T(8,128)}, f32[128,1024]{1,0:T(8,128)S(1)}, u32[]{:S(2)}) copy-start(f32[128,1024]{1,0:T(8,128)S(1)} %fusion.6) | copy-start | bytes 1572868
  101.6 20.3 %slice-start = ((s8[12582912]{0:T(1024)(128)(4,1)}), s8[4194304]{0:T(1024)(128)(4,1)S(1)}, s32[]{:S(2)}) async-start(s8[12582912]{0:T(1024)(128)(4,1)} %bitcast.63), calls=%async_computation.10 | async-start | bytes 8388608
  101.6 20.3 %slice-start.1 = ((s8[12582912]{0:T(1024)(128)(4,1)}), s8[4194304]{0:T(1024)(128)(4,1)S(1)}, s32[]{:S(2)}) async-start(s8[12582912]{0:T(1024)(128)(4,1)} %bitcast.63), calls=%async_computation.11 | async-start | bytes 8388608
  111.3 10.6 %copy-start.8 = (bf16[128,1024]{1,0:T(8,128)(2,1)}, bf16[128,1024]{1,0:T(8,128)(2,1)S(1)}, u32[]{:S(2)}) copy-start(bf16[128,1024]{1,0:T(8,128)(2,1)S(1)} %get-tuple-element.6) | copy-start | bytes 786436
  111.3 10.6 %slice-start.2 = ((s8[12582912]{0:T(1024)(128)(4,1)}), s8[4194304]{0:T(1024)(128)(4,1)S(1)}, s32[]{:S(2)}) async-start(s8[12582912]{0:T(1024)(128)(4,1)} %bitcast.63), calls=%async_computation.12 | async-start | bytes 8388608
  129.8 33.1 %copy-start.3 = (bf16[8,16,6144]{2,1,0:T(8,128)(2,1)S(1)}, bf16[8,16,6144]{2,1,0:T(8,128)(2,1)}, u32[]{:S(2)}) copy-start(bf16[8,16,6144]{2,1,0:T(8,128)(2,1)} %all-gather.6.cloned.1.call-done) | copy-start | bytes 4718596
  129.8 33.1 %copy-start.9 = (bf16[128,1024]{1,0:T(8,128)(2,1)S(1)}, bf16[128,1024]{1,0:T(8,128)(2,1)}, u32[]{:S(2)}) copy-start(bf16[128,1024]{1,0:T(8,128)(2,1)} %copy-done.8) | copy-start | bytes 786436
  151.5 54.9 %all-to-all-start.5 = ((bf16[4,1,16]{2,1,0:T(2,128)(2,1)}), bf16[4,1,16]{2,1,0:T(2,128)(2,1)S(1)}, u32[]{:S(2)}, u32[]{:S(2)}) async-start(bf16[4,1,16]{2,1,0:T(2,128)(2,1)} %copy.46), calls=%async_computation.6 | async-start | bytes 4096 | tf_op jit(solution)/shard_map/all_to_all | solution.py:106
  154.8 55.7 %copy-start.5 = (f32[128,1024]{1,0:T(8,128)S(1)}, f32[128,1024]{1,0:T(8,128)}, u32[]{:S(2)}) copy-start(f32[128,1024]{1,0:T(8,128)} %copy-done.4) | copy-start | bytes 1572868
  154.8 55.7 %copy-start.7 = (f32[128,1024]{1,0:T(8,128)S(1)}, f32[128,1024]{1,0:T(8,128)}, u32[]{:S(2)}) copy-start(f32[128,1024]{1,0:T(8,128)} %copy-done.6) | copy-start | bytes 1572868
  154.8 73.4 %copy-start.1 = (bf16[16,1536]{1,0:T(8,128)(2,1)S(1)}, bf16[16,1536]{1,0:T(8,128)(2,1)}, u32[]{:S(2)}) copy-start(bf16[16,1536]{1,0:T(8,128)(2,1)} %param.7) | copy-start | bytes 147460
  206.5 12.2 %all-to-all-start.3 = ((bf16[16,4,1536]{2,0,1:T(8,128)(2,1)}), bf16[16,4,1536]{2,0,1:T(8,128)(2,1)}, u32[]{:S(2)}, u32[]{:S(2)}) async-start(bf16[16,4,1536]{2,0,1:T(8,128)(2,1)} %bitcast.62), calls=%async_computation.4 | async-start | bytes 393216 | tf_op jit(solution)/shard_map/all_to_all | solution.py:100
  218.7 8.7 %all-to-all-start.4 = ((bf16[4,16,1536]{2,1,0:T(8,128)(2,1)}), bf16[4,16,1536]{2,1,0:T(8,128)(2,1)S(1)}, u32[]{:S(2)}, u32[]{:S(2)}) async-start(bf16[4,16,1536]{2,1,0:T(8,128)(2,1)} %bitcast.9), calls=%async_computation.5 | async-start | bytes 393216 | tf_op jit(solution)/shard_map/all_to_all | solution.py:105
Sparse Core Ops, SparseCore 0:
  39.3 26.1 all-gather.5
  75.2 26.3 all-gather.3
  130.0 74.7 reduce-scatter.1
where the time goes:
time: 236 us; the launch traced here: 235 us
  blocking collectives  73.7 us (31%)
  matrix products  68.5 us (29%)
  waiting for transfers between devices  55.3 us (23%)
  starting transfers between devices  17.3 us (7%)
  between operations  14 us (6%)
  local copies, waits for them, and re-layouts  3.28 us (1%)
  other arithmetic  2.68 us (1%)
    reduce_scatter x1, waiting for transfers between devices, per_device(): lax.psum_scatter(result + lax.dot_general(flat_up, w_up, contract_cols, p...  35.3 us
    psum x1, blocking collectives, per_device(): totals = lax.psum(parts_all, ('seq', 'tensor'))  21 us
    all_gather x1, blocking collectives, per_device(): lax.all_gather(recv_rows, 'tensor', axis=2, tiled=True)  20.3 us
    all_gather x1, blocking collectives, per_device(): lax.all_gather(recv_grads, 'tensor', axis=2, tiled=True)  18.7 us
    all_gather x1, waiting for transfers between devices, per_device(): grads_piece = lax.all_gather(full_grads, 'seq', axis=0, tiled=True)  12.7 us
    dot_general x1, matrix products, per_device(): lax.dot_general(flat_gate, w_gate, contract_cols, preferred_element_type=...  10.6 us
    dot_general x1, matrix products, per_device(): lax.dot_general(grad_block, w_down, contract_cols, preferred_element_type...  9.66 us
    all_to_all x1, blocking collectives, per_device(): lax.all_to_all(send_rows, 'expert', split_axis=0, concat_axis=0, tiled=True)  9.35 us
  transfers between devices with their start and end apart: 8, of which 5 were waited for; matrix products, arithmetic and copies ran while one was open for 18% of the time, Pallas kernels for 0%

commit v1 on v0

v1 whole, which is shorter than its diff:
```python
import functools

import jax
import jax.numpy as jnp
from jax import lax
from jax.experimental import pallas as pl
from jax.experimental.pallas import tpu as pltpu
from jax.sharding import PartitionSpec as P

EXTRA = 128
MIB = 1 << 20
CONTRACT_ROWS = (((0,), (0,)), ((), ()))
CONTRACT_COLS = (((1,), (1,)), ((), ()))


def params(mib):
    return pltpu.CompilerParams(vmem_limit_bytes=mib * MIB)


def cost(flops, moved):
    return pl.CostEstimate(flops=int(flops), bytes_accessed=int(moved), transcendentals=0)


def chunk_of(features):
    for size in (768, 512, 384, 256, 128):
        if features % size == 0:
            return size
    return features


def relative_chunk(step, home, pieces, per_piece):
    owner = step // per_piece
    return lax.rem(home - owner + pieces, pieces) * per_piece + lax.rem(step, per_piece)


def matmul(a, b, dims=None):
    if dims is None:
        return jnp.dot(a, b, preferred_element_type=jnp.float32)
    return lax.dot_general(a, b, dims, preferred_element_type=jnp.float32)


def gate_up_kernel(home, xp, xo, wg, wu, gate, up):
    @pl.when(pl.program_id(0) == 0)
    def _():
        gate[...] = jnp.zeros_like(gate)
        up[...] = jnp.zeros_like(up)

    rows = jnp.concatenate([xp[...], xo[...]], axis=0)
    gate[...] += matmul(rows, wg[0])
    up[...] += matmul(rows, wu[0])


def gate_up(home, pieces, near, far, w_gate, w_up):
    half = near.shape[0]
    _, depth, hidden = w_gate.shape
    size = chunk_of(depth // pieces)
    per_piece = depth // pieces // size
    rel = functools.partial(relative_chunk, pieces=pieces, per_piece=per_piece)
    out = jax.ShapeDtypeStruct((2 * half, hidden), jnp.float32)
    rows = pl.BlockSpec((half, size), lambda j, home: (0, rel(j, home[0])))
    weights = pl.BlockSpec((1, size, hidden), lambda j, home: (0, j, 0))
    whole = pl.BlockSpec((2 * half, hidden), lambda j, home: (0, 0))
    return pl.pallas_call(
        gate_up_kernel,
        grid_spec=pltpu.PrefetchScalarGridSpec(
            num_scalar_prefetch=1,
            grid=(depth // size,),
            in_specs=[rows, rows, weights, weights],
            out_specs=[whole, whole],
        ),
        out_shape=[out, out],
        compiler_params=params(32),
        cost_estimate=cost(8 * half * depth * hidden, 4 * depth * hidden),
        name="gate_up",
    )(home, near, far, w_gate, w_up)


def delta_kernel(home, me, gp, go, wd, gate, up, xpw, xow, dgate, dup, hidw, part, raw, *, experts):
    step = pl.program_id(0)

    @pl.when(step == 0)
    def _():
        raw[...] = jnp.zeros_like(raw)

    rows = jnp.concatenate([gp[...], go[...]], axis=0)
    raw[...] += matmul(rows, wd[0], CONTRACT_COLS)

    @pl.when(step == pl.num_programs(0) - 1)
    def _():
        lane = lax.broadcasted_iota(jnp.int32, (1, EXTRA), 1)
        weights = jnp.concatenate([xpw[...], xow[...]], axis=0).astype(jnp.float32)
        mine = lane == me[0]
        weight = jnp.sum(jnp.where(mine, weights, 0.0), axis=1, keepdims=True)
        gate_value = gate[...]
        up_value = up[...]
        raw_value = raw[...]
        sigmoid_gate = jax.nn.sigmoid(gate_value)
        activated = gate_value * sigmoid_gate
        hidden_value = activated * up_value
        scaled = weight * raw_value
        slope = sigmoid_gate * (1.0 + gate_value * (1.0 - sigmoid_gate))
        dgate[...] = (scaled * up_value * slope).astype(jnp.bfloat16)
        dup[...] = (scaled * activated).astype(jnp.bfloat16)
        hidw[...] = (weight * hidden_value).astype(jnp.bfloat16)
        total = jnp.sum(hidden_value * raw_value, axis=1, keepdims=True)
        high = total.astype(jnp.bfloat16).astype(jnp.float32)
        low = total - high
        placed = jnp.where(mine, high, 0.0) + jnp.where(lane == me[0] + experts, low, 0.0)
        part[...] = placed.astype(jnp.bfloat16)


def deltas(home, me, experts, pieces, near, far, w_down, gate, up, near_x, far_x):
    half = near.shape[0]
    _, hidden, depth = w_down.shape
    size = chunk_of(depth // pieces)
    per_piece = depth // pieces // size
    rel = functools.partial(relative_chunk, pieces=pieces, per_piece=per_piece)
    rows = pl.BlockSpec((half, size), lambda j, home, me: (0, rel(j, home[0])))
    weights = pl.BlockSpec((1, hidden, size), lambda j, home, me: (0, 0, j))
    whole = pl.BlockSpec((2 * half, hidden), lambda j, home, me: (0, 0))
    extra_in = pl.BlockSpec((half, EXTRA), lambda j, home, me: (0, depth // EXTRA))
    extra_out = pl.BlockSpec((2 * half, EXTRA), lambda j, home, me: (0, 0))
    out = jax.ShapeDtypeStruct((2 * half, hidden), jnp.bfloat16)
    return pl.pallas_call(
        functools.partial(delta_kernel, experts=experts),
        grid_spec=pltpu.PrefetchScalarGridSpec(
            num_scalar_prefetch=2,
            grid=(depth // size,),
            in_specs=[rows, rows, weights, whole, whole, extra_in, extra_in],
            out_specs=[whole, whole, whole, extra_out],
            scratch_shapes=[pltpu.VMEM((2 * half, hidden), jnp.float32)],
        ),
        out_shape=[out, out, out, jax.ShapeDtypeStruct((2 * half, EXTRA), jnp.bfloat16)],
        compiler_params=params(32),
        cost_estimate=cost(4 * half * depth * hidden, 2 * depth * hidden),
        name="deltas",
    )(home, me, near, far, w_down, gate, up, near_x, far_x)


def input_kernel(home, dgate, dup, wg, wu, part, near, far, *, pieces, per_piece):
    step = pl.program_id(0)
    size = wg.shape[1]
    half = near.shape[0]
    depth = near.shape[1] - EXTRA
    value = matmul(dgate[...], wg[0], CONTRACT_COLS) + matmul(dup[...], wu[0], CONTRACT_COLS)
    value = value.astype(jnp.bfloat16)
    start = pl.multiple_of(relative_chunk(step, home[0], pieces, per_piece) * size, size)
    near[:, pl.ds(start, size)] = value[:half]
    far[:, pl.ds(start, size)] = value[half:]

    @pl.when(step == 0)
    def _():
        near[:, depth:] = part[:half, :]
        far[:, depth:] = part[half:, :]


def input_grads(home, pieces, dgate, dup, w_gate, w_up, part):
    rows, hidden = dgate.shape
    half = rows // 2
    depth = w_gate.shape[1]
    size = chunk_of(depth // pieces)
    per_piece = depth // pieces // size
    weights = pl.BlockSpec((1, size, hidden), lambda j, home: (0, j, 0))
    whole = pl.BlockSpec((rows, hidden), lambda j, home: (0, 0))
    extra = pl.BlockSpec((rows, EXTRA), lambda j, home: (0, 0))
    result = pl.BlockSpec((half, depth + EXTRA), lambda j, home: (0, 0))
    out = jax.ShapeDtypeStruct((half, depth + EXTRA), jnp.bfloat16)
    return pl.pallas_call(
        functools.partial(input_kernel, pieces=pieces, per_piece=per_piece),
        grid_spec=pltpu.PrefetchScalarGridSpec(
            num_scalar_prefetch=1,
            grid=(depth // size,),
            in_specs=[whole, whole, weights, weights, extra],
            out_specs=[result, result],
        ),
        out_shape=[out, out],
        compiler_params=params(32),
        cost_estimate=cost(4 * rows * depth * hidden, 4 * depth * hidden),
        name="input_grads",
    )(home, dgate, dup, w_gate, w_up, part)


def columns_kernel(home, xp, xo, delta, out):
    rows = jnp.concatenate([xp[...], xo[...]], axis=0)
    out[0] = matmul(rows, delta[...], CONTRACT_ROWS).astype(jnp.bfloat16)


def columns_grad(home, pieces, near, far, delta, depth):
    half = near.shape[0]
    hidden = delta.shape[1]
    size = chunk_of(depth // pieces)
    per_piece = depth // pieces // size
    rel = functools.partial(relative_chunk, pieces=pieces, per_piece=per_piece)
    rows = pl.BlockSpec((half, size), lambda j, home: (0, rel(j, home[0])))
    return pl.pallas_call(
        columns_kernel,
        grid_spec=pltpu.PrefetchScalarGridSpec(
            num_scalar_prefetch=1,
            grid=(depth // size,),
            in_specs=[rows, rows, pl.BlockSpec((2 * half, hidden), lambda j, home: (0, 0))],
            out_specs=pl.BlockSpec((1, size, hidden), lambda j, home: (0, j, 0)),
        ),
        out_shape=jax.ShapeDtypeStruct((1, depth, hidden), jnp.bfloat16),
        compiler_params=params(32),
        cost_estimate=cost(4 * half * depth * hidden, 2 * depth * hidden),
        name="columns_grad",
    )(home, near, far, delta)


def down_kernel(home, gp, go, hidw, out):
    rows = jnp.concatenate([gp[...], go[...]], axis=0)
    out[0] = matmul(hidw[...], rows, CONTRACT_ROWS).astype(jnp.bfloat16)


def down_grads(home, pieces, near, far, hidw, depth):
    half = near.shape[0]
    hidden = hidw.shape[1]
    size = chunk_of(depth // pieces)
    per_piece = depth // pieces // size
    rel = functools.partial(relative_chunk, pieces=pieces, per_piece=per_piece)
    rows = pl.BlockSpec((half, size), lambda j, home: (0, rel(j, home[0])))
    return pl.pallas_call(
        down_kernel,
        grid_spec=pltpu.PrefetchScalarGridSpec(
            num_scalar_prefetch=1,
            grid=(depth // size,),
            in_specs=[rows, rows, pl.BlockSpec((2 * half, hidden), lambda j, home: (0, 0))],
            out_specs=pl.BlockSpec((1, hidden, size), lambda j, home: (0, 0, j)),
        ),
        out_shape=jax.ShapeDtypeStruct((1, hidden, depth), jnp.bfloat16),
        compiler_params=params(32),
        cost_estimate=cost(4 * half * depth * hidden, 2 * depth * hidden),
        name="down_grads",
    )(home, near, far, hidw)


def resplit(extra, experts):
    total = extra[:, :experts] + extra[:, experts : 2 * experts]
    high = total.astype(jnp.bfloat16)
    low = (total - high.astype(jnp.float32)).astype(jnp.bfloat16)
    rest = jnp.zeros((extra.shape[0], EXTRA - 2 * experts), jnp.bfloat16)
    return jnp.concatenate([high, low, rest], axis=1)


def tree_sum(parts):
    while len(parts) > 1:
        middle = len(parts) // 2
        parts = [a + b for a, b in zip(parts[:middle], parts[middle:], strict=True)]
    return parts[0]


def per_device(tokens_in, out_grad, route_ids, route_weight, gate_weight, up_weight, down_weight):
    experts = lax.axis_size("expert")
    seqs = lax.axis_size("seq")
    pieces = lax.axis_size("tensor")
    rows, width = tokens_in.shape
    depth = width * pieces
    home = lax.axis_index("tensor").astype(jnp.int32).reshape(1)
    me = lax.axis_index("expert").astype(jnp.int32).reshape(1)
    chips = experts // 2
    planes = [(dx, ds) for ds in range(seqs) for dx in range(chips)]

    def along(value, shift):
        pairs = [(i, (i + shift) % pieces) for i in range(pieces)]
        return lax.ppermute(value, "tensor", pairs)

    def across(value, dx, ds):
        pairs = []
        for e in range(experts):
            for s in range(seqs):
                to_e = ((e // 2 + dx) % chips) * 2 + e % 2
                pairs.append((e * seqs + s, to_e * seqs + (s + ds) % seqs))
        return lax.ppermute(value, ("expert", "seq"), pairs)

    def swap(value):
        return lax.ppermute(value, "expert", [(e, e ^ 1) for e in range(experts)])

    def gather(value, extra):
        blocks = [value] + [along(value, k) for k in range(1, pieces)] + extra
        line = jnp.concatenate(blocks, axis=1)
        near = jnp.concatenate([line] + [across(line, dx, ds) for dx, ds in planes[1:]], axis=0)
        return near, swap(near)

    expert_ids = jnp.arange(EXTRA, dtype=jnp.int32)
    chosen = (route_ids[:, :, None] == expert_ids[None, None, :]).astype(jnp.float32)
    weights = jnp.sum(chosen * route_weight.astype(jnp.float32)[:, :, None], axis=1)
    near_x, far_x = gather(tokens_in, [weights.astype(jnp.bfloat16)])
    near_g, far_g = gather(out_grad, [])

    gate, up = gate_up(home, pieces, near_x, far_x, gate_weight, up_weight)
    dgate, dup, hidw, part = deltas(
        home, me, experts, pieces, near_g, far_g, down_weight, gate, up, near_x, far_x
    )
    near_d, far_d = input_grads(home, pieces, dgate, dup, gate_weight, up_weight, part)

    other_d = swap(far_d)
    wide = near_d.astype(jnp.float32) + other_d.astype(jnp.float32)
    both = jnp.concatenate(
        [wide[:, :depth].astype(jnp.bfloat16), resplit(wide[:, depth:], experts)], axis=1
    )
    blocks = [both[i * rows : (i + 1) * rows] for i in range(len(planes))]
    arrived = [
        across(block, -dx, -ds) for block, (dx, ds) in zip(blocks[1:], planes[1:], strict=True)
    ]
    wide = sum([b.astype(jnp.float32) for b in arrived], blocks[0].astype(jnp.float32))
    line = wide[:, :depth].astype(jnp.bfloat16)
    extra = resplit(wide[:, depth:], experts)
    sends = [
        jnp.concatenate([line[:, k * width : (k + 1) * width], extra], axis=1)
        for k in range(pieces)
    ]
    finals = [sends[0]] + [along(sends[k], -k) for k in range(1, pieces)]
    total = tree_sum([f.astype(jnp.float32) for f in finals])
    x_grad = total[:, :width].astype(jnp.bfloat16)
    routes = total[:, width : width + experts] + total[:, width + experts : width + 2 * experts]
    routes = routes.astype(jnp.bfloat16).astype(jnp.float32)
    route_grad = jnp.sum(chosen[:, :, :experts] * routes[:, None, :], axis=2).astype(jnp.bfloat16)

    gate_grad = columns_grad(home, pieces, near_x, far_x, dgate, depth)
    up_grad = columns_grad(home, pieces, near_x, far_x, dup, depth)
    down_grad = down_grads(home, pieces, near_g, far_g, hidw, depth)
    return (x_grad, route_grad, gate_grad, up_grad, down_grad)


def solution(mesh):
    in_specs = (
        P(("expert", "seq"), "tensor"),
        P(("expert", "seq"), "tensor"),
        P(("expert", "seq"), None),
        P(("expert", "seq"), None),
        P("expert", None, ("seq", "tensor")),
        P("expert", None, ("seq", "tensor")),
        P("expert", ("seq", "tensor"), None),
    )
    out_specs = (
        P(("expert", "seq"), "tensor"),
        P(("expert", "seq"), None),
        P("expert", None, ("seq", "tensor")),
        P("expert", None, ("seq", "tensor")),
        P("expert", ("seq", "tensor"), None),
    )
    return jax.shard_map(
        per_device, mesh=mesh, in_specs=in_specs, out_specs=out_specs, check_vma=False
    )
```

time: 236 us -> 115 us (0.49)
  blocking collectives: 73.7 us -> 0 us
  matrix products: 68.5 us -> 0 us
  Pallas kernels: 0 us -> 52.5 us
  waiting for transfers between devices: 55.3 us -> 17 us
  between operations: 14 us -> 0.92 us
  local copies, waits for them, and re-layouts: 3.28 us -> 16 us
  starting transfers between devices: 17.3 us -> 24.9 us
    dot_general x13 -> x0, matrix products: 68.5 us -> none  [the longest x1 10.6 us: per_device(): lax.dot_general(flat_gate, w_gate, contract_cols, preferred_element_type=...]
    pallas_call x0 -> x6, Pallas kernels: none -> 52.5 us  [the longest x2 15.6 us: columns_grad(): pl.pallas_call(columns_kernel, grid_spec=pltpu.PrefetchScalarGridSpec(num...]
    all_gather x3 -> x0, blocking collectives: 43.4 us -> none  [the longest x1 20.3 us: per_device(): lax.all_gather(recv_rows, 'tensor', axis=2, tiled=True)]
    reduce_scatter x1 -> x0, waiting for transfers between devices: 35.3 us -> none  [per_device(): lax.psum_scatter(result + lax.dot_general(flat_up, w_up, contract_cols, p...]
    ppermute x0 -> x21, starting transfers between devices: none -> 24.9 us  [the longest x9 12.6 us: along(): return lax.ppermute(value, 'tensor', pairs)]
    psum x1 -> x0, blocking collectives: 21 us -> none  [per_device(): totals = lax.psum(parts_all, ('seq', 'tensor'))]
    all_to_all x5 -> x0, starting transfers between devices: 17.2 us -> none  [the longest x1 3.99 us: per_device(): lax.all_to_all(shares.astype(jnp.bfloat16), 'tensor', split_axis=1, conca...]
    ppermute x0 -> x21, waiting for transfers between devices: none -> 17 us  [the longest x9 9.32 us: across(): return lax.ppermute(value, ('expert', 'seq'), pairs)]
  transfers between devices with their start and end apart: 8 -> 21, of which waited for: 5 -> 9; matrix products, arithmetic and copies ran while one was open for 18% -> 3% of each run, Pallas kernels for 0% -> 29%
where the time goes in v1:
time: 115 us
  Pallas kernels  52.5 us (46%)
  starting transfers between devices  24.9 us (22%)
  waiting for transfers between devices  17 us (15%)
  local copies, waits for them, and re-layouts  16 us (14%)
  other arithmetic  3.71 us (3%)
    pallas_call x2, Pallas kernels, columns_grad(): pl.pallas_call(columns_kernel, grid_spec=pltpu.PrefetchScalarGridSpec(num...  15.6 us
    ppermute x9, starting transfers between devices, along(): return lax.ppermute(value, 'tensor', pairs)  12.6 us
    pallas_call x1, Pallas kernels, input_grads(): pl.pallas_call(functools.partial(input_kernel, pieces=pieces, per_piece=p...  11.9 us
    ppermute x9, starting transfers between devices, across(): return lax.ppermute(value, ('expert', 'seq'), pairs)  11.6 us
    unnamed x31, local copies, waits for them, and re-layouts  10.8 us
    pallas_call x1, Pallas kernels, gate_up(): pl.pallas_call(gate_up_kernel, grid_spec=pltpu.PrefetchScalarGridSpec(num...  10.2 us
    ppermute x9, waiting for transfers between devices, across(): return lax.ppermute(value, ('expert', 'seq'), pairs)  9.32 us
    pallas_call x1, Pallas kernels, down_grads(): pl.pallas_call(down_kernel, grid_spec=pltpu.PrefetchScalarGridSpec(num_sc...  7.8 us
  transfers between devices with their start and end apart: 21, of which 9 were waited for; matrix products, arithmetic and copies ran while one was open for 3% of the time, Pallas kernels for 29%

profile of v1, /device:TPU:0, one launch (start us, length us, event | category | flops | bytes accessed | tf_op | source)
XLA Modules:
  0.0 114.9 jit_solution(2134383026759911348)
XLA Ops:
  0.6 3.1 %collective-permute-start = (bf16[16,1536]{1,0:T(8,128)(2,1)}, bf16[16,1536]{1,0:T(8,128)(2,1)S(1)}, u32[]{:S(2)}, u32[]{:S(2)}) collective-permute-start(bf16[16,1536]{1,0:T(8,128)(2,1)} %param.8), channel_id=1, source_target_pairs={{0,1},{1,2},{2,3},{3,0},{4,5},{5,6},{6,7},{7,4},{8,9},{9,10},{10,1... | collective-permute-start | bytes 147464 | tf_op jit(solution)/shard_map/ppermute | solution.py:265
  3.7 2.6 %collective-permute-start.1 = (bf16[16,1536]{1,0:T(8,128)(2,1)}, bf16[16,1536]{1,0:T(8,128)(2,1)S(1)}, u32[]{:S(2)}, u32[]{:S(2)}) collective-permute-start(bf16[16,1536]{1,0:T(8,128)(2,1)} %param.8), channel_id=1, source_target_pairs={{0,2},{1,3},{2,0},{3,1},{4,6},{5,7},{6,4},{7,5},{8,10},{9,11},{10,... | collective-permute-start | bytes 147464 | tf_op jit(solution)/shard_map/ppermute | solution.py:265
  11.7 2.2 %collective-permute-done.7 = bf16[16,1536]{1,0:T(8,128)(2,1)S(1)} collective-permute-done((bf16[16,1536]{1,0:T(8,128)(2,1)}, bf16[16,1536]{1,0:T(8,128)(2,1)S(1)}, u32[]{:S(2)}, u32[]{:S(2)}) %collective-permute-start.7) | collective-permute-done | bytes 49184 | tf_op jit(solution)/shard_map/ppermute | solution.py:265
  14.6 3.6 %collective-permute-done.9 = bf16[16,1536]{1,0:T(8,128)(2,1)S(1)} collective-permute-done((bf16[16,1536]{1,0:T(8,128)(2,1)}, bf16[16,1536]{1,0:T(8,128)(2,1)S(1)}, u32[]{:S(2)}, u32[]{:S(2)}) %collective-permute-start.9) | collective-permute-done | bytes 49184 | tf_op jit(solution)/shard_map/ppermute | solution.py:265
  18.2 2.5 %collective-permute-start.12 = (bf16[16,6272]{1,0:T(8,128)(2,1)S(1)}, bf16[16,6272]{1,0:T(8,128)(2,1)S(1)}, u32[]{:S(2)}, u32[]{:S(2)}) collective-permute-start(bf16[16,6272]{1,0:T(8,128)(2,1)S(1)} %constant_dynamic-update-slice_fusion.4), channel_id=1, source_target_pairs={{0,20},{4,16},{8,28},{12,24},{16,4},{20,0},{24,12},{28,8},{1,21},{... | collective-permute-start | bytes 602120 | tf_op jit(solution)/shard_map/ppermute | solution.py:273
  21.8 2.5 %collective-permute-start.5 = (bf16[16,6144]{1,0:T(8,128)(2,1)S(1)}, bf16[16,6144]{1,0:T(8,128)(2,1)S(1)}, u32[]{:S(2)}, u32[]{:S(2)}) collective-permute-start(bf16[16,6144]{1,0:T(8,128)(2,1)S(1)} %constant_dynamic-update-slice_fusion), channel_id=1, source_target_pairs={{0,20},{4,16},{8,28},{12,24},{16,4},{20,0},{24,12},{28,8},{1,21},{... | collective-permute-start | bytes 589832 | tf_op jit(solution)/shard_map/ppermute | solution.py:273
  24.8 2.4 %collective-permute-done.12 = bf16[16,6272]{1,0:T(8,128)(2,1)S(1)} collective-permute-done((bf16[16,6272]{1,0:T(8,128)(2,1)S(1)}, bf16[16,6272]{1,0:T(8,128)(2,1)S(1)}, u32[]{:S(2)}, u32[]{:S(2)}) %collective-permute-start.12) | collective-permute-done | bytes 200736 | tf_op jit(solution)/shard_map/ppermute | solution.py:273
  27.2 1.5 %collective-permute-start.3 = (bf16[16,6144]{1,0:T(8,128)(2,1)S(1)}, bf16[16,6144]{1,0:T(8,128)(2,1)S(1)}, u32[]{:S(2)}, u32[]{:S(2)}) collective-permute-start(bf16[16,6144]{1,0:T(8,128)(2,1)S(1)} %constant_dynamic-update-slice_fusion), channel_id=1, source_target_pairs={{0,16},{4,20},{8,24},{12,28},{16,0},{20,4},{24,8},{28,12},{1,17},{... | collective-permute-start | bytes 589832 | tf_op jit(solution)/shard_map/ppermute | solution.py:273
  28.6 2.7 %collective-permute-done.11 = bf16[16,6272]{1,0:T(8,128)(2,1)S(1)} collective-permute-done((bf16[16,6272]{1,0:T(8,128)(2,1)S(1)}, bf16[16,6272]{1,0:T(8,128)(2,1)S(1)}, u32[]{:S(2)}, u32[]{:S(2)}) %collective-permute-start.11) | collective-permute-done | bytes 200736 | tf_op jit(solution)/shard_map/ppermute | solution.py:273
  31.6 2.3 %collective-permute-done.5 = bf16[16,6144]{1,0:T(8,128)(2,1)S(1)} collective-permute-done((bf16[16,6144]{1,0:T(8,128)(2,1)S(1)}, bf16[16,6144]{1,0:T(8,128)(2,1)S(1)}, u32[]{:S(2)}, u32[]{:S(2)}) %collective-permute-start.5) | collective-permute-done | bytes 196640 | tf_op jit(solution)/shard_map/ppermute | solution.py:273
  33.9 1.7 %collective-permute-done.4 = bf16[16,6144]{1,0:T(8,128)(2,1)S(1)} collective-permute-done((bf16[16,6144]{1,0:T(8,128)(2,1)S(1)}, bf16[16,6144]{1,0:T(8,128)(2,1)S(1)}, u32[]{:S(2)}, u32[]{:S(2)}) %collective-permute-start.4) | collective-permute-done | bytes 196640 | tf_op jit(solution)/shard_map/ppermute | solution.py:273
  35.9 4.6 %copy-done = bf16[1,6144,1024]{2,1,0:T(8,128)(2,1)S(1)} copy-done((bf16[1,6144,1024]{2,1,0:T(8,128)(2,1)S(1)}, bf16[1,6144,1024]{2,1,0:T(8,128)(2,1)}, u32[]{:S(2)}) %copy-start) | copy-done | bytes 12582936
  40.5 10.2 %gate_up.1 = (f32[128,1024]{1,0:T(8,128)S(1)}, f32[128,1024]{1,0:T(8,128)S(1)}) custom-call(s32[1]{0:T(128)} %bitcast.home, bf16[64,6272]{1,0:T(8,128)(2,1)S(1)} %pad_maximum_fusion.xp.xpw, bf16[64,6272]{1,0:T(8,128)(2,1)S(1)} %collective-permute-done.13.xo.xow, bf16[1,6144,1024]{2,1,0:T(8,128)(2,1)S(1)} %copy-done, bf16[1,6144,1024]{2,1,0:T(8,128)(2,1)} %wu.3), custom_call_target="tpu_custom_call" | custom-call | flops 3221225472 | bytes 25165824 | tf_op jit(solution)/shard_map/gate_up/pallas_call | solution.py:63
  50.7 4.6 %copy-done.1 = bf16[1,1024,6144]{2,1,0:T(8,128)(2,1)S(1)} copy-done((bf16[1,1024,6144]{2,1,0:T(8,128)(2,1)S(1)}, bf16[1,1024,6144]{2,1,0:T(8,128)(2,1)}, u32[]{:S(2)}) %copy-start.1) | copy-done | bytes 12582936
  55.3 7.1 %deltas.1 = (bf16[128,1024]{1,0:T(8,128)(2,1)S(1)}, bf16[128,1024]{1,0:T(8,128)(2,1)S(1)}, bf16[128,1024]{1,0:T(8,128)(2,1)S(1)}, bf16[128,128]{1,0:T(8,128)(2,1)S(1)}) custom-call(s32[1]{0:T(128)} %bitcast.home, s32[1]{0:T(128)} %bitcast.1.me, bf16[64,6144]{1,0:T(8,128)(2,1)S(1)} %pad_maximum_fusion.1.gp, bf16[64,6144]{1,0:T(8,128)(2,1)S(1)} %collective-permute-done.6.go, ...), custom_call_target="tpu_custom_call" | custom-call | flops 1610612736 | bytes 12582912 | tf_op jit(solution)/shard_map/deltas/pallas_call | solution.py:124
  62.4 11.9 %input_grads.1 = (bf16[64,6272]{1,0:T(8,128)(2,1)S(1)}, bf16[64,6272]{1,0:T(8,128)(2,1)S(1)}) custom-call(s32[1]{0:T(128)} %bitcast.home, bf16[128,1024]{1,0:T(8,128)(2,1)S(1)} %get-tuple-element.15.dgate.delta, bf16[128,1024]{1,0:T(8,128)(2,1)S(1)} %get-tuple-element.16.dup.delta, bf16[1,6144,1024]{2,1,0:T(8,128)(2,1)S(1)} %bitcast.3, ...), custom_call_target="tpu_custom_call" | custom-call | flops 3221225472 | bytes 25165824 | tf_op jit(solution)/shard_map/input_grads/pallas_call | solution.py:168
  74.9 1.9 %collective-permute-done.14 = bf16[64,6272]{1,0:T(8,128)(2,1)S(1)} collective-permute-done((bf16[64,6272]{1,0:T(8,128)(2,1)S(1)}, bf16[64,6272]{1,0:T(8,128)(2,1)S(1)}, u32[]{:S(2)}, u32[]{:S(2)}) %collective-permute-start.14) | collective-permute-done | bytes 802848 | tf_op jit(solution)/shard_map/ppermute | solution.py:276
  78.0 2.0 %concatenate.36 = bf16[64,6272]{1,0:T(8,128)(2,1)} concatenate(bf16[64,6144]{1,0:T(8,128)(2,1)} %slice.132, bf16[64,4]{1,0:T(8,128)(2,1)S(1)} %get-tuple-element.26, bf16[64,4]{1,0:T(8,128)(2,1)S(1)} %get-tuple-element.25, bf16[64,120]{1,0:T(8,128)(2,1)S(1)} %broadcast_in_dim.4), dimensions={1} | concatenate | bytes 1605632 | tf_op jit(solution)/shard_map/concatenate | solution.py:298
  81.2 1.6 %collective-permute-start.17 = (bf16[16,6272]{1,0:T(8,128)(2,1)S(1)}, bf16[16,6272]{1,0:T(8,128)(2,1)S(1)}, u32[]{:S(2)}, u32[]{:S(2)}) collective-permute-start(bf16[16,6272]{1,0:T(8,128)(2,1)S(1)} %get-tuple-element.28), channel_id=1, source_target_pairs={{0,20},{4,16},{8,28},{12,24},{16,4},{20,0},{24,12},{28,8},{1,21},{... | collective-permute-start | bytes 602120 | tf_op jit(solution)/shard_map/ppermute | solution.py:273
  84.7 7.8 %columns_grad.2 = bf16[1,6144,1024]{2,1,0:T(8,128)(2,1)} custom-call(s32[1]{0:T(128)} %bitcast.home, bf16[64,6272]{1,0:T(8,128)(2,1)S(1)} %pad_maximum_fusion.xp.xpw, bf16[64,6272]{1,0:T(8,128)(2,1)S(1)} %collective-permute-done.13.xo.xow, bf16[128,1024]{1,0:T(8,128)(2,1)S(1)} %copy-done.5), custom_call_target="tpu_custom_call" | custom-call | flops 1610612736 | bytes 12582912 | tf_op jit(solution)/shard_map/columns_grad/pallas_call | solution.py:195
  92.5 7.8 %columns_grad.3 = bf16[1,6144,1024]{2,1,0:T(8,128)(2,1)} custom-call(s32[1]{0:T(128)} %bitcast.home, bf16[64,6272]{1,0:T(8,128)(2,1)S(1)} %pad_maximum_fusion.xp.xpw, bf16[64,6272]{1,0:T(8,128)(2,1)S(1)} %collective-permute-done.13.xo.xow, bf16[128,1024]{1,0:T(8,128)(2,1)S(1)} %copy-done.3), custom_call_target="tpu_custom_call" | custom-call | flops 1610612736 | bytes 12582912 | tf_op jit(solution)/shard_map/columns_grad/pallas_call | solution.py:195
  101.6 1.7 %collective-permute-start.20 = (bf16[16,1664]{1,0:T(8,128)(2,1)S(1)}, bf16[16,1664]{1,0:T(8,128)(2,1)S(1)}, u32[]{:S(2)}, u32[]{:S(2)}) collective-permute-start(bf16[16,1664]{1,0:T(8,128)(2,1)S(1)} %concatenate.40), channel_id=1, source_target_pairs={{0,1},{1,2},{2,3},{3,0},{4,5},{5,6},{6,7},{7,4},{8,9},{9,10},{10,1... | collective-permute-start | bytes 159752 | tf_op jit(solution)/shard_map/ppermute | solution.py:265
  103.5 2.1 %collective-permute-start.19 = (bf16[16,1664]{1,0:T(8,128)(2,1)S(1)}, bf16[16,1664]{1,0:T(8,128)(2,1)S(1)}, u32[]{:S(2)}, u32[]{:S(2)}) collective-permute-start(bf16[16,1664]{1,0:T(8,128)(2,1)S(1)} %concatenate.39), channel_id=1, source_target_pairs={{0,3},{1,0},{2,1},{3,2},{4,7},{5,4},{6,5},{7,6},{8,11},{9,8},{10,9... | collective-permute-start | bytes 159752 | tf_op jit(solution)/shard_map/ppermute | solution.py:265
  105.7 7.8 %down_grads.1 = bf16[1,1024,6144]{2,1,0:T(8,128)(2,1)} custom-call(s32[1]{0:T(128)} %bitcast.home, bf16[64,6144]{1,0:T(8,128)(2,1)S(1)} %pad_maximum_fusion.1.gp, bf16[64,6144]{1,0:T(8,128)(2,1)S(1)} %collective-permute-done.6.go, bf16[128,1024]{1,0:T(8,128)(2,1)S(1)} %copy-done.7), custom_call_target="tpu_custom_call" | custom-call | flops 1610612736 | bytes 12582912 | tf_op jit(solution)/shard_map/down_grads/pallas_call | solution.py:222
  (81 shorter events, 16.1 us)
Async XLA Ops:
  0.6 20.6 %collective-permute-start = (bf16[16,1536]{1,0:T(8,128)(2,1)}, bf16[16,1536]{1,0:T(8,128)(2,1)S(1)}, u32[]{:S(2)}, u32[]{:S(2)}) collective-permute-start(bf16[16,1536]{1,0:T(8,128)(2,1)} %param.8), channel_id=1, source_target_pairs={{0,1},{1,2},{2,3},{3,0},{4,5},{5,6},{6,7},{7,4},{8,9},{9,10},{10,1... | collective-permute-start | bytes 147464 | tf_op jit(solution)/shard_map/ppermute | solution.py:265
  3.7 18.0 %collective-permute-start.1 = (bf16[16,1536]{1,0:T(8,128)(2,1)}, bf16[16,1536]{1,0:T(8,128)(2,1)S(1)}, u32[]{:S(2)}, u32[]{:S(2)}) collective-permute-start(bf16[16,1536]{1,0:T(8,128)(2,1)} %param.8), channel_id=1, source_target_pairs={{0,2},{1,3},{2,0},{3,1},{4,6},{5,7},{6,4},{7,5},{8,10},{9,11},{10,... | collective-permute-start | bytes 147464 | tf_op jit(solution)/shard_map/ppermute | solution.py:265
  6.3 15.5 %collective-permute-start.2 = (bf16[16,1536]{1,0:T(8,128)(2,1)}, bf16[16,1536]{1,0:T(8,128)(2,1)S(1)}, u32[]{:S(2)}, u32[]{:S(2)}) collective-permute-start(bf16[16,1536]{1,0:T(8,128)(2,1)} %param.8), channel_id=1, source_target_pairs={{0,3},{1,0},{2,1},{3,2},{4,7},{5,4},{6,5},{7,6},{8,11},{9,8},{10,9... | collective-permute-start | bytes 147464 | tf_op jit(solution)/shard_map/ppermute | solution.py:265
  7.6 6.2 %collective-permute-start.7 = (bf16[16,1536]{1,0:T(8,128)(2,1)}, bf16[16,1536]{1,0:T(8,128)(2,1)S(1)}, u32[]{:S(2)}, u32[]{:S(2)}) collective-permute-start(bf16[16,1536]{1,0:T(8,128)(2,1)} %param.7), channel_id=1, source_target_pairs={{0,1},{1,2},{2,3},{3,0},{4,5},{5,6},{6,7},{7,4},{8,9},{9,10},{10,1... | collective-permute-start | bytes 147464 | tf_op jit(solution)/shard_map/ppermute | solution.py:265
  8.3 6.3 %collective-permute-start.8 = (bf16[16,1536]{1,0:T(8,128)(2,1)}, bf16[16,1536]{1,0:T(8,128)(2,1)S(1)}, u32[]{:S(2)}, u32[]{:S(2)}) collective-permute-start(bf16[16,1536]{1,0:T(8,128)(2,1)} %param.7), channel_id=1, source_target_pairs={{0,2},{1,3},{2,0},{3,1},{4,6},{5,7},{6,4},{7,5},{8,10},{9,11},{10,... | collective-permute-start | bytes 147464 | tf_op jit(solution)/shard_map/ppermute | solution.py:265
  13.8 4.3 %collective-permute-start.9 = (bf16[16,1536]{1,0:T(8,128)(2,1)}, bf16[16,1536]{1,0:T(8,128)(2,1)S(1)}, u32[]{:S(2)}, u32[]{:S(2)}) collective-permute-start(bf16[16,1536]{1,0:T(8,128)(2,1)} %param.7), channel_id=1, source_target_pairs={{0,3},{1,0},{2,1},{3,2},{4,7},{5,4},{6,5},{7,6},{8,11},{9,8},{10,9... | collective-permute-start | bytes 147464 | tf_op jit(solution)/shard_map/ppermute | solution.py:265
  18.2 9.0 %collective-permute-start.12 = (bf16[16,6272]{1,0:T(8,128)(2,1)S(1)}, bf16[16,6272]{1,0:T(8,128)(2,1)S(1)}, u32[]{:S(2)}, u32[]{:S(2)}) collective-permute-start(bf16[16,6272]{1,0:T(8,128)(2,1)S(1)} %constant_dynamic-update-slice_fusion.4), channel_id=1, source_target_pairs={{0,20},{4,16},{8,28},{12,24},{16,4},{20,0},{24,12},{28,8},{1,21},{... | collective-permute-start | bytes 602120 | tf_op jit(solution)/shard_map/ppermute | solution.py:273
  20.7 10.7 %collective-permute-start.11 = (bf16[16,6272]{1,0:T(8,128)(2,1)S(1)}, bf16[16,6272]{1,0:T(8,128)(2,1)S(1)}, u32[]{:S(2)}, u32[]{:S(2)}) collective-permute-start(bf16[16,6272]{1,0:T(8,128)(2,1)S(1)} %constant_dynamic-update-slice_fusion.4), channel_id=1, source_target_pairs={{0,4},{4,0},{8,12},{12,8},{16,20},{20,16},{24,28},{28,24},{1,5},{5... | collective-permute-start | bytes 602120 | tf_op jit(solution)/shard_map/ppermute | solution.py:273
  21.2 10.3 %collective-permute-start.10 = (bf16[16,6272]{1,0:T(8,128)(2,1)S(1)}, bf16[16,6272]{1,0:T(8,128)(2,1)S(1)}, u32[]{:S(2)}, u32[]{:S(2)}) collective-permute-start(bf16[16,6272]{1,0:T(8,128)(2,1)S(1)} %constant_dynamic-update-slice_fusion.4), channel_id=1, source_target_pairs={{0,16},{4,20},{8,24},{12,28},{16,0},{20,4},{24,8},{28,12},{1,17},{... | collective-permute-start | bytes 602120 | tf_op jit(solution)/shard_map/ppermute | solution.py:273
  21.8 12.1 %collective-permute-start.5 = (bf16[16,6144]{1,0:T(8,128)(2,1)S(1)}, bf16[16,6144]{1,0:T(8,128)(2,1)S(1)}, u32[]{:S(2)}, u32[]{:S(2)}) collective-permute-start(bf16[16,6144]{1,0:T(8,128)(2,1)S(1)} %constant_dynamic-update-slice_fusion), channel_id=1, source_target_pairs={{0,20},{4,16},{8,28},{12,24},{16,4},{20,0},{24,12},{28,8},{1,21},{... | collective-permute-start | bytes 589832 | tf_op jit(solution)/shard_map/ppermute | solution.py:273
  24.3 11.3 %collective-permute-start.4 = (bf16[16,6144]{1,0:T(8,128)(2,1)S(1)}, bf16[16,6144]{1,0:T(8,128)(2,1)S(1)}, u32[]{:S(2)}, u32[]{:S(2)}) collective-permute-start(bf16[16,6144]{1,0:T(8,128)(2,1)S(1)} %constant_dynamic-update-slice_fusion), channel_id=1, source_target_pairs={{0,4},{4,0},{8,12},{12,8},{16,20},{20,16},{24,28},{28,24},{1,5},{5... | collective-permute-start | bytes 589832 | tf_op jit(solution)/shard_map/ppermute | solution.py:273
  27.2 8.6 %collective-permute-start.3 = (bf16[16,6144]{1,0:T(8,128)(2,1)S(1)}, bf16[16,6144]{1,0:T(8,128)(2,1)S(1)}, u32[]{:S(2)}, u32[]{:S(2)}) collective-permute-start(bf16[16,6144]{1,0:T(8,128)(2,1)S(1)} %constant_dynamic-update-slice_fusion), channel_id=1, source_target_pairs={{0,16},{4,20},{8,24},{12,28},{16,0},{20,4},{24,8},{28,12},{1,17},{... | collective-permute-start | bytes 589832 | tf_op jit(solution)/shard_map/ppermute | solution.py:273
  31.5 4.4 %collective-permute-start.13 = (bf16[64,6272]{1,0:T(8,128)(2,1)S(1)}, bf16[64,6272]{1,0:T(8,128)(2,1)S(1)}, u32[]{:S(2)}, u32[]{:S(2)}) collective-permute-start(bf16[64,6272]{1,0:T(8,128)(2,1)S(1)} %pad_maximum_fusion.xp.xpw), channel_id=1, source_target_pairs={{0,8},{8,0},{16,24},{24,16},{1,9},{9,1},{17,25},{25,17},{2,10},{10... | collective-permute-start | bytes 2408456 | tf_op jit(solution)/shard_map/ppermute | solution.py:276
  35.8 14.9 %collective-permute-start.6 = (bf16[64,6144]{1,0:T(8,128)(2,1)S(1)}, bf16[64,6144]{1,0:T(8,128)(2,1)S(1)}, u32[]{:S(2)}, u32[]{:S(2)}) collective-permute-start(bf16[64,6144]{1,0:T(8,128)(2,1)S(1)} %pad_maximum_fusion.1.gp), channel_id=1, source_target_pairs={{0,8},{8,0},{16,24},{24,16},{1,9},{9,1},{17,25},{25,17},{2,10},{10... | collective-permute-start | bytes 2359304 | tf_op jit(solution)/shard_map/ppermute | solution.py:276
  40.5 21.9 %slice-start = ((s8[12582912]{0:T(1024)(128)(4,1)}), s8[4194304]{0:T(1024)(128)(4,1)S(1)}, s32[]{:S(2)}) async-start(s8[12582912]{0:T(1024)(128)(4,1)} %bitcast.2), calls=%async_computation | async-start | bytes 8388608
  40.5 21.9 %slice-start.1 = ((s8[12582912]{0:T(1024)(128)(4,1)}), s8[4194304]{0:T(1024)(128)(4,1)S(1)}, s32[]{:S(2)}) async-start(s8[12582912]{0:T(1024)(128)(4,1)} %bitcast.2), calls=%async_computation.1 | async-start | bytes 8388608
  62.4 12.4 %copy-start.8 = (s32[16,2]{0,1:T(2,128)S(1)}, s32[16,2]{0,1:T(2,128)}, u32[]{:S(2)}) copy-start(s32[16,2]{0,1:T(2,128)} %param.9) | copy-start | bytes 388
  74.3 2.5 %collective-permute-start.14 = (bf16[64,6272]{1,0:T(8,128)(2,1)S(1)}, bf16[64,6272]{1,0:T(8,128)(2,1)S(1)}, u32[]{:S(2)}, u32[]{:S(2)}) collective-permute-start(bf16[64,6272]{1,0:T(8,128)(2,1)S(1)} %get-tuple-element.19), channel_id=1, source_target_pairs={{0,8},{8,0},{16,24},{24,16},{1,9},{9,1},{17,25},{25,17},{2,10},{10... | collective-permute-start | bytes 2408456 | tf_op jit(solution)/shard_map/ppermute | solution.py:276
  81.2 19.2 %collective-permute-start.17 = (bf16[16,6272]{1,0:T(8,128)(2,1)S(1)}, bf16[16,6272]{1,0:T(8,128)(2,1)S(1)}, u32[]{:S(2)}, u32[]{:S(2)}) collective-permute-start(bf16[16,6272]{1,0:T(8,128)(2,1)S(1)} %get-tuple-element.28), channel_id=1, source_target_pairs={{0,20},{4,16},{8,28},{12,24},{16,4},{20,0},{24,12},{28,8},{1,21},{... | collective-permute-start | bytes 602120 | tf_op jit(solution)/shard_map/ppermute | solution.py:273
  82.8 17.5 %collective-permute-start.16 = (bf16[16,6272]{1,0:T(8,128)(2,1)S(1)}, bf16[16,6272]{1,0:T(8,128)(2,1)S(1)}, u32[]{:S(2)}, u32[]{:S(2)}) collective-permute-start(bf16[16,6272]{1,0:T(8,128)(2,1)S(1)} %get-tuple-element.29), channel_id=1, source_target_pairs={{0,4},{4,0},{8,12},{12,8},{16,20},{20,16},{24,28},{28,24},{1,5},{5... | collective-permute-start | bytes 602120 | tf_op jit(solution)/shard_map/ppermute | solution.py:273
  84.2 16.1 %collective-permute-start.15 = (bf16[16,6272]{1,0:T(8,128)(2,1)S(1)}, bf16[16,6272]{1,0:T(8,128)(2,1)S(1)}, u32[]{:S(2)}, u32[]{:S(2)}) collective-permute-start(bf16[16,6272]{1,0:T(8,128)(2,1)S(1)} %get-tuple-element.27), channel_id=1, source_target_pairs={{0,16},{4,20},{8,24},{12,28},{16,0},{20,4},{24,8},{28,12},{1,17},{... | collective-permute-start | bytes 602120 | tf_op jit(solution)/shard_map/ppermute | solution.py:273
  101.6 11.9 %collective-permute-start.20 = (bf16[16,1664]{1,0:T(8,128)(2,1)S(1)}, bf16[16,1664]{1,0:T(8,128)(2,1)S(1)}, u32[]{:S(2)}, u32[]{:S(2)}) collective-permute-start(bf16[16,1664]{1,0:T(8,128)(2,1)S(1)} %concatenate.40), channel_id=1, source_target_pairs={{0,1},{1,2},{2,3},{3,0},{4,5},{5,6},{6,7},{7,4},{8,9},{9,10},{10,1... | collective-permute-start | bytes 159752 | tf_op jit(solution)/shard_map/ppermute | solution.py:265
  103.5 10.1 %collective-permute-start.19 = (bf16[16,1664]{1,0:T(8,128)(2,1)S(1)}, bf16[16,1664]{1,0:T(8,128)(2,1)S(1)}, u32[]{:S(2)}, u32[]{:S(2)}) collective-permute-start(bf16[16,1664]{1,0:T(8,128)(2,1)S(1)} %concatenate.39), channel_id=1, source_target_pairs={{0,3},{1,0},{2,1},{3,2},{4,7},{5,4},{6,5},{7,6},{8,11},{9,8},{10,9... | collective-permute-start | bytes 159752 | tf_op jit(solution)/shard_map/ppermute | solution.py:265
  105.6 7.9 %collective-permute-start.18 = (bf16[16,1664]{1,0:T(8,128)(2,1)S(1)}, bf16[16,1664]{1,0:T(8,128)(2,1)S(1)}, u32[]{:S(2)}, u32[]{:S(2)}) collective-permute-start(bf16[16,1664]{1,0:T(8,128)(2,1)S(1)} %concatenate.38), channel_id=1, source_target_pairs={{0,2},{1,3},{2,0},{3,1},{4,6},{5,7},{6,4},{7,5},{8,10},{9,11},{10,... | collective-permute-start | bytes 159752 | tf_op jit(solution)/shard_map/ppermute | solution.py:265
  (9 other events, 72.6 us)

commit v2 on v0

v2 whole, which is shorter than its diff:
```python
import functools

import jax
import jax.numpy as jnp
from jax import lax
from jax.experimental import pallas as pl
from jax.experimental.pallas import tpu as pltpu
from jax.sharding import PartitionSpec as P

EXTRA = 128
MIB = 1 << 20
PLAIN = (((1,), (0,)), ((), ()))
CONTRACT_ROWS = (((0,), (0,)), ((), ()))
CONTRACT_COLS = (((1,), (1,)), ((), ()))
VMEM = pl.BlockSpec(memory_space=pltpu.VMEM)
SMEM = pl.BlockSpec(memory_space=pltpu.SMEM)
ANY = pl.BlockSpec(memory_space=pl.ANY)
HBM = pl.BlockSpec(memory_space=pltpu.HBM)


def matmul(a, b, dims=PLAIN):
    return lax.dot_general(a, b, dims, preferred_element_type=jnp.float32)


def shaped(shape, dtype=jnp.bfloat16):
    return jax.ShapeDtypeStruct(shape, dtype)


def local_call(
    body, name, mib, flops, moved, in_specs, out_specs, out_shape, scratch=(), aliases=None
):
    return pl.pallas_call(
        body,
        in_specs=in_specs,
        out_specs=out_specs,
        out_shape=out_shape,
        scratch_shapes=list(scratch),
        input_output_aliases=aliases or {},
        compiler_params=pltpu.CompilerParams(vmem_limit_bytes=mib * MIB),
        cost_estimate=pl.CostEstimate(
            flops=int(flops), bytes_accessed=int(moved), transcendentals=0
        ),
        name=name,
    )


def chunk_of(features):
    for size in (768, 512, 384, 256, 128):
        if features % size == 0:
            return size
    return features


def whole_chunks(home, pieces, depth):
    width = depth // pieces
    size = chunk_of(width)
    found = []
    for k in range(pieces):
        owner = lax.rem(home - k + pieces, pieces)
        for c in range(width // size):
            start = pl.multiple_of(owner * width + c * size, size)
            found.append((k * width + c * size, start))
    return size, found


def both_rows(near, far, start, size):
    return jnp.concatenate([near[:, start : start + size], far[:, start : start + size]], axis=0)


def turned_kernel(place, w, *refs, pieces, by_rows, first, count):
    *outs, buf, sems = refs[-count - 2 :]
    depth = w.shape[1] if by_rows else w.shape[2]
    width = depth // pieces
    size, chunks = whole_chunks(place[0], pieces, depth)
    chunks = [c for c in chunks if first <= c[0] // width < first + count]
    slots = buf.shape[0]

    def copy(j):
        span = pl.ds(chunks[j][1], size)
        source = w.at[0, span] if by_rows else w.at[0, :, span]
        return pltpu.make_async_copy(source, buf.at[j % slots], sems.at[j % slots])

    for j in range(min(slots, len(chunks))):
        copy(j).start()
    for j, (rel, _) in enumerate(chunks):
        copy(j).wait()
        out, base = outs[rel // width - first], rel % width
        for at in range(0, buf.shape[2], EXTRA):
            value = buf[j % slots, :, at : at + EXTRA].T
            if by_rows:
                out[at : at + EXTRA, base : base + size] = value
            else:
                out[base + at : base + at + EXTRA, :] = value
        if j + slots < len(chunks):
            copy(j + slots).start()


def turned(place, pieces, weights, by_rows, which, after=()):
    _, up_to, across = weights.shape
    depth, hidden = (up_to, across) if by_rows else (across, up_to)
    width = depth // pieces
    size = chunk_of(width)
    shape = (hidden, width) if by_rows else (width, hidden)
    return local_call(
        functools.partial(
            turned_kernel, pieces=pieces, by_rows=by_rows, first=which.start, count=len(which)
        ),
        "turned",
        8,
        0,
        0,
        [SMEM, HBM] + [ANY] * len(after),
        [VMEM] * len(which),
        [shaped(shape)] * len(which),
        [
            pltpu.VMEM((4, size, hidden) if by_rows else (4, hidden, size), jnp.bfloat16),
            pltpu.SemaphoreType.DMA((4,)),
        ],
    )(place, pltpu.with_memory_space_constraint(weights, pltpu.HBM), *after)


def gate_up_kernel(place, xp, xo, *refs, pieces):
    weights, (gate, up, weight) = refs[: 2 * pieces], refs[2 * pieces :]
    hidden, width = weights[0].shape
    for half, out in ((weights[:pieces], gate), (weights[pieces:], up)):
        for k, w in enumerate(half):
            rows = both_rows(xp, xo, k * width, width)
            for at in range(0, hidden, EXTRA):
                value = matmul(rows, w[at : at + EXTRA, :], CONTRACT_COLS)
                if k == 0:
                    out[:, at : at + EXTRA] = value
                else:
                    out[:, at : at + EXTRA] += value
    lane = lax.broadcasted_iota(jnp.int32, (1, EXTRA), 1)
    mine = both_rows(xp, xo, width * pieces, EXTRA).astype(jnp.float32)
    total = jnp.sum(jnp.where(lane == place[1], mine, 0.0), axis=1, keepdims=True)
    weight[...] = jnp.broadcast_to(total, weight.shape)


def gate_up(place, near, far, turned_gate, turned_up):
    half = near.shape[0]
    pieces = len(turned_gate)
    hidden = turned_gate[0].shape[0]
    out = shaped((2 * half, hidden), jnp.float32)
    return local_call(
        functools.partial(gate_up_kernel, pieces=pieces),
        "gate_up",
        3,
        0,
        0,
        [SMEM] + [VMEM] * (2 + 2 * pieces),
        [VMEM] * 3,
        [out, out, shaped((2 * half, EXTRA), jnp.float32)],
    )(place, near, far, *turned_gate, *turned_up)


def middle_kernel(
    place, gp, go, weight_in, gate, up, *refs, pieces, experts
):
    wd, wg, wu = refs[:pieces], refs[pieces : 2 * pieces], refs[2 * pieces : 3 * pieces]
    near, far, dgate, dup, hidw, raw = refs[3 * pieces :]
    width = wg[0].shape[1]
    half = near.shape[0]
    depth = width * pieces
    for k in range(pieces):
        value = matmul(both_rows(gp, go, k * width, width), wd[k][...])
        if k == 0:
            raw[...] = value
        else:
            raw[...] += value
    lane = lax.broadcasted_iota(jnp.int32, (1, EXTRA), 1)
    mine = lane == place[1]
    weight = weight_in[:, :1]
    gate_value = gate[...]
    up_value = up[...]
    raw_value = raw[...]
    sigmoid_gate = jax.nn.sigmoid(gate_value)
    activated = gate_value * sigmoid_gate
    hidden_value = activated * up_value
    scaled = weight * raw_value
    slope = sigmoid_gate * (1.0 + gate_value * (1.0 - sigmoid_gate))
    dgate[...] = (scaled * up_value * slope).astype(jnp.bfloat16)
    dup[...] = (scaled * activated).astype(jnp.bfloat16)
    hidw[...] = (weight * hidden_value).astype(jnp.bfloat16)
    total = jnp.sum(hidden_value * raw_value, axis=1, keepdims=True)
    high = total.astype(jnp.bfloat16).astype(jnp.float32)
    low = total - high
    placed = jnp.where(mine, high, 0.0) + jnp.where(lane == place[1] + experts, low, 0.0)
    placed = placed.astype(jnp.bfloat16)
    near[:, depth:] = placed[:half]
    far[:, depth:] = placed[half:]
    step = chunk_of(width)
    for at in range(0, depth, step):
        k, base = at // width, at % width
        span = slice(base, base + step)
        value = matmul(dgate[...], wg[k][:, span]) + matmul(dup[...], wu[k][:, span])
        value = value.astype(jnp.bfloat16)
        near[:, at : at + step] = value[:half]
        far[:, at : at + step] = value[half:]


def middle(place, experts, pieces, near, far, weight, gate, up, turned_down, turned_gate, turned_up):
    half = near.shape[0]
    hidden, width = turned_gate[0].shape
    depth = width * pieces
    out = shaped((2 * half, hidden))
    result = shaped((half, depth + EXTRA))
    return local_call(
        functools.partial(middle_kernel, pieces=pieces, experts=experts),
        "middle",
        4,
        0,
        0,
        [SMEM] + [VMEM] * (5 + 3 * pieces),
        [VMEM] * 5,
        [result, result, out, out, out],
        [pltpu.VMEM((2 * half, hidden), jnp.float32)],
    )(place, near, far, weight, gate, up, *turned_down, *turned_gate, *turned_up)


def columns_kernel(place, xp, xo, delta, out, buf, sems, *, pieces):
    depth = out.shape[1]
    size, chunks = whole_chunks(place[0], pieces, depth)
    copies = []
    for j, (rel, start) in enumerate(chunks):
        rows = both_rows(xp, xo, rel, size)
        slot = j
        buf[slot] = matmul(rows, delta[...], CONTRACT_ROWS).astype(jnp.bfloat16)
        copy = pltpu.make_async_copy(
            buf.at[slot], out.at[0, pl.ds(start, size)], sems.at[slot]
        )
        copy.start()
        copies.append(copy)
    for copy in copies:
        copy.wait()


def columns_grad(place, pieces, near, far, delta, depth):
    half = near.shape[0]
    hidden = delta.shape[1]
    count = depth // chunk_of(depth // pieces)
    return local_call(
        functools.partial(columns_kernel, pieces=pieces),
        "columns_grad",
        16,
        4 * half * depth * hidden,
        2 * depth * hidden,
        [SMEM, VMEM, VMEM, VMEM],
        ANY,
        shaped((1, depth, hidden)),
        [
            pltpu.VMEM((count, chunk_of(depth // pieces), hidden), jnp.bfloat16),
            pltpu.SemaphoreType.DMA((count,)),
        ],
    )(place, near, far, delta)


def down_kernel(place, gp, go, hidw, *refs, pieces, first, last):
    out, buf, sems = refs[-3:]
    depth = out.shape[2]
    size, chunks = whole_chunks(place[0], pieces, depth)
    copies = []
    for j, (rel, start) in enumerate(chunks[first:last]):
        rows = both_rows(gp, go, rel, size)
        buf[j] = matmul(hidw[...], rows, CONTRACT_ROWS).astype(jnp.bfloat16)
        copy = pltpu.make_async_copy(buf.at[j], out.at[0, :, pl.ds(start, size)], sems.at[j])
        copy.start()
        copies.append(copy)
    for copy in copies:
        copy.wait()


def down_grads(place, pieces, near, far, hidw, depth, first, last, partial=()):
    half = near.shape[0]
    hidden = hidw.shape[1]
    count = last - first
    size = chunk_of(depth // pieces)
    partial = [pltpu.with_memory_space_constraint(p, pltpu.HBM) for p in partial]
    return local_call(
        functools.partial(down_kernel, pieces=pieces, first=first, last=last),
        "down_grads",
        16,
        4 * half * size * count * hidden,
        2 * size * count * hidden,
        [SMEM, VMEM, VMEM, VMEM] + [HBM] * len(partial),
        ANY,
        shaped((1, hidden, depth)),
        [
            pltpu.VMEM((count, hidden, size), jnp.bfloat16),
            pltpu.SemaphoreType.DMA((count,)),
        ],
        aliases={4: 0} if partial else None,
    )(place, near, far, hidw, *partial)


def stack_kernel(*refs, axis, count):
    out = refs[-1]
    at = 0
    for ref in refs[:count]:
        size = ref.shape[axis]
        if axis:
            out[:, at : at + size] = ref[...]
        else:
            out[at : at + size, :] = ref[...]
        at += size


def stacked(blocks, axis, after=()):
    shape = list(blocks[0].shape)
    shape[axis] = sum(b.shape[axis] for b in blocks)
    count = shape[0] * shape[1]
    return local_call(
        functools.partial(stack_kernel, axis=axis, count=len(blocks)),
        "stacked",
        2,
        0,
        4 * count,
        [VMEM] * len(blocks) + [ANY] * len(after),
        VMEM,
        shaped(tuple(shape)),
    )(*blocks, *after)


def first_kernel(x, g, out, sems):
    rows = x.shape[0]
    copies = [
        pltpu.make_async_copy(ref, out.at[pl.ds(i * rows, rows)], sems.at[i])
        for i, ref in enumerate((x, g))
    ]
    for copy in copies:
        copy.start()
    for copy in copies:
        copy.wait()


def first_pair(x, g):
    rows, width = x.shape
    return local_call(
        first_kernel,
        "first_pair",
        1,
        0,
        8 * rows * width,
        [HBM] * 2,
        VMEM,
        shaped((2 * rows, width)),
        [pltpu.SemaphoreType.DMA((2,))],
    )(*(pltpu.with_memory_space_constraint(v, pltpu.HBM) for v in (x, g)))


def line_pair_kernel(*refs):
    *blocks, extra, _, line_x, line_g = refs
    rows = line_x.shape[0]
    width = blocks[0].shape[1]
    for k, block in enumerate(blocks):
        line_x[:, k * width : (k + 1) * width] = block[:rows, :]
        line_g[:, k * width : (k + 1) * width] = block[rows:, :]
    line_x[:, len(blocks) * width :] = extra[...]


def line_pair(blocks, extra, after):
    rows = extra.shape[0]
    depth = blocks[0].shape[1] * len(blocks)
    return local_call(
        line_pair_kernel,
        "line_pair",
        2,
        0,
        8 * rows * depth,
        [VMEM] * (len(blocks) + 1) + [ANY],
        [VMEM] * 2,
        [shaped((rows, depth + EXTRA)), shaped((rows, depth))],
    )(*blocks, extra, after)


def resplit(extra, experts):
    lane = lax.broadcasted_iota(jnp.int32, extra.shape, 1)
    total = extra + pltpu.roll(extra, EXTRA - experts, 1)
    total = jnp.where(lane < experts, total, 0.0)
    high = total.astype(jnp.bfloat16).astype(jnp.float32)
    return (high + pltpu.roll(total - high, experts, 1)).astype(jnp.bfloat16)


def pair_kernel(near, other, *outs, experts):
    rows, width = outs[0].shape
    depth = width - EXTRA
    for i, out in enumerate(outs):
        span = pl.ds(i * rows, rows)
        value = near[span, :].astype(jnp.float32) + other[span, :].astype(jnp.float32)
        out[:, :depth] = value[:, :depth].astype(jnp.bfloat16)
        out[:, depth:] = resplit(value[:, depth:], experts)


def pair_sums(near, other, experts, count):
    rows, width = near.shape[0] // count, near.shape[1]
    return local_call(
        functools.partial(pair_kernel, experts=experts),
        "pair_sums",
        2,
        0,
        6 * near.size,
        [VMEM] * 2,
        [VMEM] * count,
        [shaped((rows, width))] * count,
    )(near, other)


def plane_kernel(*refs, experts, pieces):
    blocks, outs = refs[:-pieces], refs[-pieces:]
    width = outs[0].shape[1] - EXTRA
    depth = width * pieces

    def total(start, size):
        values = [b[:, start : start + size].astype(jnp.float32) for b in blocks]
        return functools.reduce(lambda a, b: a + b, values)

    extra = resplit(total(depth, EXTRA), experts)
    for k, out in enumerate(outs):
        out[:, :width] = total(k * width, width).astype(jnp.bfloat16)
        out[:, width:] = extra


def plane_sums(blocks, experts, pieces):
    rows, width = blocks[0].shape[0], (blocks[0].shape[1] - EXTRA) // pieces + EXTRA
    return local_call(
        functools.partial(plane_kernel, experts=experts, pieces=pieces),
        "plane_sums",
        2,
        0,
        2 * blocks[0].size * len(blocks),
        [VMEM] * len(blocks),
        [VMEM] * pieces,
        [shaped((rows, width))] * pieces,
    )(*blocks)


def tree_sum(parts):
    while len(parts) > 1:
        middle = len(parts) // 2
        parts = [a + b for a, b in zip(parts[:middle], parts[middle:], strict=True)]
    return parts[0]


def line_kernel(*refs, experts):
    blocks, (grads, routes) = refs[:-2], refs[-2:]
    width = grads.shape[1]
    grads[...] = tree_sum([b[:, :width].astype(jnp.float32) for b in blocks]).astype(jnp.bfloat16)
    extra = tree_sum([b[:, width:].astype(jnp.float32) for b in blocks])
    total = extra + pltpu.roll(extra, EXTRA - experts, 1)
    routes[...] = total.astype(jnp.bfloat16).astype(jnp.float32)


def line_sums(blocks, experts):
    rows, width = blocks[0].shape[0], blocks[0].shape[1] - EXTRA
    return local_call(
        functools.partial(line_kernel, experts=experts),
        "line_sums",
        2,
        0,
        2 * blocks[0].size * len(blocks),
        [VMEM] * len(blocks),
        [VMEM] * 2,
        [shaped((rows, width)), shaped((rows, EXTRA), jnp.float32)],
    )(*blocks)


def per_device(tokens_in, out_grad, route_ids, route_weight, gate_weight, up_weight, down_weight):
    experts = lax.axis_size("expert")
    seqs = lax.axis_size("seq")
    pieces = lax.axis_size("tensor")
    depth = tokens_in.shape[1] * pieces
    place = jnp.stack([lax.axis_index("tensor"), lax.axis_index("expert")]).astype(jnp.int32)
    chips = experts // 2
    planes = [(dx, ds) for ds in range(seqs) for dx in range(chips)]

    def along(value, shift):
        pairs = [(i, (i + shift) % pieces) for i in range(pieces)]
        return lax.ppermute(value, "tensor", pairs)

    def across(value, dx, ds):
        pairs = []
        for e in range(experts):
            for s in range(seqs):
                to_e = ((e // 2 + dx) % chips) * 2 + e % 2
                pairs.append((e * seqs + s, to_e * seqs + (s + ds) % seqs))
        return lax.ppermute(value, ("expert", "seq"), pairs)

    def swap(value):
        return lax.ppermute(value, "expert", [(e, e ^ 1) for e in range(experts)])

    expert_ids = jnp.arange(EXTRA, dtype=jnp.int32)
    chosen = (route_ids[:, :, None] == expert_ids[None, None, :]).astype(jnp.float32)
    weights = jnp.sum(chosen * route_weight.astype(jnp.float32)[:, :, None], axis=1)
    both = first_pair(tokens_in, out_grad)
    arrived = [along(both, k) for k in range(1, pieces)]
    early, late = range(pieces // 2), range(pieces // 2, pieces)
    turned_down = turned(place, pieces, down_weight, False, early)
    line_x, line_g = line_pair([both] + arrived, weights.astype(jnp.bfloat16), turned_down[0])
    from_x = [across(line_x, dx, ds) for dx, ds in planes[1:]]
    turned_gate = turned(place, pieces, gate_weight, True, range(pieces))
    turned_up = turned(place, pieces, up_weight, True, early)
    near_x = stacked([line_x] + from_x, 0, [turned_gate[0], turned_up[0]])
    far_x = swap(near_x)
    from_g = [across(line_g, dx, ds) for dx, ds in planes[1:]]
    turned_up = turned_up + turned(place, pieces, up_weight, True, late, [near_x])
    gate, up, weight = gate_up(place, near_x, far_x, turned_gate, turned_up)
    near_g = stacked([line_g] + from_g, 0, [weight])
    far_g = swap(near_g)
    turned_down = turned_down + turned(place, pieces, down_weight, False, late, [near_g])
    near_d, far_d, dgate, dup, hidw = middle(
        place, experts, pieces, near_g, far_g, weight, gate, up, turned_down, turned_gate, turned_up
    )

    other_d = swap(far_d)
    chunks = depth // chunk_of(depth // pieces)
    down_grad = down_grads(place, pieces, near_g, far_g, hidw, depth, 0, chunks // 2)
    gate_grad = columns_grad(place, pieces, near_x, far_x, dgate, depth)
    up_grad = columns_grad(place, pieces, near_x, far_x, dup, depth)
    down_grad = down_grads(
        place, pieces, near_g, far_g, hidw, depth, chunks // 2, chunks, [down_grad]
    )

    blocks = pair_sums(near_d, other_d, experts, len(planes))
    arrived = [
        across(block, -dx, -ds) for block, (dx, ds) in zip(blocks[1:], planes[1:], strict=True)
    ]
    sends = plane_sums([blocks[0]] + arrived, experts, pieces)
    finals = [sends[0]] + [along(sends[k], -k) for k in range(1, pieces)]
    x_grad, routes = line_sums(finals, experts)
    route_grad = jnp.sum(chosen * routes[:, None, :], axis=2).astype(jnp.bfloat16)
    return (x_grad, route_grad, gate_grad, up_grad, down_grad)


def solution(mesh):
    in_specs = (
        P(("expert", "seq"), "tensor"),
        P(("expert", "seq"), "tensor"),
        P(("expert", "seq"), None),
        P(("expert", "seq"), None),
        P("expert", None, ("seq", "tensor")),
        P("expert", None, ("seq", "tensor")),
        P("expert", ("seq", "tensor"), None),
    )
    out_specs = (
        P(("expert", "seq"), "tensor"),
        P(("expert", "seq"), None),
        P("expert", None, ("seq", "tensor")),
        P("expert", None, ("seq", "tensor")),
        P("expert", ("seq", "tensor"), None),
    )
    return jax.shard_map(
        per_device, mesh=mesh, in_specs=in_specs, out_specs=out_specs, check_vma=False
    )
```

time: 236 us -> 84.2 us (0.36)
  blocking collectives: 73.7 us -> 0 us
  matrix products: 68.5 us -> 0 us
  Pallas kernels: 0 us -> 56.7 us
  waiting for transfers between devices: 55.3 us -> 2.26 us
  between operations: 14 us -> 0.9 us
  starting transfers between devices: 17.3 us -> 22.7 us
  local copies, waits for them, and re-layouts: 3.28 us -> 0.01 us
    dot_general x13 -> x0, matrix products: 68.5 us -> none  [the longest x1 10.6 us: per_device(): lax.dot_general(flat_gate, w_gate, contract_cols, preferred_element_type=...]
    pallas_call x0 -> x18, Pallas kernels: none -> 56.7 us  [the longest x5 21.5 us: turned(): local_call(functools.partial(turned_kernel, pieces=pieces, by_rows=by_row...]
    all_gather x3 -> x0, blocking collectives: 43.4 us -> none  [the longest x1 20.3 us: per_device(): lax.all_gather(recv_rows, 'tensor', axis=2, tiled=True)]
    reduce_scatter x1 -> x0, waiting for transfers between devices: 35.3 us -> none  [per_device(): lax.psum_scatter(result + lax.dot_general(flat_up, w_up, contract_cols, p...]
    ppermute x0 -> x18, starting transfers between devices: none -> 22.7 us  [the longest x6 11.3 us: along(): return lax.ppermute(value, 'tensor', pairs)]
    psum x1 -> x0, blocking collectives: 21 us -> none  [per_device(): totals = lax.psum(parts_all, ('seq', 'tensor'))]
    all_to_all x5 -> x0, starting transfers between devices: 17.2 us -> none  [the longest x1 3.99 us: per_device(): lax.all_to_all(shares.astype(jnp.bfloat16), 'tensor', split_axis=1, conca...]
    all_gather x2 -> x0, waiting for transfers between devices: 12.7 us -> none  [the longest x1 12.7 us: per_device(): grads_piece = lax.all_gather(full_grads, 'seq', axis=0, tiled=True)]
  transfers between devices with their start and end apart: 8 -> 18, of which waited for: 5 -> 3; matrix products, arithmetic and copies ran while one was open for 18% -> 1% of each run, Pallas kernels for 0% -> 58%
where the time goes in v2:
time: 84.2 us; the launch traced here: 84 us
  Pallas kernels  56.7 us (67%)
  starting transfers between devices  22.7 us (27%)
  waiting for transfers between devices  2.26 us (3%)
  other arithmetic  1.47 us (2%)
  between operations  0.9 us (1%)
    pallas_call x5, Pallas kernels, turned(): local_call(functools.partial(turned_kernel, pieces=pieces, by_rows=by_row...  21.5 us
    pallas_call x2, Pallas kernels, columns_grad(): local_call(functools.partial(columns_kernel, pieces=pieces), 'columns_gra...  11.6 us
    ppermute x6, starting transfers between devices, along(): return lax.ppermute(value, 'tensor', pairs)  11.3 us
    ppermute x9, starting transfers between devices, across(): return lax.ppermute(value, ('expert', 'seq'), pairs)  10.7 us
    pallas_call x2, Pallas kernels, down_grads(): local_call(functools.partial(down_kernel, pieces=pieces, first=first, las...  8 us
    pallas_call x1, Pallas kernels, gate_up(): local_call(functools.partial(gate_up_kernel, pieces=pieces), 'gate_up', 3...  7.37 us
    pallas_call x1, Pallas kernels, middle(): local_call(functools.partial(middle_kernel, pieces=pieces, experts=expert...  6.08 us
    ppermute x6, waiting for transfers between devices, along(): return lax.ppermute(value, 'tensor', pairs)  2.22 us
  transfers between devices with their start and end apart: 18, of which 3 were waited for; matrix products, arithmetic and copies ran while one was open for 1% of the time, Pallas kernels for 58%

profile of v2, /device:TPU:0, one launch (start us, length us, event | category | flops | bytes accessed | tf_op | source)
XLA Modules:
  0.0 84.0 jit_solution(16715669713077504714)
XLA Ops:
  0.6 0.8 %first_pair.1.refs_0_ = bf16[32,1536]{1,0:T(8,128)(2,1)S(1)} custom-call(bf16[16,1536]{1,0:T(8,128)(2,1)} %x.1, bf16[16,1536]{1,0:T(8,128)(2,1)} %g.1), custom_call_target="tpu_custom_call" | custom-call | bytes 196608 | tf_op jit(solution)/shard_map/first_pair/pallas_call | solution.py:338
  1.5 3.1 %collective-permute-start = (bf16[32,1536]{1,0:T(8,128)(2,1)S(1)}, bf16[32,1536]{1,0:T(8,128)(2,1)S(1)}, u32[]{:S(2)}, u32[]{:S(2)}) collective-permute-start(bf16[32,1536]{1,0:T(8,128)(2,1)S(1)} %first_pair.1.refs_0_), channel_id=1, source_target_pairs={{0,1},{1,2},{2,3},{3,0},{4,5},{5,6},{6,7},{7,4},{8,9},{9,10},{10,1... | collective-permute-start | bytes 294920 | tf_op jit(solution)/shard_map/ppermute | solution.py:478
  4.6 2.6 %collective-permute-start.1 = (bf16[32,1536]{1,0:T(8,128)(2,1)S(1)}, bf16[32,1536]{1,0:T(8,128)(2,1)S(1)}, u32[]{:S(2)}, u32[]{:S(2)}) collective-permute-start(bf16[32,1536]{1,0:T(8,128)(2,1)S(1)} %first_pair.1.refs_0_), channel_id=1, source_target_pairs={{0,2},{1,3},{2,0},{3,1},{4,6},{5,7},{6,4},{7,5},{8,10},{9,11},{10,... | collective-permute-start | bytes 294920 | tf_op jit(solution)/shard_map/ppermute | solution.py:478
  7.1 1.3 %collective-permute-start.2 = (bf16[32,1536]{1,0:T(8,128)(2,1)S(1)}, bf16[32,1536]{1,0:T(8,128)(2,1)S(1)}, u32[]{:S(2)}, u32[]{:S(2)}) collective-permute-start(bf16[32,1536]{1,0:T(8,128)(2,1)S(1)} %first_pair.1.refs_0_), channel_id=1, source_target_pairs={{0,3},{1,0},{2,1},{3,2},{4,7},{5,4},{6,5},{7,6},{8,11},{9,8},{10,9... | collective-permute-start | bytes 294920 | tf_op jit(solution)/shard_map/ppermute | solution.py:478
  9.2 3.9 %turned.5 = (bf16[1536,1024]{1,0:T(8,128)(2,1)S(1)}, bf16[1536,1024]{1,0:T(8,128)(2,1)S(1)}) custom-call(s32[2]{0:T(128)S(1)} %pad_add_fusion.place, bf16[1,1024,6144]{2,1,0:T(8,128)(2,1)} %w.9), custom_call_target="tpu_custom_call" | custom-call | tf_op jit(solution)/shard_map/turned/pallas_call | solution.py:104
  13.8 1.6 %collective-permute-start.6 = (bf16[16,6272]{1,0:T(8,128)(2,1)S(1)}, bf16[16,6272]{1,0:T(8,128)(2,1)S(1)}, u32[]{:S(2)}, u32[]{:S(2)}) collective-permute-start(bf16[16,6272]{1,0:T(8,128)(2,1)S(1)} %get-tuple-element.39.refs_0_), channel_id=1, source_target_pairs={{0,16},{4,20},{8,24},{12,28},{16,0},{20,4},{24,8},{28,12},{1,17},{... | collective-permute-start | bytes 602120 | tf_op jit(solution)/shard_map/ppermute | solution.py:486
  15.4 1.5 %collective-permute-start.7 = (bf16[16,6272]{1,0:T(8,128)(2,1)S(1)}, bf16[16,6272]{1,0:T(8,128)(2,1)S(1)}, u32[]{:S(2)}, u32[]{:S(2)}) collective-permute-start(bf16[16,6272]{1,0:T(8,128)(2,1)S(1)} %get-tuple-element.39.refs_0_), channel_id=1, source_target_pairs={{0,4},{4,0},{8,12},{12,8},{16,20},{20,16},{24,28},{28,24},{1,5},{5... | collective-permute-start | bytes 602120 | tf_op jit(solution)/shard_map/ppermute | solution.py:486
  17.4 5.9 %turned.6 = (bf16[1024,1536]{1,0:T(8,128)(2,1)S(1)}, bf16[1024,1536]{1,0:T(8,128)(2,1)S(1)}, bf16[1024,1536]{1,0:T(8,128)(2,1)S(1)}, bf16[1024,1536]{1,0:T(8,128)(2,1)S(1)}) custom-call(s32[2]{0:T(128)S(1)} %pad_add_fusion.place, bf16[1,6144,1024]{2,1,0:T(8,128)(2,1)} %w.6), custom_call_target="tpu_custom_call" | custom-call | tf_op jit(solution)/shard_map/turned/pallas_call | solution.py:104
  23.3 3.9 %turned.7 = (bf16[1024,1536]{1,0:T(8,128)(2,1)S(1)}, bf16[1024,1536]{1,0:T(8,128)(2,1)S(1)}) custom-call(s32[2]{0:T(128)S(1)} %pad_add_fusion.place, bf16[1,6144,1024]{2,1,0:T(8,128)(2,1)} %w.8), custom_call_target="tpu_custom_call" | custom-call | tf_op jit(solution)/shard_map/turned/pallas_call | solution.py:104
  27.4 1.6 %collective-permute-start.3 = (bf16[16,6144]{1,0:T(8,128)(2,1)S(1)}, bf16[16,6144]{1,0:T(8,128)(2,1)S(1)}, u32[]{:S(2)}, u32[]{:S(2)}) collective-permute-start(bf16[16,6144]{1,0:T(8,128)(2,1)S(1)} %get-tuple-element.38.refs_0_), channel_id=1, source_target_pairs={{0,16},{4,20},{8,24},{12,28},{16,0},{20,4},{24,8},{28,12},{1,17},{... | collective-permute-start | bytes 589832 | tf_op jit(solution)/shard_map/ppermute | solution.py:486
  28.9 1.5 %collective-permute-start.4 = (bf16[16,6144]{1,0:T(8,128)(2,1)S(1)}, bf16[16,6144]{1,0:T(8,128)(2,1)S(1)}, u32[]{:S(2)}, u32[]{:S(2)}) collective-permute-start(bf16[16,6144]{1,0:T(8,128)(2,1)S(1)} %get-tuple-element.38.refs_0_), channel_id=1, source_target_pairs={{0,4},{4,0},{8,12},{12,8},{16,20},{20,16},{24,28},{28,24},{1,5},{5... | collective-permute-start | bytes 589832 | tf_op jit(solution)/shard_map/ppermute | solution.py:486
  30.9 3.9 %turned.8 = (bf16[1024,1536]{1,0:T(8,128)(2,1)S(1)}, bf16[1024,1536]{1,0:T(8,128)(2,1)S(1)}) custom-call(s32[2]{0:T(128)S(1)} %pad_add_fusion.place, bf16[1,6144,1024]{2,1,0:T(8,128)(2,1)} %w.8, bf16[64,6272]{1,0:T(8,128)(2,1)S(1)} %stacked.2.refs_0_.xp), custom_call_target="tpu_custom_call" | custom-call | tf_op jit(solution)/shard_map/turned/pallas_call | solution.py:104
  34.8 7.4 %gate_up.1 = (f32[128,1024]{1,0:T(8,128)S(1)}, f32[128,1024]{1,0:T(8,128)S(1)}, f32[128,128]{1,0:T(8,128)S(1)}) custom-call(s32[2]{0:T(128)S(1)} %pad_add_fusion.place, bf16[64,6272]{1,0:T(8,128)(2,1)S(1)} %stacked.2.refs_0_.xp, bf16[64,6272]{1,0:T(8,128)(2,1)S(1)} %collective-permute-done.9.xo, bf16[1024,1536]{1,0:T(8,128)(2,1)S(1)} %get-tuple-element.40.refs_4_.refs_0_, ...), custom_call_target="tpu_custom_call" | custom-call | tf_op jit(solution)/shard_map/gate_up/pallas_call | solution.py:145
  42.4 3.9 %turned.9 = (bf16[1536,1024]{1,0:T(8,128)(2,1)S(1)}, bf16[1536,1024]{1,0:T(8,128)(2,1)S(1)}) custom-call(s32[2]{0:T(128)S(1)} %pad_add_fusion.place, bf16[1,1024,6144]{2,1,0:T(8,128)(2,1)} %w.9, bf16[64,6144]{1,0:T(8,128)(2,1)S(1)} %stacked.3.refs_0_.gp), custom_call_target="tpu_custom_call" | custom-call | tf_op jit(solution)/shard_map/turned/pallas_call | solution.py:104
  46.3 6.1 %middle.1 = (bf16[64,6272]{1,0:T(8,128)(2,1)S(1)}, bf16[64,6272]{1,0:T(8,128)(2,1)S(1)}, bf16[128,1024]{1,0:T(8,128)(2,1)S(1)}, bf16[128,1024]{1,0:T(8,128)(2,1)S(1)}, bf16[128,1024]{1,0:T(8,128)(2,1)S(1)}) custom-call(s32[2]{0:T(128)S(1)} %pad_add_fusion.place, bf16[64,6144]{1,0:T(8,128)(2,1)S(1)} %stacked.3.refs_0_.gp, ...), custom_call_target="tpu_custom_call" | custom-call | tf_op jit(solution)/shard_map/middle/pallas_call | solution.py:208
  52.9 5.8 %columns_grad.3 = bf16[1,6144,1024]{2,1,0:T(8,128)(2,1)} custom-call(s32[2]{0:T(128)S(1)} %pad_add_fusion.place, bf16[64,6272]{1,0:T(8,128)(2,1)S(1)} %stacked.2.refs_0_.xp, bf16[64,6272]{1,0:T(8,128)(2,1)S(1)} %collective-permute-done.9.xo, bf16[128,1024]{1,0:T(8,128)(2,1)S(1)} %get-tuple-element.67.delta), custom_call_target="tpu_custom_call" | custom-call | flops 1610612736 | bytes 12582912 | tf_op jit(solution)/shard_map/columns_grad/pallas_call | solution.py:242
  59.1 1.6 %collective-permute-start.12 = (bf16[16,6272]{1,0:T(8,128)(2,1)S(1)}, bf16[16,6272]{1,0:T(8,128)(2,1)S(1)}, u32[]{:S(2)}, u32[]{:S(2)}) collective-permute-start(bf16[16,6272]{1,0:T(8,128)(2,1)S(1)} %get-tuple-element.57), channel_id=1, source_target_pairs={{0,16},{4,20},{8,24},{12,28},{16,0},{20,4},{24,8},{28,12},{1,17},{... | collective-permute-start | bytes 602120 | tf_op jit(solution)/shard_map/ppermute | solution.py:486
  60.7 1.5 %collective-permute-start.13 = (bf16[16,6272]{1,0:T(8,128)(2,1)S(1)}, bf16[16,6272]{1,0:T(8,128)(2,1)S(1)}, u32[]{:S(2)}, u32[]{:S(2)}) collective-permute-start(bf16[16,6272]{1,0:T(8,128)(2,1)S(1)} %get-tuple-element.58), channel_id=1, source_target_pairs={{0,4},{4,0},{8,12},{12,8},{16,20},{20,16},{24,28},{28,24},{1,5},{5... | collective-permute-start | bytes 602120 | tf_op jit(solution)/shard_map/ppermute | solution.py:486
  62.7 4.0 %down_grads.2.refs_0_ = bf16[1,1024,6144]{2,1,0:T(8,128)(2,1)} custom-call(s32[2]{0:T(128)S(1)} %pad_add_fusion.place, bf16[64,6144]{1,0:T(8,128)(2,1)S(1)} %stacked.3.refs_0_.gp, bf16[64,6144]{1,0:T(8,128)(2,1)S(1)} %collective-permute-done.10.go, bf16[128,1024]{1,0:T(8,128)(2,1)S(1)} %get-tuple-element.68.hidw), custom_call_target="tpu_custom_call" | custom-call | flops 805306368 | bytes 6291456 | tf_op jit(solution)/shard_map/down_grads/pallas_call | solution.py:279
  66.7 5.8 %columns_grad.2 = bf16[1,6144,1024]{2,1,0:T(8,128)(2,1)} custom-call(s32[2]{0:T(128)S(1)} %pad_add_fusion.place, bf16[64,6272]{1,0:T(8,128)(2,1)S(1)} %stacked.2.refs_0_.xp, bf16[64,6272]{1,0:T(8,128)(2,1)S(1)} %collective-permute-done.9.xo, bf16[128,1024]{1,0:T(8,128)(2,1)S(1)} %get-tuple-element.66.delta), custom_call_target="tpu_custom_call" | custom-call | flops 1610612736 | bytes 12582912 | tf_op jit(solution)/shard_map/columns_grad/pallas_call | solution.py:242
  72.7 3.6 %collective-permute-start.15 = (bf16[16,1664]{1,0:T(8,128)(2,1)S(1)}, bf16[16,1664]{1,0:T(8,128)(2,1)S(1)}, u32[]{:S(2)}, u32[]{:S(2)}) collective-permute-start(bf16[16,1664]{1,0:T(8,128)(2,1)S(1)} %get-tuple-element.61), channel_id=1, source_target_pairs={{0,3},{1,0},{2,1},{3,2},{4,7},{5,4},{6,5},{7,6},{8,11},{9,8},{10,9... | collective-permute-start | bytes 159752 | tf_op jit(solution)/shard_map/ppermute | solution.py:478
  77.0 4.0 %down_grads.3 = bf16[1,1024,6144]{2,1,0:T(8,128)(2,1)} custom-call(s32[2]{0:T(128)S(1)} %pad_add_fusion.place, bf16[64,6144]{1,0:T(8,128)(2,1)S(1)} %stacked.3.refs_0_.gp, bf16[64,6144]{1,0:T(8,128)(2,1)S(1)} %collective-permute-done.10.go, bf16[128,1024]{1,0:T(8,128)(2,1)S(1)} %get-tuple-element.68.hidw, ...), custom_call_target="tpu_custom_call", output_to_operand_aliasing={{}: (4, {})} | custom-call | flops 805306368 | bytes 6291456 | tf_op jit(solution)/shard_map/down_grads/pallas_call | solution.py:279
  81.4 1.3 %collective-permute-done.17.refs_3_ = bf16[16,1664]{1,0:T(8,128)(2,1)S(1)} collective-permute-done((bf16[16,1664]{1,0:T(8,128)(2,1)S(1)}, bf16[16,1664]{1,0:T(8,128)(2,1)S(1)}, u32[]{:S(2)}, u32[]{:S(2)}) %collective-permute-start.17) | collective-permute-done | bytes 53280 | tf_op jit(solution)/shard_map/ppermute | solution.py:478
  83.4 0.7 select_reduce_fusion
  (36 shorter events, 5.9 us)
Async XLA Ops:
  1.5 11.7 %collective-permute-start = (bf16[32,1536]{1,0:T(8,128)(2,1)S(1)}, bf16[32,1536]{1,0:T(8,128)(2,1)S(1)}, u32[]{:S(2)}, u32[]{:S(2)}) collective-permute-start(bf16[32,1536]{1,0:T(8,128)(2,1)S(1)} %first_pair.1.refs_0_), channel_id=1, source_target_pairs={{0,1},{1,2},{2,3},{3,0},{4,5},{5,6},{6,7},{7,4},{8,9},{9,10},{10,1... | collective-permute-start | bytes 294920 | tf_op jit(solution)/shard_map/ppermute | solution.py:478
  4.6 9.2 %collective-permute-start.1 = (bf16[32,1536]{1,0:T(8,128)(2,1)S(1)}, bf16[32,1536]{1,0:T(8,128)(2,1)S(1)}, u32[]{:S(2)}, u32[]{:S(2)}) collective-permute-start(bf16[32,1536]{1,0:T(8,128)(2,1)S(1)} %first_pair.1.refs_0_), channel_id=1, source_target_pairs={{0,2},{1,3},{2,0},{3,1},{4,6},{5,7},{6,4},{7,5},{8,10},{9,11},{10,... | collective-permute-start | bytes 294920 | tf_op jit(solution)/shard_map/ppermute | solution.py:478
  7.1 6.6 %collective-permute-start.2 = (bf16[32,1536]{1,0:T(8,128)(2,1)S(1)}, bf16[32,1536]{1,0:T(8,128)(2,1)S(1)}, u32[]{:S(2)}, u32[]{:S(2)}) collective-permute-start(bf16[32,1536]{1,0:T(8,128)(2,1)S(1)} %first_pair.1.refs_0_), channel_id=1, source_target_pairs={{0,3},{1,0},{2,1},{3,2},{4,7},{5,4},{6,5},{7,6},{8,11},{9,8},{10,9... | collective-permute-start | bytes 294920 | tf_op jit(solution)/shard_map/ppermute | solution.py:478
  9.2 3.9 %copy-start = (s32[16,2]{0,1:T(2,128)S(1)}, s32[16,2]{0,1:T(2,128)}, u32[]{:S(2)}) copy-start(s32[16,2]{0,1:T(2,128)} %param.9) | copy-start | bytes 388
  13.8 13.4 %collective-permute-start.6 = (bf16[16,6272]{1,0:T(8,128)(2,1)S(1)}, bf16[16,6272]{1,0:T(8,128)(2,1)S(1)}, u32[]{:S(2)}, u32[]{:S(2)}) collective-permute-start(bf16[16,6272]{1,0:T(8,128)(2,1)S(1)} %get-tuple-element.39.refs_0_), channel_id=1, source_target_pairs={{0,16},{4,20},{8,24},{12,28},{16,0},{20,4},{24,8},{28,12},{1,17},{... | collective-permute-start | bytes 602120 | tf_op jit(solution)/shard_map/ppermute | solution.py:486
  15.4 11.9 %collective-permute-start.7 = (bf16[16,6272]{1,0:T(8,128)(2,1)S(1)}, bf16[16,6272]{1,0:T(8,128)(2,1)S(1)}, u32[]{:S(2)}, u32[]{:S(2)}) collective-permute-start(bf16[16,6272]{1,0:T(8,128)(2,1)S(1)} %get-tuple-element.39.refs_0_), channel_id=1, source_target_pairs={{0,4},{4,0},{8,12},{12,8},{16,20},{20,16},{24,28},{28,24},{1,5},{5... | collective-permute-start | bytes 602120 | tf_op jit(solution)/shard_map/ppermute | solution.py:486
  16.9 10.3 %collective-permute-start.8 = (bf16[16,6272]{1,0:T(8,128)(2,1)S(1)}, bf16[16,6272]{1,0:T(8,128)(2,1)S(1)}, u32[]{:S(2)}, u32[]{:S(2)}) collective-permute-start(bf16[16,6272]{1,0:T(8,128)(2,1)S(1)} %get-tuple-element.39.refs_0_), channel_id=1, source_target_pairs={{0,20},{4,16},{8,28},{12,24},{16,4},{20,0},{24,12},{28,8},{1,21},{... | collective-permute-start | bytes 602120 | tf_op jit(solution)/shard_map/ppermute | solution.py:486
  27.3 7.5 %collective-permute-start.9 = (bf16[64,6272]{1,0:T(8,128)(2,1)S(1)}, bf16[64,6272]{1,0:T(8,128)(2,1)S(1)}, u32[]{:S(2)}, u32[]{:S(2)}) collective-permute-start(bf16[64,6272]{1,0:T(8,128)(2,1)S(1)} %stacked.2.refs_0_.xp), channel_id=1, source_target_pairs={{0,8},{8,0},{16,24},{24,16},{1,9},{9,1},{17,25},{25,17},{2,10},{10... | collective-permute-start | bytes 2408456 | tf_op jit(solution)/shard_map/ppermute | solution.py:489
  27.4 14.8 %collective-permute-start.3 = (bf16[16,6144]{1,0:T(8,128)(2,1)S(1)}, bf16[16,6144]{1,0:T(8,128)(2,1)S(1)}, u32[]{:S(2)}, u32[]{:S(2)}) collective-permute-start(bf16[16,6144]{1,0:T(8,128)(2,1)S(1)} %get-tuple-element.38.refs_0_), channel_id=1, source_target_pairs={{0,16},{4,20},{8,24},{12,28},{16,0},{20,4},{24,8},{28,12},{1,17},{... | collective-permute-start | bytes 589832 | tf_op jit(solution)/shard_map/ppermute | solution.py:486
  28.9 13.3 %collective-permute-start.4 = (bf16[16,6144]{1,0:T(8,128)(2,1)S(1)}, bf16[16,6144]{1,0:T(8,128)(2,1)S(1)}, u32[]{:S(2)}, u32[]{:S(2)}) collective-permute-start(bf16[16,6144]{1,0:T(8,128)(2,1)S(1)} %get-tuple-element.38.refs_0_), channel_id=1, source_target_pairs={{0,4},{4,0},{8,12},{12,8},{16,20},{20,16},{24,28},{28,24},{1,5},{5... | collective-permute-start | bytes 589832 | tf_op jit(solution)/shard_map/ppermute | solution.py:486
  30.4 11.8 %collective-permute-start.5 = (bf16[16,6144]{1,0:T(8,128)(2,1)S(1)}, bf16[16,6144]{1,0:T(8,128)(2,1)S(1)}, u32[]{:S(2)}, u32[]{:S(2)}) collective-permute-start(bf16[16,6144]{1,0:T(8,128)(2,1)S(1)} %get-tuple-element.38.refs_0_), channel_id=1, source_target_pairs={{0,20},{4,16},{8,28},{12,24},{16,4},{20,0},{24,12},{28,8},{1,21},{... | collective-permute-start | bytes 589832 | tf_op jit(solution)/shard_map/ppermute | solution.py:486
  42.3 4.0 %collective-permute-start.10 = (bf16[64,6144]{1,0:T(8,128)(2,1)S(1)}, bf16[64,6144]{1,0:T(8,128)(2,1)S(1)}, u32[]{:S(2)}, u32[]{:S(2)}) collective-permute-start(bf16[64,6144]{1,0:T(8,128)(2,1)S(1)} %stacked.3.refs_0_.gp), channel_id=1, source_target_pairs={{0,8},{8,0},{16,24},{24,16},{1,9},{9,1},{17,25},{25,17},{2,10},{10... | collective-permute-start | bytes 2359304 | tf_op jit(solution)/shard_map/ppermute | solution.py:489
  52.4 6.4 %collective-permute-start.11 = (bf16[64,6272]{1,0:T(8,128)(2,1)S(1)}, bf16[64,6272]{1,0:T(8,128)(2,1)S(1)}, u32[]{:S(2)}, u32[]{:S(2)}) collective-permute-start(bf16[64,6272]{1,0:T(8,128)(2,1)S(1)} %get-tuple-element.55), channel_id=1, source_target_pairs={{0,8},{8,0},{16,24},{24,16},{1,9},{9,1},{17,25},{25,17},{2,10},{10... | collective-permute-start | bytes 2408456 | tf_op jit(solution)/shard_map/ppermute | solution.py:489
  59.1 13.4 %collective-permute-start.12 = (bf16[16,6272]{1,0:T(8,128)(2,1)S(1)}, bf16[16,6272]{1,0:T(8,128)(2,1)S(1)}, u32[]{:S(2)}, u32[]{:S(2)}) collective-permute-start(bf16[16,6272]{1,0:T(8,128)(2,1)S(1)} %get-tuple-element.57), channel_id=1, source_target_pairs={{0,16},{4,20},{8,24},{12,28},{16,0},{20,4},{24,8},{28,12},{1,17},{... | collective-permute-start | bytes 602120 | tf_op jit(solution)/shard_map/ppermute | solution.py:486
  60.7 11.8 %collective-permute-start.13 = (bf16[16,6272]{1,0:T(8,128)(2,1)S(1)}, bf16[16,6272]{1,0:T(8,128)(2,1)S(1)}, u32[]{:S(2)}, u32[]{:S(2)}) collective-permute-start(bf16[16,6272]{1,0:T(8,128)(2,1)S(1)} %get-tuple-element.58), channel_id=1, source_target_pairs={{0,4},{4,0},{8,12},{12,8},{16,20},{20,16},{24,28},{28,24},{1,5},{5... | collective-permute-start | bytes 602120 | tf_op jit(solution)/shard_map/ppermute | solution.py:486
  62.2 10.3 %collective-permute-start.14 = (bf16[16,6272]{1,0:T(8,128)(2,1)S(1)}, bf16[16,6272]{1,0:T(8,128)(2,1)S(1)}, u32[]{:S(2)}, u32[]{:S(2)}) collective-permute-start(bf16[16,6272]{1,0:T(8,128)(2,1)S(1)} %get-tuple-element.59), channel_id=1, source_target_pairs={{0,20},{4,16},{8,28},{12,24},{16,4},{20,0},{24,12},{28,8},{1,21},{... | collective-permute-start | bytes 602120 | tf_op jit(solution)/shard_map/ppermute | solution.py:486
  72.7 8.3 %collective-permute-start.15 = (bf16[16,1664]{1,0:T(8,128)(2,1)S(1)}, bf16[16,1664]{1,0:T(8,128)(2,1)S(1)}, u32[]{:S(2)}, u32[]{:S(2)}) collective-permute-start(bf16[16,1664]{1,0:T(8,128)(2,1)S(1)} %get-tuple-element.61), channel_id=1, source_target_pairs={{0,3},{1,0},{2,1},{3,2},{4,7},{5,4},{6,5},{7,6},{8,11},{9,8},{10,9... | collective-permute-start | bytes 159752 | tf_op jit(solution)/shard_map/ppermute | solution.py:478
  76.4 5.0 %collective-permute-start.16 = (bf16[16,1664]{1,0:T(8,128)(2,1)S(1)}, bf16[16,1664]{1,0:T(8,128)(2,1)S(1)}, u32[]{:S(2)}, u32[]{:S(2)}) collective-permute-start(bf16[16,1664]{1,0:T(8,128)(2,1)S(1)} %get-tuple-element.62), channel_id=1, source_target_pairs={{0,2},{1,3},{2,0},{3,1},{4,6},{5,7},{6,4},{7,5},{8,10},{9,11},{10,... | collective-permute-start | bytes 159752 | tf_op jit(solution)/shard_map/ppermute | solution.py:478
  76.8 5.9 %collective-permute-start.17 = (bf16[16,1664]{1,0:T(8,128)(2,1)S(1)}, bf16[16,1664]{1,0:T(8,128)(2,1)S(1)}, u32[]{:S(2)}, u32[]{:S(2)}) collective-permute-start(bf16[16,1664]{1,0:T(8,128)(2,1)S(1)} %get-tuple-element.63), channel_id=1, source_target_pairs={{0,1},{1,2},{2,3},{3,0},{4,5},{5,6},{6,7},{7,4},{8,9},{9,10},{10,1... | collective-permute-start | bytes 159752 | tf_op jit(solution)/shard_map/ppermute | solution.py:478

commit v3 on v2

--- a/solution.py
+++ b/solution.py
@@ -8,6 +8,9 @@
 from jax.sharding import PartitionSpec as P
 
 EXTRA = 128
+SLOTS = 6
+TURN_CHUNK = 384
+GRAD_CHUNK = 256
 MIB = 1 << 20
 PLAIN = (((1,), (0,)), ((), ()))
 CONTRACT_ROWS = (((0,), (0,)), ((), ()))
@@ -44,16 +47,16 @@
     )
 
 
-def chunk_of(features):
+def chunk_of(features, most=768):
     for size in (768, 512, 384, 256, 128):
-        if features % size == 0:
+        if features % size == 0 and size <= most:
             return size
     return features
 
 
-def whole_chunks(home, pieces, depth):
+def whole_chunks(home, pieces, depth, most=768):
     width = depth // pieces
-    size = chunk_of(width)
+    size = chunk_of(width, most)
     found = []
     for k in range(pieces):
         owner = lax.rem(home - k + pieces, pieces)
@@ -67,91 +70,145 @@
     return jnp.concatenate([near[:, start : start + size], far[:, start : start + size]], axis=0)
 
 
-def turned_kernel(place, w, *refs, pieces, by_rows, first, count):
-    *outs, buf, sems = refs[-count - 2 :]
-    depth = w.shape[1] if by_rows else w.shape[2]
+def jobs_chunks(place, pieces, jobs, depth):
     width = depth // pieces
-    size, chunks = whole_chunks(place[0], pieces, depth)
-    chunks = [c for c in chunks if first <= c[0] // width < first + count]
+    size, chunks = whole_chunks(place[0], pieces, depth, TURN_CHUNK)
+    found, base = [], 0
+    for weight, by_rows, which in jobs:
+        for rel, start in chunks:
+            if rel // width in which:
+                found.append((weight, by_rows, base + rel // width - which.start, rel % width, start))
+        base += len(which)
+    return size, found
+
+
+def turn_into(out, base, value, by_rows):
+    rows, columns = value.shape
+    for at in range(0, columns, EXTRA):
+        turned_part = value[:, at : at + EXTRA].T
+        if by_rows:
+            out[at : at + EXTRA, base : base + rows] = turned_part
+        else:
+            out[base + at : base + at + EXTRA, :] = turned_part
+
+
+def turned_kernel(place, *refs, pieces, jobs, depth):
+    weights = refs[: len(jobs)]
+    count = sum(len(which) for _, _, which in jobs)
+    *outs, flat, tall, sems = refs[-count - 3 :]
+    jobs = [(w, by_rows, which) for w, (_, by_rows, which) in zip(weights, jobs, strict=True)]
+    size, chunks = jobs_chunks(place, pieces, jobs, depth)
+
+    def buffer(j):
+        return (flat if chunks[j][1] else tall).at[j % SLOTS]
+
+    def copy(j):
+        weight, by_rows, _, _, start = chunks[j]
+        span = pl.ds(start, size)
+        source = weight.at[0, span] if by_rows else weight.at[0, :, span]
+        return pltpu.make_async_copy(source, buffer(j), sems.at[j % SLOTS])
+
+    for j in range(min(SLOTS, len(chunks))):
+        copy(j).start()
+    for j, (_, by_rows, out, base, _) in enumerate(chunks):
+        copy(j).wait()
+        turn_into(outs[out], base, buffer(j), by_rows)
+        if j + SLOTS < len(chunks):
+            copy(j + SLOTS).start()
+
+
+def turned(place, pieces, jobs, depth, after=()):
+    width = depth // pieces
+    size = chunk_of(width, TURN_CHUNK)
+    hidden = jobs[0][0].shape[2] if jobs[0][1] else jobs[0][0].shape[1]
+    shapes = []
+    for _, by_rows, which in jobs:
+        shapes += [shaped((hidden, width) if by_rows else (width, hidden))] * len(which)
+    kinds = {by_rows for _, by_rows, _ in jobs}
+    weights = [pltpu.with_memory_space_constraint(w, pltpu.HBM) for w, _, _ in jobs]
+    shared = functools.partial(
+        turned_kernel, pieces=pieces, jobs=[(None, b, which) for _, b, which in jobs], depth=depth
+    )
+    found = local_call(
+        shared,
+        "turned",
+        7 * len(kinds),
+        0,
+        0,
+        [SMEM] + [HBM] * len(weights) + [ANY] * len(after),
+        [VMEM] * len(shapes),
+        shapes,
+        [
+            pltpu.VMEM((SLOTS if True in kinds else 1, size, hidden), jnp.bfloat16),
+            pltpu.VMEM((SLOTS if False in kinds else 1, hidden, size), jnp.bfloat16),
+            pltpu.SemaphoreType.DMA((SLOTS,)),
+        ],
+    )(place, *weights, *after)
+    result, at = [], 0
+    for _, _, which in jobs:
+        result.append(found[at : at + len(which)])
+        at += len(which)
+    return result
+
+
+def gate_up_kernel(place, xp, xo, wu, *refs, pieces):
+    wg, refs = refs[:pieces], refs[pieces:]
+    gate, up, weight, *outs, buf, sems = refs
+    hidden, width = wg[0].shape
+    size, chunks = whole_chunks(place[0], pieces, width * pieces, TURN_CHUNK)
     slots = buf.shape[0]
 
     def copy(j):
         span = pl.ds(chunks[j][1], size)
-        source = w.at[0, span] if by_rows else w.at[0, :, span]
-        return pltpu.make_async_copy(source, buf.at[j % slots], sems.at[j % slots])
+        return pltpu.make_async_copy(wu.at[0, span], buf.at[j % slots], sems.at[j % slots])
 
     for j in range(min(slots, len(chunks))):
         copy(j).start()
-    for j, (rel, _) in enumerate(chunks):
-        copy(j).wait()
-        out, base = outs[rel // width - first], rel % width
-        for at in range(0, buf.shape[2], EXTRA):
-            value = buf[j % slots, :, at : at + EXTRA].T
-            if by_rows:
-                out[at : at + EXTRA, base : base + size] = value
+    for k, w in enumerate(wg):
+        rows = both_rows(xp, xo, k * width, width)
+        for at in range(0, hidden, EXTRA):
+            value = matmul(rows, w[at : at + EXTRA, :], CONTRACT_COLS)
+            if k == 0:
+                gate[:, at : at + EXTRA] = value
             else:
-                out[base + at : base + at + EXTRA, :] = value
-        if j + slots < len(chunks):
-            copy(j + slots).start()
-
-
-def turned(place, pieces, weights, by_rows, which, after=()):
-    _, up_to, across = weights.shape
-    depth, hidden = (up_to, across) if by_rows else (across, up_to)
-    width = depth // pieces
-    size = chunk_of(width)
-    shape = (hidden, width) if by_rows else (width, hidden)
-    return local_call(
-        functools.partial(
-            turned_kernel, pieces=pieces, by_rows=by_rows, first=which.start, count=len(which)
-        ),
-        "turned",
-        8,
-        0,
-        0,
-        [SMEM, HBM] + [ANY] * len(after),
-        [VMEM] * len(which),
-        [shaped(shape)] * len(which),
-        [
-            pltpu.VMEM((4, size, hidden) if by_rows else (4, hidden, size), jnp.bfloat16),
-            pltpu.SemaphoreType.DMA((4,)),
-        ],
-    )(place, pltpu.with_memory_space_constraint(weights, pltpu.HBM), *after)
-
-
-def gate_up_kernel(place, xp, xo, *refs, pieces):
-    weights, (gate, up, weight) = refs[: 2 * pieces], refs[2 * pieces :]
-    hidden, width = weights[0].shape
-    for half, out in ((weights[:pieces], gate), (weights[pieces:], up)):
-        for k, w in enumerate(half):
-            rows = both_rows(xp, xo, k * width, width)
-            for at in range(0, hidden, EXTRA):
-                value = matmul(rows, w[at : at + EXTRA, :], CONTRACT_COLS)
-                if k == 0:
-                    out[:, at : at + EXTRA] = value
-                else:
-                    out[:, at : at + EXTRA] += value
+                gate[:, at : at + EXTRA] += value
     lane = lax.broadcasted_iota(jnp.int32, (1, EXTRA), 1)
     mine = both_rows(xp, xo, width * pieces, EXTRA).astype(jnp.float32)
     total = jnp.sum(jnp.where(lane == place[1], mine, 0.0), axis=1, keepdims=True)
     weight[...] = jnp.broadcast_to(total, weight.shape)
-
-
-def gate_up(place, near, far, turned_gate, turned_up):
+    for j, (rel, _) in enumerate(chunks):
+        copy(j).wait()
+        piece = buf.at[j % slots]
+        value = matmul(both_rows(xp, xo, rel, size), piece[...])
+        if j == 0:
+            up[...] = value
+        else:
+            up[...] += value
+        turn_into(outs[rel // width], rel % width, piece, True)
+        if j + slots < len(chunks):
+            copy(j + slots).start()
+
+
+def gate_up(place, near, far, turned_gate, w_up):
     half = near.shape[0]
     pieces = len(turned_gate)
-    hidden = turned_gate[0].shape[0]
+    hidden, width = turned_gate[0].shape
     out = shaped((2 * half, hidden), jnp.float32)
-    return local_call(
+    gate, up, weight, *turned_up = local_call(
         functools.partial(gate_up_kernel, pieces=pieces),
         "gate_up",
-        3,
-        0,
-        0,
-        [SMEM] + [VMEM] * (2 + 2 * pieces),
-        [VMEM] * 3,
-        [out, out, shaped((2 * half, EXTRA), jnp.float32)],
-    )(place, near, far, *turned_gate, *turned_up)
+        10,
+        0,
+        0,
+        [SMEM] + [VMEM] * 2 + [HBM] + [VMEM] * pieces,
+        [VMEM] * (3 + pieces),
+        [out, out, shaped((2 * half, EXTRA), jnp.float32)] + [shaped((hidden, width))] * pieces,
+        [
+            pltpu.VMEM((8, chunk_of(width, TURN_CHUNK), hidden), jnp.bfloat16),
+            pltpu.SemaphoreType.DMA((8,)),
+        ],
+    )(place, near, far, pltpu.with_memory_space_constraint(w_up, pltpu.HBM), *turned_gate)
+    return gate, up, weight, turned_up
 
 
 def middle_kernel(
@@ -218,79 +275,53 @@
     )(place, near, far, weight, gate, up, *turned_down, *turned_gate, *turned_up)
 
 
-def columns_kernel(place, xp, xo, delta, out, buf, sems, *, pieces):
-    depth = out.shape[1]
-    size, chunks = whole_chunks(place[0], pieces, depth)
+def weight_kernel(place, near, far, *refs, pieces, jobs, by_rows):
+    deltas = refs[: len(jobs)]
+    *outs, buf, sems = refs[-len(jobs) - 2 :]
+    depth = outs[0].shape[1] if by_rows else outs[0].shape[2]
+    size, chunks = whole_chunks(place[0], pieces, depth, GRAD_CHUNK)
     copies = []
-    for j, (rel, start) in enumerate(chunks):
-        rows = both_rows(xp, xo, rel, size)
-        slot = j
-        buf[slot] = matmul(rows, delta[...], CONTRACT_ROWS).astype(jnp.bfloat16)
-        copy = pltpu.make_async_copy(
-            buf.at[slot], out.at[0, pl.ds(start, size)], sems.at[slot]
-        )
-        copy.start()
-        copies.append(copy)
+    for delta, out, (first, last) in zip(deltas, outs, jobs, strict=True):
+        for rel, start in chunks[first:last]:
+            j = len(copies)
+            rows = both_rows(near, far, rel, size)
+            span = pl.ds(start, size)
+            if by_rows:
+                value, target = matmul(rows, delta[...], CONTRACT_ROWS), out.at[0, span]
+            else:
+                value, target = matmul(delta[...], rows, CONTRACT_ROWS), out.at[0, :, span]
+            buf[j] = value.astype(jnp.bfloat16)
+            copy = pltpu.make_async_copy(buf.at[j], target, sems.at[j])
+            copy.start()
+            copies.append(copy)
     for copy in copies:
         copy.wait()
 
 
-def columns_grad(place, pieces, near, far, delta, depth):
+def weight_grads(place, pieces, near, far, depth, by_rows, jobs):
     half = near.shape[0]
-    hidden = delta.shape[1]
-    count = depth // chunk_of(depth // pieces)
-    return local_call(
-        functools.partial(columns_kernel, pieces=pieces),
-        "columns_grad",
-        16,
-        4 * half * depth * hidden,
-        2 * depth * hidden,
-        [SMEM, VMEM, VMEM, VMEM],
-        ANY,
-        shaped((1, depth, hidden)),
+    hidden = jobs[0][0].shape[1]
+    size = chunk_of(depth // pieces, GRAD_CHUNK)
+    count = sum(last - first for _, first, last, _ in jobs)
+    there = [(i, job[3]) for i, job in enumerate(jobs) if job[3] is not None]
+    held = [pltpu.with_memory_space_constraint(g, pltpu.HBM) for _, g in there]
+    return local_call(
+        functools.partial(
+            weight_kernel, pieces=pieces, jobs=[job[1:3] for job in jobs], by_rows=by_rows
+        ),
+        "weight_grads",
+        4 + (count * size * hidden * 2) // MIB,
+        4 * half * size * count * hidden,
+        2 * size * count * hidden,
+        [SMEM] + [VMEM] * (2 + len(jobs)) + [HBM] * len(held),
+        [ANY] * len(jobs),
+        [shaped((1, depth, hidden) if by_rows else (1, hidden, depth))] * len(jobs),
         [
-            pltpu.VMEM((count, chunk_of(depth // pieces), hidden), jnp.bfloat16),
+            pltpu.VMEM((count, size, hidden) if by_rows else (count, hidden, size), jnp.bfloat16),
             pltpu.SemaphoreType.DMA((count,)),
         ],
-    )(place, near, far, delta)
-
-
-def down_kernel(place, gp, go, hidw, *refs, pieces, first, last):
-    out, buf, sems = refs[-3:]
-    depth = out.shape[2]
-    size, chunks = whole_chunks(place[0], pieces, depth)
-    copies = []
-    for j, (rel, start) in enumerate(chunks[first:last]):
-        rows = both_rows(gp, go, rel, size)
-        buf[j] = matmul(hidw[...], rows, CONTRACT_ROWS).astype(jnp.bfloat16)
-        copy = pltpu.make_async_copy(buf.at[j], out.at[0, :, pl.ds(start, size)], sems.at[j])
-        copy.start()
-        copies.append(copy)
-    for copy in copies:
-        copy.wait()
-
-
-def down_grads(place, pieces, near, far, hidw, depth, first, last, partial=()):
-    half = near.shape[0]
-    hidden = hidw.shape[1]
-    count = last - first
-    size = chunk_of(depth // pieces)
-    partial = [pltpu.with_memory_space_constraint(p, pltpu.HBM) for p in partial]
-    return local_call(
-        functools.partial(down_kernel, pieces=pieces, first=first, last=last),
-        "down_grads",
-        16,
-        4 * half * size * count * hidden,
-        2 * size * count * hidden,
-        [SMEM, VMEM, VMEM, VMEM] + [HBM] * len(partial),
-        ANY,
-        shaped((1, hidden, depth)),
-        [
-            pltpu.VMEM((count, hidden, size), jnp.bfloat16),
-            pltpu.SemaphoreType.DMA((count,)),
-        ],
-        aliases={4: 0} if partial else None,
-    )(place, near, far, hidw, *partial)
+        aliases={3 + len(jobs) + n: i for n, (i, _) in enumerate(there)},
+    )(place, near, far, *[job[0] for job in jobs], *held)
 
 
 def stack_kernel(*refs, axis, count):
@@ -493,31 +524,35 @@
     weights = jnp.sum(chosen * route_weight.astype(jnp.float32)[:, :, None], axis=1)
     both = first_pair(tokens_in, out_grad)
     arrived = [along(both, k) for k in range(1, pieces)]
+    everything = range(pieces)
     early, late = range(pieces // 2), range(pieces // 2, pieces)
-    turned_down = turned(place, pieces, down_weight, False, early)
+    (turned_down,) = turned(place, pieces, [(down_weight, False, early)], depth)
     line_x, line_g = line_pair([both] + arrived, weights.astype(jnp.bfloat16), turned_down[0])
     from_x = [across(line_x, dx, ds) for dx, ds in planes[1:]]
-    turned_gate = turned(place, pieces, gate_weight, True, range(pieces))
-    turned_up = turned(place, pieces, up_weight, True, early)
-    near_x = stacked([line_x] + from_x, 0, [turned_gate[0], turned_up[0]])
+    turned_gate, more_down = turned(
+        place, pieces, [(gate_weight, True, everything), (down_weight, False, late)], depth
+    )
+    near_x = stacked([line_x] + from_x, 0, [turned_gate[0]])
     far_x = swap(near_x)
     from_g = [across(line_g, dx, ds) for dx, ds in planes[1:]]
-    turned_up = turned_up + turned(place, pieces, up_weight, True, late, [near_x])
-    gate, up, weight = gate_up(place, near_x, far_x, turned_gate, turned_up)
+    gate, up, weight, turned_up = gate_up(place, near_x, far_x, turned_gate, up_weight)
     near_g = stacked([line_g] + from_g, 0, [weight])
     far_g = swap(near_g)
-    turned_down = turned_down + turned(place, pieces, down_weight, False, late, [near_g])
     near_d, far_d, dgate, dup, hidw = middle(
-        place, experts, pieces, near_g, far_g, weight, gate, up, turned_down, turned_gate, turned_up
+        place, experts, pieces, near_g, far_g, weight, gate, up,
+        turned_down + more_down, turned_gate, turned_up,
     )
 
     other_d = swap(far_d)
-    chunks = depth // chunk_of(depth // pieces)
-    down_grad = down_grads(place, pieces, near_g, far_g, hidw, depth, 0, chunks // 2)
-    gate_grad = columns_grad(place, pieces, near_x, far_x, dgate, depth)
-    up_grad = columns_grad(place, pieces, near_x, far_x, dup, depth)
-    down_grad = down_grads(
-        place, pieces, near_g, far_g, hidw, depth, chunks // 2, chunks, [down_grad]
+    chunks = depth // chunk_of(depth // pieces, GRAD_CHUNK)
+    some = chunks // 3
+    (gate_grad,) = weight_grads(place, pieces, near_x, far_x, depth, True, [(dgate, 0, some, None)])
+    gate_grad, up_grad = weight_grads(
+        place, pieces, near_x, far_x, depth, True,
+        [(dgate, some, chunks, gate_grad), (dup, 0, chunks, None)],
+    )
+    (down_grad,) = weight_grads(
+        place, pieces, near_g, far_g, depth, False, [(hidw, 0, chunks, None)]
     )
 
     blocks = pair_sums(near_d, other_d, experts, len(planes))

time: 84.2 us -> 76.3 us (0.906)
  Pallas kernels: 56.7 us -> 47.1 us
  waiting for transfers between devices: 2.26 us -> 4.45 us
    pallas_call x10 -> x6, Pallas kernels: 48.4 us -> 38.9 us  [the longest x3 16.9 us: weight_grads(): local_call(functools.partial(weight_kernel, pieces=pieces, jobs=[job[1:3]...]
    ppermute x3, waiting for transfers between devices: 0.01 us -> 2.28 us  [swap(): return lax.ppermute(value, 'expert', [(e, e ^ 1) for e in range(experts)])]
    ppermute x6, waiting for transfers between devices: 2.22 us -> 0.67 us  [along(): return lax.ppermute(value, 'tensor', pairs)]
    ppermute x9, waiting for transfers between devices: 0.02 us -> 1.5 us  [across(): return lax.ppermute(value, ('expert', 'seq'), pairs)]
  transfers between devices with their start and end apart: 18 -> 18, of which waited for: 3 -> 5; matrix products, arithmetic and copies ran while one was open for 1% -> 1% of each run, Pallas kernels for 58% -> 51%
where the time goes in v3:
time: 76.3 us; the launch traced here: 76.1 us
  Pallas kernels  47.1 us (62%)
  starting transfers between devices  22.2 us (29%)
  waiting for transfers between devices  4.45 us (6%)
  other arithmetic  1.47 us (2%)
  between operations  0.83 us (1%)
    pallas_call x3, Pallas kernels, weight_grads(): local_call(functools.partial(weight_kernel, pieces=pieces, jobs=[job[1:3]...  16.9 us
    pallas_call x2, Pallas kernels, turned(): local_call(shared, 'turned', 7 * len(kinds), 0, 0, [SMEM] + [HBM] * len(w...  12 us
    ppermute x6, starting transfers between devices, along(): return lax.ppermute(value, 'tensor', pairs)  11.2 us
    ppermute x9, starting transfers between devices, across(): return lax.ppermute(value, ('expert', 'seq'), pairs)  10.7 us
    pallas_call x1, Pallas kernels, gate_up(): local_call(functools.partial(gate_up_kernel, pieces=pieces), 'gate_up', 1...  9.95 us
    pallas_call x1, Pallas kernels, middle(): local_call(functools.partial(middle_kernel, pieces=pieces, experts=expert...  6.07 us
    ppermute x3, waiting for transfers between devices, swap(): return lax.ppermute(value, 'expert', [(e, e ^ 1) for e in range(experts)])  2.28 us
  transfers between devices with their start and end apart: 18, of which 5 were waited for; matrix products, arithmetic and copies ran while one was open for 1% of the time, Pallas kernels for 51%

profile of v3, /device:TPU:0, one launch (start us, length us, event | category | flops | bytes accessed | tf_op | source)
XLA Modules:
  0.0 76.1 jit_solution(1083514544767520894)
XLA Ops:
  0.6 0.8 %first_pair.1.refs_0_ = bf16[32,1536]{1,0:T(8,128)(2,1)S(1)} custom-call(bf16[16,1536]{1,0:T(8,128)(2,1)} %x.1, bf16[16,1536]{1,0:T(8,128)(2,1)} %g.1), custom_call_target="tpu_custom_call" | custom-call | bytes 196608 | tf_op jit(solution)/shard_map/first_pair/pallas_call | solution.py:369
  1.5 3.1 %collective-permute-start = (bf16[32,1536]{1,0:T(8,128)(2,1)S(1)}, bf16[32,1536]{1,0:T(8,128)(2,1)S(1)}, u32[]{:S(2)}, u32[]{:S(2)}) collective-permute-start(bf16[32,1536]{1,0:T(8,128)(2,1)S(1)} %first_pair.1.refs_0_), channel_id=1, source_target_pairs={{0,1},{1,2},{2,3},{3,0},{4,5},{5,6},{6,7},{7,4},{8,9},{9,10},{10,1... | collective-permute-start | bytes 294920 | tf_op jit(solution)/shard_map/ppermute | solution.py:509
  4.6 2.6 %collective-permute-start.1 = (bf16[32,1536]{1,0:T(8,128)(2,1)S(1)}, bf16[32,1536]{1,0:T(8,128)(2,1)S(1)}, u32[]{:S(2)}, u32[]{:S(2)}) collective-permute-start(bf16[32,1536]{1,0:T(8,128)(2,1)S(1)} %first_pair.1.refs_0_), channel_id=1, source_target_pairs={{0,2},{1,3},{2,0},{3,1},{4,6},{5,7},{6,4},{7,5},{8,10},{9,11},{10,... | collective-permute-start | bytes 294920 | tf_op jit(solution)/shard_map/ppermute | solution.py:509
  7.1 1.3 %collective-permute-start.2 = (bf16[32,1536]{1,0:T(8,128)(2,1)S(1)}, bf16[32,1536]{1,0:T(8,128)(2,1)S(1)}, u32[]{:S(2)}, u32[]{:S(2)}) collective-permute-start(bf16[32,1536]{1,0:T(8,128)(2,1)S(1)} %first_pair.1.refs_0_), channel_id=1, source_target_pairs={{0,3},{1,0},{2,1},{3,2},{4,7},{5,4},{6,5},{7,6},{8,11},{9,8},{10,9... | collective-permute-start | bytes 294920 | tf_op jit(solution)/shard_map/ppermute | solution.py:509
  9.2 3.9 %turned.2 = (bf16[1536,1024]{1,0:T(8,128)(2,1)S(1)}, bf16[1536,1024]{1,0:T(8,128)(2,1)S(1)}) custom-call(s32[2]{0:T(128)S(1)} %pad_add_fusion.place, bf16[1,1024,6144]{2,1,0:T(8,128)(2,1)} %refs_1_.1), custom_call_target="tpu_custom_call" | custom-call | tf_op jit(solution)/shard_map/turned/pallas_call | solution.py:132
  13.8 1.6 %collective-permute-start.6 = (bf16[16,6272]{1,0:T(8,128)(2,1)S(1)}, bf16[16,6272]{1,0:T(8,128)(2,1)S(1)}, u32[]{:S(2)}, u32[]{:S(2)}) collective-permute-start(bf16[16,6272]{1,0:T(8,128)(2,1)S(1)} %get-tuple-element.41.refs_0_), channel_id=1, source_target_pairs={{0,16},{4,20},{8,24},{12,28},{16,0},{20,4},{24,8},{28,12},{1,17},{... | collective-permute-start | bytes 602120 | tf_op jit(solution)/shard_map/ppermute | solution.py:517
  15.4 1.5 %collective-permute-start.7 = (bf16[16,6272]{1,0:T(8,128)(2,1)S(1)}, bf16[16,6272]{1,0:T(8,128)(2,1)S(1)}, u32[]{:S(2)}, u32[]{:S(2)}) collective-permute-start(bf16[16,6272]{1,0:T(8,128)(2,1)S(1)} %get-tuple-element.41.refs_0_), channel_id=1, source_target_pairs={{0,4},{4,0},{8,12},{12,8},{16,20},{20,16},{24,28},{28,24},{1,5},{5... | collective-permute-start | bytes 602120 | tf_op jit(solution)/shard_map/ppermute | solution.py:517
  17.4 8.0 %turned.3 = (bf16[1024,1536]{1,0:T(8,128)(2,1)S(1)}, bf16[1024,1536]{1,0:T(8,128)(2,1)S(1)}, bf16[1024,1536]{1,0:T(8,128)(2,1)S(1)}, bf16[1024,1536]{1,0:T(8,128...) custom-call(s32[2]{0:T(128)S(1)} %pad_add_fusion.place, bf16[1,6144,1024]{2,1,0:T(8,128)(2,1)} %refs_0_.3, ...), custom_call_target="tpu_custom_call" | custom-call | tf_op jit(solution)/shard_map/turned/pallas_call | solution.py:132
  25.4 0.7 collective-permute-done.7.refs_2_
  26.3 1.3 %collective-permute-start.3 = (bf16[16,6144]{1,0:T(8,128)(2,1)S(1)}, bf16[16,6144]{1,0:T(8,128)(2,1)S(1)}, u32[]{:S(2)}, u32[]{:S(2)}) collective-permute-start(bf16[16,6144]{1,0:T(8,128)(2,1)S(1)} %get-tuple-element.40.refs_0_), channel_id=1, source_target_pairs={{0,16},{4,20},{8,24},{12,28},{16,0},{20,4},{24,8},{28,12},{1,17},{... | collective-permute-start | bytes 589832 | tf_op jit(solution)/shard_map/ppermute | solution.py:517
  27.6 1.1 %collective-permute-start.4 = (bf16[16,6144]{1,0:T(8,128)(2,1)S(1)}, bf16[16,6144]{1,0:T(8,128)(2,1)S(1)}, u32[]{:S(2)}, u32[]{:S(2)}) collective-permute-start(bf16[16,6144]{1,0:T(8,128)(2,1)S(1)} %get-tuple-element.40.refs_0_), channel_id=1, source_target_pairs={{0,4},{4,0},{8,12},{12,8},{16,20},{20,16},{24,28},{28,24},{1,5},{5... | collective-permute-start | bytes 589832 | tf_op jit(solution)/shard_map/ppermute | solution.py:517
  28.7 1.2 %collective-permute-start.5 = (bf16[16,6144]{1,0:T(8,128)(2,1)S(1)}, bf16[16,6144]{1,0:T(8,128)(2,1)S(1)}, u32[]{:S(2)}, u32[]{:S(2)}) collective-permute-start(bf16[16,6144]{1,0:T(8,128)(2,1)S(1)} %get-tuple-element.40.refs_0_), channel_id=1, source_target_pairs={{0,20},{4,16},{8,28},{12,24},{16,4},{20,0},{24,12},{28,8},{1,21},{... | collective-permute-start | bytes 589832 | tf_op jit(solution)/shard_map/ppermute | solution.py:517
  29.9 10.0 %gate_up.1 = (f32[128,1024]{1,0:T(8,128)S(1)}, f32[128,1024]{1,0:T(8,128)S(1)}, f32[128,128]{1,0:T(8,128)S(1)}, bf16[1024,1536]{1,0:T(8,128)(2,1)S(1)}, bf16[102...) custom-call(s32[2]{0:T(128)S(1)} %pad_add_fusion.place, ...), custom_call_target="tpu_custom_call" | custom-call | tf_op jit(solution)/shard_map/gate_up/pallas_call | solution.py:197
  40.0 2.3 %collective-permute-done.10.go.far = bf16[64,6144]{1,0:T(8,128)(2,1)S(1)} collective-permute-done((bf16[64,6144]{1,0:T(8,128)(2,1)S(1)}, bf16[64,6144]{1,0:T(8,128)(2,1)S(1)}, u32[]{:S(2)}, u32[]{:S(2)}) %collective-permute-start.10) | collective-permute-done | bytes 786464 | tf_op jit(solution)/shard_map/ppermute | solution.py:520
  42.3 6.1 %middle.1 = (bf16[64,6272]{1,0:T(8,128)(2,1)S(1)}, bf16[64,6272]{1,0:T(8,128)(2,1)S(1)}, bf16[128,1024]{1,0:T(8,128)(2,1)S(1)}, bf16[128,1024]{1,0:T(8,128)(2,1)S(1)}, bf16[128,1024]{1,0:T(8,128)(2,1)S(1)}) custom-call(s32[2]{0:T(128)S(1)} %pad_add_fusion.place, bf16[64,6144]{1,0:T(8,128)(2,1)S(1)} %stacked.3.gp.near, ...), custom_call_target="tpu_custom_call" | custom-call | tf_op jit(solution)/shard_map/middle/pallas_call | solution.py:265
  48.5 2.9 %weight_grads.3.refs_2_ = bf16[1,6144,1024]{2,1,0:T(8,128)(2,1)} custom-call(s32[2]{0:T(128)S(1)} %pad_add_fusion.place, bf16[64,6272]{1,0:T(8,128)(2,1)S(1)} %stacked.2.xp.near, bf16[64,6272]{1,0:T(8,128)(2,1)S(1)} %collective-permute-done.9.xo.far, bf16[128,1024]{1,0:T(8,128)(2,1)S(1)} %get-tuple-element.68.refs_0_), custom_call_target="tpu_custom_call" | custom-call | flops 536870912 | bytes 4194304 | tf_op jit(solution)/shard_map/weight_grads/pallas_call | solution.py:308
  51.9 1.3 %collective-permute-start.12 = (bf16[16,6272]{1,0:T(8,128)(2,1)S(1)}, bf16[16,6272]{1,0:T(8,128)(2,1)S(1)}, u32[]{:S(2)}, u32[]{:S(2)}) collective-permute-start(bf16[16,6272]{1,0:T(8,128)(2,1)S(1)} %get-tuple-element.59), channel_id=1, source_target_pairs={{0,16},{4,20},{8,24},{12,28},{16,0},{20,4},{24,8},{28,12},{1,17},{... | collective-permute-start | bytes 602120 | tf_op jit(solution)/shard_map/ppermute | solution.py:517
  53.2 1.1 %collective-permute-start.13 = (bf16[16,6272]{1,0:T(8,128)(2,1)S(1)}, bf16[16,6272]{1,0:T(8,128)(2,1)S(1)}, u32[]{:S(2)}, u32[]{:S(2)}) collective-permute-start(bf16[16,6272]{1,0:T(8,128)(2,1)S(1)} %get-tuple-element.60), channel_id=1, source_target_pairs={{0,4},{4,0},{8,12},{12,8},{16,20},{20,16},{24,28},{28,24},{1,5},{5... | collective-permute-start | bytes 602120 | tf_op jit(solution)/shard_map/ppermute | solution.py:517
  54.2 1.2 %collective-permute-start.14 = (bf16[16,6272]{1,0:T(8,128)(2,1)S(1)}, bf16[16,6272]{1,0:T(8,128)(2,1)S(1)}, u32[]{:S(2)}, u32[]{:S(2)}) collective-permute-start(bf16[16,6272]{1,0:T(8,128)(2,1)S(1)} %get-tuple-element.61), channel_id=1, source_target_pairs={{0,20},{4,16},{8,28},{12,24},{16,4},{20,0},{24,12},{28,8},{1,21},{... | collective-permute-start | bytes 602120 | tf_op jit(solution)/shard_map/ppermute | solution.py:517
  55.4 8.3 %weight_grads.4 = (bf16[1,6144,1024]{2,1,0:T(8,128)(2,1)}, bf16[1,6144,1024]{2,1,0:T(8,128)(2,1)}) custom-call(s32[2]{0:T(128)S(1)} %pad_add_fusion.place, bf16[64,6272]{1,0:T(8,128)(2,1)S(1)} %stacked.2.xp.near, bf16[64,6272]{1,0:T(8,128)(2,1)S(1)} %collective-permute-done.9.xo.far, ...), custom_call_target="tpu_custom_call", output_to_operand_aliasing={{0}: (5, {})} | custom-call | flops 2684354560 | bytes 20971520 | tf_op jit(solution)/shard_map/weight_grads/pallas_call | solution.py:308
  63.7 0.7 collective-permute-done.14.refs_3_
  64.7 3.2 %collective-permute-start.15 = (bf16[16,1664]{1,0:T(8,128)(2,1)S(1)}, bf16[16,1664]{1,0:T(8,128)(2,1)S(1)}, u32[]{:S(2)}, u32[]{:S(2)}) collective-permute-start(bf16[16,1664]{1,0:T(8,128)(2,1)S(1)} %get-tuple-element.63), channel_id=1, source_target_pairs={{0,3},{1,0},{2,1},{3,2},{4,7},{5,4},{6,5},{7,6},{8,11},{9,8},{10,9... | collective-permute-start | bytes 159752 | tf_op jit(solution)/shard_map/ppermute | solution.py:509
  67.8 1.0 %collective-permute-start.16 = (bf16[16,1664]{1,0:T(8,128)(2,1)S(1)}, bf16[16,1664]{1,0:T(8,128)(2,1)S(1)}, u32[]{:S(2)}, u32[]{:S(2)}) collective-permute-start(bf16[16,1664]{1,0:T(8,128)(2,1)S(1)} %get-tuple-element.64), channel_id=1, source_target_pairs={{0,2},{1,3},{2,0},{3,1},{4,6},{5,7},{6,4},{7,5},{8,10},{9,11},{10,... | collective-permute-start | bytes 159752 | tf_op jit(solution)/shard_map/ppermute | solution.py:509
  68.8 5.8 %weight_grads.5 = bf16[1,1024,6144]{2,1,0:T(8,128)(2,1)} custom-call(s32[2]{0:T(128)S(1)} %pad_add_fusion.place, bf16[64,6144]{1,0:T(8,128)(2,1)S(1)} %stacked.3.gp.near, bf16[64,6144]{1,0:T(8,128)(2,1)S(1)} %collective-permute-done.10.go.far, bf16[128,1024]{1,0:T(8,128)(2,1)S(1)} %get-tuple-element.72.refs_0_), custom_call_target="tpu_custom_call" | custom-call | flops 1610612736 | bytes 12582912 | tf_op jit(solution)/shard_map/weight_grads/pallas_call | solution.py:308
  (32 shorter events, 4.3 us)
Async XLA Ops:
  1.5 11.8 %collective-permute-start = (bf16[32,1536]{1,0:T(8,128)(2,1)S(1)}, bf16[32,1536]{1,0:T(8,128)(2,1)S(1)}, u32[]{:S(2)}, u32[]{:S(2)}) collective-permute-start(bf16[32,1536]{1,0:T(8,128)(2,1)S(1)} %first_pair.1.refs_0_), channel_id=1, source_target_pairs={{0,1},{1,2},{2,3},{3,0},{4,5},{5,6},{6,7},{7,4},{8,9},{9,10},{10,1... | collective-permute-start | bytes 294920 | tf_op jit(solution)/shard_map/ppermute | solution.py:509
  4.6 9.2 %collective-permute-start.1 = (bf16[32,1536]{1,0:T(8,128)(2,1)S(1)}, bf16[32,1536]{1,0:T(8,128)(2,1)S(1)}, u32[]{:S(2)}, u32[]{:S(2)}) collective-permute-start(bf16[32,1536]{1,0:T(8,128)(2,1)S(1)} %first_pair.1.refs_0_), channel_id=1, source_target_pairs={{0,2},{1,3},{2,0},{3,1},{4,6},{5,7},{6,4},{7,5},{8,10},{9,11},{10,... | collective-permute-start | bytes 294920 | tf_op jit(solution)/shard_map/ppermute | solution.py:509
  7.1 6.6 %collective-permute-start.2 = (bf16[32,1536]{1,0:T(8,128)(2,1)S(1)}, bf16[32,1536]{1,0:T(8,128)(2,1)S(1)}, u32[]{:S(2)}, u32[]{:S(2)}) collective-permute-start(bf16[32,1536]{1,0:T(8,128)(2,1)S(1)} %first_pair.1.refs_0_), channel_id=1, source_target_pairs={{0,3},{1,0},{2,1},{3,2},{4,7},{5,4},{6,5},{7,6},{8,11},{9,8},{10,9... | collective-permute-start | bytes 294920 | tf_op jit(solution)/shard_map/ppermute | solution.py:509
  9.2 3.9 %copy-start = (s32[16,2]{0,1:T(2,128)S(1)}, s32[16,2]{0,1:T(2,128)}, u32[]{:S(2)}) copy-start(s32[16,2]{0,1:T(2,128)} %param.9) | copy-start | bytes 388
  13.8 11.6 %collective-permute-start.6 = (bf16[16,6272]{1,0:T(8,128)(2,1)S(1)}, bf16[16,6272]{1,0:T(8,128)(2,1)S(1)}, u32[]{:S(2)}, u32[]{:S(2)}) collective-permute-start(bf16[16,6272]{1,0:T(8,128)(2,1)S(1)} %get-tuple-element.41.refs_0_), channel_id=1, source_target_pairs={{0,16},{4,20},{8,24},{12,28},{16,0},{20,4},{24,8},{28,12},{1,17},{... | collective-permute-start | bytes 602120 | tf_op jit(solution)/shard_map/ppermute | solution.py:517
  15.4 10.8 %collective-permute-start.7 = (bf16[16,6272]{1,0:T(8,128)(2,1)S(1)}, bf16[16,6272]{1,0:T(8,128)(2,1)S(1)}, u32[]{:S(2)}, u32[]{:S(2)}) collective-permute-start(bf16[16,6272]{1,0:T(8,128)(2,1)S(1)} %get-tuple-element.41.refs_0_), channel_id=1, source_target_pairs={{0,4},{4,0},{8,12},{12,8},{16,20},{20,16},{24,28},{28,24},{1,5},{5... | collective-permute-start | bytes 602120 | tf_op jit(solution)/shard_map/ppermute | solution.py:517
  16.9 9.3 %collective-permute-start.8 = (bf16[16,6272]{1,0:T(8,128)(2,1)S(1)}, bf16[16,6272]{1,0:T(8,128)(2,1)S(1)}, u32[]{:S(2)}, u32[]{:S(2)}) collective-permute-start(bf16[16,6272]{1,0:T(8,128)(2,1)S(1)} %get-tuple-element.41.refs_0_), channel_id=1, source_target_pairs={{0,20},{4,16},{8,28},{12,24},{16,4},{20,0},{24,12},{28,8},{1,21},{... | collective-permute-start | bytes 602120 | tf_op jit(solution)/shard_map/ppermute | solution.py:517
  26.2 3.6 %collective-permute-start.9 = (bf16[64,6272]{1,0:T(8,128)(2,1)S(1)}, bf16[64,6272]{1,0:T(8,128)(2,1)S(1)}, u32[]{:S(2)}, u32[]{:S(2)}) collective-permute-start(bf16[64,6272]{1,0:T(8,128)(2,1)S(1)} %stacked.2.xp.near), channel_id=1, source_target_pairs={{0,8},{8,0},{16,24},{24,16},{1,9},{9,1},{17,25},{25,17},{2,10},{10... | collective-permute-start | bytes 2408456 | tf_op jit(solution)/shard_map/ppermute | solution.py:520
  26.3 13.5 %collective-permute-start.3 = (bf16[16,6144]{1,0:T(8,128)(2,1)S(1)}, bf16[16,6144]{1,0:T(8,128)(2,1)S(1)}, u32[]{:S(2)}, u32[]{:S(2)}) collective-permute-start(bf16[16,6144]{1,0:T(8,128)(2,1)S(1)} %get-tuple-element.40.refs_0_), channel_id=1, source_target_pairs={{0,16},{4,20},{8,24},{12,28},{16,0},{20,4},{24,8},{28,12},{1,17},{... | collective-permute-start | bytes 589832 | tf_op jit(solution)/shard_map/ppermute | solution.py:517
  27.6 12.2 %collective-permute-start.4 = (bf16[16,6144]{1,0:T(8,128)(2,1)S(1)}, bf16[16,6144]{1,0:T(8,128)(2,1)S(1)}, u32[]{:S(2)}, u32[]{:S(2)}) collective-permute-start(bf16[16,6144]{1,0:T(8,128)(2,1)S(1)} %get-tuple-element.40.refs_0_), channel_id=1, source_target_pairs={{0,4},{4,0},{8,12},{12,8},{16,20},{20,16},{24,28},{28,24},{1,5},{5... | collective-permute-start | bytes 589832 | tf_op jit(solution)/shard_map/ppermute | solution.py:517
  28.7 11.2 %collective-permute-start.5 = (bf16[16,6144]{1,0:T(8,128)(2,1)S(1)}, bf16[16,6144]{1,0:T(8,128)(2,1)S(1)}, u32[]{:S(2)}, u32[]{:S(2)}) collective-permute-start(bf16[16,6144]{1,0:T(8,128)(2,1)S(1)} %get-tuple-element.40.refs_0_), channel_id=1, source_target_pairs={{0,20},{4,16},{8,28},{12,24},{16,4},{20,0},{24,12},{28,8},{1,21},{... | collective-permute-start | bytes 589832 | tf_op jit(solution)/shard_map/ppermute | solution.py:517
  39.9 2.4 %collective-permute-start.10 = (bf16[64,6144]{1,0:T(8,128)(2,1)S(1)}, bf16[64,6144]{1,0:T(8,128)(2,1)S(1)}, u32[]{:S(2)}, u32[]{:S(2)}) collective-permute-start(bf16[64,6144]{1,0:T(8,128)(2,1)S(1)} %stacked.3.gp.near), channel_id=1, source_target_pairs={{0,8},{8,0},{16,24},{24,16},{1,9},{9,1},{17,25},{25,17},{2,10},{10... | collective-permute-start | bytes 2359304 | tf_op jit(solution)/shard_map/ppermute | solution.py:520
  48.3 3.1 %collective-permute-start.11 = (bf16[64,6272]{1,0:T(8,128)(2,1)S(1)}, bf16[64,6272]{1,0:T(8,128)(2,1)S(1)}, u32[]{:S(2)}, u32[]{:S(2)}) collective-permute-start(bf16[64,6272]{1,0:T(8,128)(2,1)S(1)} %get-tuple-element.57), channel_id=1, source_target_pairs={{0,8},{8,0},{16,24},{24,16},{1,9},{9,1},{17,25},{25,17},{2,10},{10... | collective-permute-start | bytes 2408456 | tf_op jit(solution)/shard_map/ppermute | solution.py:520
  51.9 11.8 %collective-permute-start.12 = (bf16[16,6272]{1,0:T(8,128)(2,1)S(1)}, bf16[16,6272]{1,0:T(8,128)(2,1)S(1)}, u32[]{:S(2)}, u32[]{:S(2)}) collective-permute-start(bf16[16,6272]{1,0:T(8,128)(2,1)S(1)} %get-tuple-element.59), channel_id=1, source_target_pairs={{0,16},{4,20},{8,24},{12,28},{16,0},{20,4},{24,8},{28,12},{1,17},{... | collective-permute-start | bytes 602120 | tf_op jit(solution)/shard_map/ppermute | solution.py:517
  53.2 10.5 %collective-permute-start.13 = (bf16[16,6272]{1,0:T(8,128)(2,1)S(1)}, bf16[16,6272]{1,0:T(8,128)(2,1)S(1)}, u32[]{:S(2)}, u32[]{:S(2)}) collective-permute-start(bf16[16,6272]{1,0:T(8,128)(2,1)S(1)} %get-tuple-element.60), channel_id=1, source_target_pairs={{0,4},{4,0},{8,12},{12,8},{16,20},{20,16},{24,28},{28,24},{1,5},{5... | collective-permute-start | bytes 602120 | tf_op jit(solution)/shard_map/ppermute | solution.py:517
  54.2 10.2 %collective-permute-start.14 = (bf16[16,6272]{1,0:T(8,128)(2,1)S(1)}, bf16[16,6272]{1,0:T(8,128)(2,1)S(1)}, u32[]{:S(2)}, u32[]{:S(2)}) collective-permute-start(bf16[16,6272]{1,0:T(8,128)(2,1)S(1)} %get-tuple-element.61), channel_id=1, source_target_pairs={{0,20},{4,16},{8,28},{12,24},{16,4},{20,0},{24,12},{28,8},{1,21},{... | collective-permute-start | bytes 602120 | tf_op jit(solution)/shard_map/ppermute | solution.py:517
  64.7 9.9 %collective-permute-start.15 = (bf16[16,1664]{1,0:T(8,128)(2,1)S(1)}, bf16[16,1664]{1,0:T(8,128)(2,1)S(1)}, u32[]{:S(2)}, u32[]{:S(2)}) collective-permute-start(bf16[16,1664]{1,0:T(8,128)(2,1)S(1)} %get-tuple-element.63), channel_id=1, source_target_pairs={{0,3},{1,0},{2,1},{3,2},{4,7},{5,4},{6,5},{7,6},{8,11},{9,8},{10,9... | collective-permute-start | bytes 159752 | tf_op jit(solution)/shard_map/ppermute | solution.py:509
  67.8 6.8 %collective-permute-start.16 = (bf16[16,1664]{1,0:T(8,128)(2,1)S(1)}, bf16[16,1664]{1,0:T(8,128)(2,1)S(1)}, u32[]{:S(2)}, u32[]{:S(2)}) collective-permute-start(bf16[16,1664]{1,0:T(8,128)(2,1)S(1)} %get-tuple-element.64), channel_id=1, source_target_pairs={{0,2},{1,3},{2,0},{3,1},{4,6},{5,7},{6,4},{7,5},{8,10},{9,11},{10,... | collective-permute-start | bytes 159752 | tf_op jit(solution)/shard_map/ppermute | solution.py:509
  68.8 5.9 %collective-permute-start.17 = (bf16[16,1664]{1,0:T(8,128)(2,1)S(1)}, bf16[16,1664]{1,0:T(8,128)(2,1)S(1)}, u32[]{:S(2)}, u32[]{:S(2)}) collective-permute-start(bf16[16,1664]{1,0:T(8,128)(2,1)S(1)} %get-tuple-element.65), channel_id=1, source_target_pairs={{0,1},{1,2},{2,3},{3,0},{4,5},{5,6},{6,7},{7,4},{8,9},{9,10},{10,1... | collective-permute-start | bytes 159752 | tf_op jit(solution)/shard_map/ppermute | solution.py:509

commit v4 on v3

--- a/solution.py
+++ b/solution.py
@@ -379,18 +379,34 @@
     )(*(pltpu.with_memory_space_constraint(v, pltpu.HBM) for v in (x, g)))
 
 
+def token_columns(table, ids, weights):
+    choices, rows = ids.shape
+    table[...] = jnp.zeros_like(table)
+    table[:choices, :rows] = ids[...].astype(jnp.float32)
+    if weights is not None:
+        table[choices : 2 * choices, :rows] = weights[...].astype(jnp.float32)
+    return table[...].T[:rows]
+
+
 def line_pair_kernel(*refs):
-    *blocks, extra, _, line_x, line_g = refs
+    *blocks, ids, weights, _, line_x, line_g, table = refs
     rows = line_x.shape[0]
     width = blocks[0].shape[1]
     for k, block in enumerate(blocks):
         line_x[:, k * width : (k + 1) * width] = block[:rows, :]
         line_g[:, k * width : (k + 1) * width] = block[rows:, :]
-    line_x[:, len(blocks) * width :] = extra[...]
-
-
-def line_pair(blocks, extra, after):
-    rows = extra.shape[0]
+    choices = ids.shape[0]
+    columns = token_columns(table, ids, weights)
+    lane = lax.broadcasted_iota(jnp.int32, (rows, EXTRA), 1).astype(jnp.float32)
+    extra = jnp.zeros((rows, EXTRA), jnp.float32)
+    for k in range(choices):
+        hit = lane == columns[:, k : k + 1]
+        extra += jnp.where(hit, columns[:, choices + k : choices + k + 1], 0.0)
+    line_x[:, len(blocks) * width :] = extra.astype(jnp.bfloat16)
+
+
+def line_pair(blocks, ids, weights, after):
+    rows = ids.shape[1]
     depth = blocks[0].shape[1] * len(blocks)
     return local_call(
         line_pair_kernel,
@@ -398,10 +414,11 @@
         2,
         0,
         8 * rows * depth,
-        [VMEM] * (len(blocks) + 1) + [ANY],
+        [VMEM] * (len(blocks) + 2) + [ANY],
         [VMEM] * 2,
         [shaped((rows, depth + EXTRA)), shaped((rows, depth))],
-    )(*blocks, extra, after)
+        [pltpu.VMEM((8, EXTRA), jnp.float32)],
+    )(*blocks, ids, weights, after)
 
 
 def resplit(extra, experts):
@@ -473,15 +490,23 @@
 
 
 def line_kernel(*refs, experts):
-    blocks, (grads, routes) = refs[:-2], refs[-2:]
-    width = grads.shape[1]
+    *blocks, ids, grads, routes, table = refs
+    rows, width = grads.shape
     grads[...] = tree_sum([b[:, :width].astype(jnp.float32) for b in blocks]).astype(jnp.bfloat16)
     extra = tree_sum([b[:, width:].astype(jnp.float32) for b in blocks])
     total = extra + pltpu.roll(extra, EXTRA - experts, 1)
-    routes[...] = total.astype(jnp.bfloat16).astype(jnp.float32)
-
-
-def line_sums(blocks, experts):
+    total = total.astype(jnp.bfloat16).astype(jnp.float32)
+    columns = token_columns(table, ids, None)
+    lane = lax.broadcasted_iota(jnp.int32, (rows, EXTRA), 1)
+    chosen = jnp.zeros((rows, EXTRA), jnp.float32)
+    for k in range(ids.shape[0]):
+        hit = lane.astype(jnp.float32) == columns[:, k : k + 1]
+        value = jnp.sum(jnp.where(hit, total, 0.0), axis=1, keepdims=True)
+        chosen += jnp.where(lane == k, value, 0.0)
+    routes[...] = chosen.T[: ids.shape[0], :].astype(jnp.bfloat16)
+
+
+def line_sums(blocks, ids, experts):
     rows, width = blocks[0].shape[0], blocks[0].shape[1] - EXTRA
     return local_call(
         functools.partial(line_kernel, experts=experts),
@@ -489,10 +514,11 @@
         2,
         0,
         2 * blocks[0].size * len(blocks),
-        [VMEM] * len(blocks),
+        [VMEM] * (len(blocks) + 1),
         [VMEM] * 2,
-        [shaped((rows, width)), shaped((rows, EXTRA), jnp.float32)],
-    )(*blocks)
+        [shaped((rows, width)), shaped(ids.shape)],
+        [pltpu.VMEM((8, EXTRA), jnp.float32)],
+    )(*blocks, ids)
 
 
 def per_device(tokens_in, out_grad, route_ids, route_weight, gate_weight, up_weight, down_weight):
@@ -519,15 +545,13 @@
     def swap(value):
         return lax.ppermute(value, "expert", [(e, e ^ 1) for e in range(experts)])
 
-    expert_ids = jnp.arange(EXTRA, dtype=jnp.int32)
-    chosen = (route_ids[:, :, None] == expert_ids[None, None, :]).astype(jnp.float32)
-    weights = jnp.sum(chosen * route_weight.astype(jnp.float32)[:, :, None], axis=1)
+    ids, choice_weights = route_ids.T, route_weight.T
     both = first_pair(tokens_in, out_grad)
     arrived = [along(both, k) for k in range(1, pieces)]
     everything = range(pieces)
     early, late = range(pieces // 2), range(pieces // 2, pieces)
     (turned_down,) = turned(place, pieces, [(down_weight, False, early)], depth)
-    line_x, line_g = line_pair([both] + arrived, weights.astype(jnp.bfloat16), turned_down[0])
+    line_x, line_g = line_pair([both] + arrived, ids, choice_weights, turned_down[0])
     from_x = [across(line_x, dx, ds) for dx, ds in planes[1:]]
     turned_gate, more_down = turned(
         place, pieces, [(gate_weight, True, everything), (down_weight, False, late)], depth
@@ -545,7 +569,7 @@
 
     other_d = swap(far_d)
     chunks = depth // chunk_of(depth // pieces, GRAD_CHUNK)
-    some = chunks // 3
+    some = chunks // 5
     (gate_grad,) = weight_grads(place, pieces, near_x, far_x, depth, True, [(dgate, 0, some, None)])
     gate_grad, up_grad = weight_grads(
         place, pieces, near_x, far_x, depth, True,
@@ -561,8 +585,8 @@
     ]
     sends = plane_sums([blocks[0]] + arrived, experts, pieces)
     finals = [sends[0]] + [along(sends[k], -k) for k in range(1, pieces)]
-    x_grad, routes = line_sums(finals, experts)
-    route_grad = jnp.sum(chosen * routes[:, None, :], axis=2).astype(jnp.bfloat16)
+    x_grad, routes = line_sums(finals, ids, experts)
+    route_grad = routes.T
     return (x_grad, route_grad, gate_grad, up_grad, down_grad)
 
 

time: 76.3 us -> 75.2 us (0.986)
  other arithmetic: 1.47 us -> 0.07 us
  transfers between devices with their start and end apart: 18 -> 18, of which waited for: 5 -> 5; matrix products, arithmetic and copies ran while one was open for 1% -> 0% of each run, Pallas kernels for 51% -> 52%
where the time goes in v4:
time: 75.2 us; the launch traced here: 75 us
  Pallas kernels  47.4 us (63%)
  starting transfers between devices  22.2 us (30%)
  waiting for transfers between devices  4.49 us (6%)
  between operations  0.83 us (1%)
    pallas_call x3, Pallas kernels, weight_grads(): local_call(functools.partial(weight_kernel, pieces=pieces, jobs=[job[1:3]...  16.9 us
    pallas_call x2, Pallas kernels, turned(): local_call(shared, 'turned', 7 * len(kinds), 0, 0, [SMEM] + [HBM] * len(w...  12 us
    ppermute x6, starting transfers between devices, along(): return lax.ppermute(value, 'tensor', pairs)  11.2 us
    ppermute x9, starting transfers between devices, across(): return lax.ppermute(value, ('expert', 'seq'), pairs)  10.7 us
    pallas_call x1, Pallas kernels, gate_up(): local_call(functools.partial(gate_up_kernel, pieces=pieces), 'gate_up', 1...  9.97 us
    pallas_call x1, Pallas kernels, middle(): local_call(functools.partial(middle_kernel, pieces=pieces, experts=expert...  6.07 us
    ppermute x3, waiting for transfers between devices, swap(): return lax.ppermute(value, 'expert', [(e, e ^ 1) for e in range(experts)])  2.28 us
  transfers between devices with their start and end apart: 18, of which 5 were waited for; matrix products, arithmetic and copies ran while one was open for 0% of the time, Pallas kernels for 52%

profile of v4, /device:TPU:0, one launch (start us, length us, event | category | flops | bytes accessed | tf_op | source)
XLA Modules:
  0.0 75.0 jit_solution(5079058709538197853)
XLA Ops:
  0.6 0.8 %first_pair.1.refs_0_ = bf16[32,1536]{1,0:T(8,128)(2,1)S(1)} custom-call(bf16[16,1536]{1,0:T(8,128)(2,1)} %x.1, bf16[16,1536]{1,0:T(8,128)(2,1)} %g.1), custom_call_target="tpu_custom_call" | custom-call | bytes 196608 | tf_op jit(solution)/shard_map/first_pair/pallas_call | solution.py:369
  1.5 3.1 %collective-permute-start = (bf16[32,1536]{1,0:T(8,128)(2,1)S(1)}, bf16[32,1536]{1,0:T(8,128)(2,1)S(1)}, u32[]{:S(2)}, u32[]{:S(2)}) collective-permute-start(bf16[32,1536]{1,0:T(8,128)(2,1)S(1)} %first_pair.1.refs_0_), channel_id=1, source_target_pairs={{0,1},{1,2},{2,3},{3,0},{4,5},{5,6},{6,7},{7,4},{8,9},{9,10},{10,1... | collective-permute-start | bytes 294920 | tf_op jit(solution)/shard_map/ppermute | solution.py:535
  4.6 2.6 %collective-permute-start.1 = (bf16[32,1536]{1,0:T(8,128)(2,1)S(1)}, bf16[32,1536]{1,0:T(8,128)(2,1)S(1)}, u32[]{:S(2)}, u32[]{:S(2)}) collective-permute-start(bf16[32,1536]{1,0:T(8,128)(2,1)S(1)} %first_pair.1.refs_0_), channel_id=1, source_target_pairs={{0,2},{1,3},{2,0},{3,1},{4,6},{5,7},{6,4},{7,5},{8,10},{9,11},{10,... | collective-permute-start | bytes 294920 | tf_op jit(solution)/shard_map/ppermute | solution.py:535
  7.1 1.3 %collective-permute-start.2 = (bf16[32,1536]{1,0:T(8,128)(2,1)S(1)}, bf16[32,1536]{1,0:T(8,128)(2,1)S(1)}, u32[]{:S(2)}, u32[]{:S(2)}) collective-permute-start(bf16[32,1536]{1,0:T(8,128)(2,1)S(1)} %first_pair.1.refs_0_), channel_id=1, source_target_pairs={{0,3},{1,0},{2,1},{3,2},{4,7},{5,4},{6,5},{7,6},{8,11},{9,8},{10,9... | collective-permute-start | bytes 294920 | tf_op jit(solution)/shard_map/ppermute | solution.py:535
  8.6 3.9 %turned.2 = (bf16[1536,1024]{1,0:T(8,128)(2,1)S(1)}, bf16[1536,1024]{1,0:T(8,128)(2,1)S(1)}) custom-call(s32[2]{0:T(128)S(1)} %pad_add_fusion.place, bf16[1,1024,6144]{2,1,0:T(8,128)(2,1)} %refs_1_.1), custom_call_target="tpu_custom_call" | custom-call | tf_op jit(solution)/shard_map/turned/pallas_call | solution.py:132
  12.5 1.2 %collective-permute-done.1.refs_2_ = bf16[32,1536]{1,0:T(8,128)(2,1)S(1)} collective-permute-done((bf16[32,1536]{1,0:T(8,128)(2,1)S(1)}, bf16[32,1536]{1,0:T(8,128)(2,1)S(1)}, u32[]{:S(2)}, u32[]{:S(2)}) %collective-permute-start.1) | collective-permute-done | bytes 98336 | tf_op jit(solution)/shard_map/ppermute | solution.py:535
  13.9 1.6 %collective-permute-start.6 = (bf16[16,6272]{1,0:T(8,128)(2,1)S(1)}, bf16[16,6272]{1,0:T(8,128)(2,1)S(1)}, u32[]{:S(2)}, u32[]{:S(2)}) collective-permute-start(bf16[16,6272]{1,0:T(8,128)(2,1)S(1)} %get-tuple-element.41.refs_0_), channel_id=1, source_target_pairs={{0,16},{4,20},{8,24},{12,28},{16,0},{20,4},{24,8},{28,12},{1,17},{... | collective-permute-start | bytes 602120 | tf_op jit(solution)/shard_map/ppermute | solution.py:543
  15.5 1.5 %collective-permute-start.7 = (bf16[16,6272]{1,0:T(8,128)(2,1)S(1)}, bf16[16,6272]{1,0:T(8,128)(2,1)S(1)}, u32[]{:S(2)}, u32[]{:S(2)}) collective-permute-start(bf16[16,6272]{1,0:T(8,128)(2,1)S(1)} %get-tuple-element.41.refs_0_), channel_id=1, source_target_pairs={{0,4},{4,0},{8,12},{12,8},{16,20},{20,16},{24,28},{28,24},{1,5},{5... | collective-permute-start | bytes 602120 | tf_op jit(solution)/shard_map/ppermute | solution.py:543
  17.5 8.0 %turned.3 = (bf16[1024,1536]{1,0:T(8,128)(2,1)S(1)}, bf16[1024,1536]{1,0:T(8,128)(2,1)S(1)}, bf16[1024,1536]{1,0:T(8,128)(2,1)S(1)}, bf16[1024,1536]{1,0:T(8,128...) custom-call(s32[2]{0:T(128)S(1)} %pad_add_fusion.place, bf16[1,6144,1024]{2,1,0:T(8,128)(2,1)} %refs_0_.3, ...), custom_call_target="tpu_custom_call" | custom-call | tf_op jit(solution)/shard_map/turned/pallas_call | solution.py:132
  26.4 1.3 %collective-permute-start.3 = (bf16[16,6144]{1,0:T(8,128)(2,1)S(1)}, bf16[16,6144]{1,0:T(8,128)(2,1)S(1)}, u32[]{:S(2)}, u32[]{:S(2)}) collective-permute-start(bf16[16,6144]{1,0:T(8,128)(2,1)S(1)} %get-tuple-element.40.refs_0_), channel_id=1, source_target_pairs={{0,16},{4,20},{8,24},{12,28},{16,0},{20,4},{24,8},{28,12},{1,17},{... | collective-permute-start | bytes 589832 | tf_op jit(solution)/shard_map/ppermute | solution.py:543
  27.7 1.1 %collective-permute-start.4 = (bf16[16,6144]{1,0:T(8,128)(2,1)S(1)}, bf16[16,6144]{1,0:T(8,128)(2,1)S(1)}, u32[]{:S(2)}, u32[]{:S(2)}) collective-permute-start(bf16[16,6144]{1,0:T(8,128)(2,1)S(1)} %get-tuple-element.40.refs_0_), channel_id=1, source_target_pairs={{0,4},{4,0},{8,12},{12,8},{16,20},{20,16},{24,28},{28,24},{1,5},{5... | collective-permute-start | bytes 589832 | tf_op jit(solution)/shard_map/ppermute | solution.py:543
  28.8 1.2 %collective-permute-start.5 = (bf16[16,6144]{1,0:T(8,128)(2,1)S(1)}, bf16[16,6144]{1,0:T(8,128)(2,1)S(1)}, u32[]{:S(2)}, u32[]{:S(2)}) collective-permute-start(bf16[16,6144]{1,0:T(8,128)(2,1)S(1)} %get-tuple-element.40.refs_0_), channel_id=1, source_target_pairs={{0,20},{4,16},{8,28},{12,24},{16,4},{20,0},{24,12},{28,8},{1,21},{... | collective-permute-start | bytes 589832 | tf_op jit(solution)/shard_map/ppermute | solution.py:543
  30.0 10.0 %gate_up.1 = (f32[128,1024]{1,0:T(8,128)S(1)}, f32[128,1024]{1,0:T(8,128)S(1)}, f32[128,128]{1,0:T(8,128)S(1)}, bf16[1024,1536]{1,0:T(8,128)(2,1)S(1)}, bf16[102...) custom-call(s32[2]{0:T(128)S(1)} %pad_add_fusion.place, ...), custom_call_target="tpu_custom_call" | custom-call | tf_op jit(solution)/shard_map/gate_up/pallas_call | solution.py:197
  40.1 2.3 %collective-permute-done.10.go.far = bf16[64,6144]{1,0:T(8,128)(2,1)S(1)} collective-permute-done((bf16[64,6144]{1,0:T(8,128)(2,1)S(1)}, bf16[64,6144]{1,0:T(8,128)(2,1)S(1)}, u32[]{:S(2)}, u32[]{:S(2)}) %collective-permute-start.10) | collective-permute-done | bytes 786464 | tf_op jit(solution)/shard_map/ppermute | solution.py:546
  42.4 6.1 %middle.1 = (bf16[64,6272]{1,0:T(8,128)(2,1)S(1)}, bf16[64,6272]{1,0:T(8,128)(2,1)S(1)}, bf16[128,1024]{1,0:T(8,128)(2,1)S(1)}, bf16[128,1024]{1,0:T(8,128)(2,1)S(1)}, bf16[128,1024]{1,0:T(8,128)(2,1)S(1)}) custom-call(s32[2]{0:T(128)S(1)} %pad_add_fusion.place, bf16[64,6144]{1,0:T(8,128)(2,1)S(1)} %stacked.3.gp.near, ...), custom_call_target="tpu_custom_call" | custom-call | tf_op jit(solution)/shard_map/middle/pallas_call | solution.py:265
  48.7 2.2 %weight_grads.3.refs_2_ = bf16[1,6144,1024]{2,1,0:T(8,128)(2,1)} custom-call(s32[2]{0:T(128)S(1)} %pad_add_fusion.place, bf16[64,6272]{1,0:T(8,128)(2,1)S(1)} %stacked.2.xp.near, bf16[64,6272]{1,0:T(8,128)(2,1)S(1)} %collective-permute-done.9.xo.far, bf16[128,1024]{1,0:T(8,128)(2,1)S(1)} %get-tuple-element.68.refs_0_), custom_call_target="tpu_custom_call" | custom-call | flops 268435456 | bytes 2097152 | tf_op jit(solution)/shard_map/weight_grads/pallas_call | solution.py:308
  51.3 1.3 %collective-permute-start.12 = (bf16[16,6272]{1,0:T(8,128)(2,1)S(1)}, bf16[16,6272]{1,0:T(8,128)(2,1)S(1)}, u32[]{:S(2)}, u32[]{:S(2)}) collective-permute-start(bf16[16,6272]{1,0:T(8,128)(2,1)S(1)} %get-tuple-element.59), channel_id=1, source_target_pairs={{0,16},{4,20},{8,24},{12,28},{16,0},{20,4},{24,8},{28,12},{1,17},{... | collective-permute-start | bytes 602120 | tf_op jit(solution)/shard_map/ppermute | solution.py:543
  52.6 1.1 %collective-permute-start.13 = (bf16[16,6272]{1,0:T(8,128)(2,1)S(1)}, bf16[16,6272]{1,0:T(8,128)(2,1)S(1)}, u32[]{:S(2)}, u32[]{:S(2)}) collective-permute-start(bf16[16,6272]{1,0:T(8,128)(2,1)S(1)} %get-tuple-element.60), channel_id=1, source_target_pairs={{0,4},{4,0},{8,12},{12,8},{16,20},{20,16},{24,28},{28,24},{1,5},{5... | collective-permute-start | bytes 602120 | tf_op jit(solution)/shard_map/ppermute | solution.py:543
  53.7 1.2 %collective-permute-start.14 = (bf16[16,6272]{1,0:T(8,128)(2,1)S(1)}, bf16[16,6272]{1,0:T(8,128)(2,1)S(1)}, u32[]{:S(2)}, u32[]{:S(2)}) collective-permute-start(bf16[16,6272]{1,0:T(8,128)(2,1)S(1)} %get-tuple-element.61), channel_id=1, source_target_pairs={{0,20},{4,16},{8,28},{12,24},{16,4},{20,0},{24,12},{28,8},{1,21},{... | collective-permute-start | bytes 602120 | tf_op jit(solution)/shard_map/ppermute | solution.py:543
  54.9 8.9 %weight_grads.4 = (bf16[1,6144,1024]{2,1,0:T(8,128)(2,1)}, bf16[1,6144,1024]{2,1,0:T(8,128)(2,1)}) custom-call(s32[2]{0:T(128)S(1)} %pad_add_fusion.place, bf16[64,6272]{1,0:T(8,128)(2,1)S(1)} %stacked.2.xp.near, bf16[64,6272]{1,0:T(8,128)(2,1)S(1)} %collective-permute-done.9.xo.far, ...), custom_call_target="tpu_custom_call", output_to_operand_aliasing={{0}: (5, {})} | custom-call | flops 2952790016 | bytes 23068672 | tf_op jit(solution)/shard_map/weight_grads/pallas_call | solution.py:308
  64.1 3.2 %collective-permute-start.15 = (bf16[16,1664]{1,0:T(8,128)(2,1)S(1)}, bf16[16,1664]{1,0:T(8,128)(2,1)S(1)}, u32[]{:S(2)}, u32[]{:S(2)}) collective-permute-start(bf16[16,1664]{1,0:T(8,128)(2,1)S(1)} %get-tuple-element.63), channel_id=1, source_target_pairs={{0,3},{1,0},{2,1},{3,2},{4,7},{5,4},{6,5},{7,6},{8,11},{9,8},{10,9... | collective-permute-start | bytes 159752 | tf_op jit(solution)/shard_map/ppermute | solution.py:535
  67.2 1.0 %collective-permute-start.16 = (bf16[16,1664]{1,0:T(8,128)(2,1)S(1)}, bf16[16,1664]{1,0:T(8,128)(2,1)S(1)}, u32[]{:S(2)}, u32[]{:S(2)}) collective-permute-start(bf16[16,1664]{1,0:T(8,128)(2,1)S(1)} %get-tuple-element.64), channel_id=1, source_target_pairs={{0,2},{1,3},{2,0},{3,1},{4,6},{5,7},{6,4},{7,5},{8,10},{9,11},{10,... | collective-permute-start | bytes 159752 | tf_op jit(solution)/shard_map/ppermute | solution.py:535
  68.2 5.8 %weight_grads.5 = bf16[1,1024,6144]{2,1,0:T(8,128)(2,1)} custom-call(s32[2]{0:T(128)S(1)} %pad_add_fusion.place, bf16[64,6144]{1,0:T(8,128)(2,1)S(1)} %stacked.3.gp.near, bf16[64,6144]{1,0:T(8,128)(2,1)S(1)} %collective-permute-done.10.go.far, bf16[128,1024]{1,0:T(8,128)(2,1)S(1)} %get-tuple-element.72.refs_0_), custom_call_target="tpu_custom_call" | custom-call | flops 1610612736 | bytes 12582912 | tf_op jit(solution)/shard_map/weight_grads/pallas_call | solution.py:308
  74.2 0.9 %line_sums.1 = (bf16[16,1536]{1,0:T(8,128)(2,1)}, bf16[2,16]{1,0:T(2,128)(2,1)}) custom-call(bf16[16,1664]{1,0:T(8,128)(2,1)S(1)} %get-tuple-element.62.refs_0_, bf16[16,1664]{1,0:T(8,128)(2,1)S(1)} %collective-permute-done.15.refs_1_, bf16[16,1664]{1,0:T(8,128)(2,1)S(1)} %collective-permute-done.16.refs_2_, ...), custom_call_target="tpu_custom_call" | custom-call | bytes 212992 | tf_op jit(solution)/shard_map/line_sums/pallas_call | solution.py:511
  (31 shorter events, 2.7 us)
Async XLA Ops:
  1.5 11.0 %collective-permute-start = (bf16[32,1536]{1,0:T(8,128)(2,1)S(1)}, bf16[32,1536]{1,0:T(8,128)(2,1)S(1)}, u32[]{:S(2)}, u32[]{:S(2)}) collective-permute-start(bf16[32,1536]{1,0:T(8,128)(2,1)S(1)} %first_pair.1.refs_0_), channel_id=1, source_target_pairs={{0,1},{1,2},{2,3},{3,0},{4,5},{5,6},{6,7},{7,4},{8,9},{9,10},{10,1... | collective-permute-start | bytes 294920 | tf_op jit(solution)/shard_map/ppermute | solution.py:535
  4.6 9.2 %collective-permute-start.1 = (bf16[32,1536]{1,0:T(8,128)(2,1)S(1)}, bf16[32,1536]{1,0:T(8,128)(2,1)S(1)}, u32[]{:S(2)}, u32[]{:S(2)}) collective-permute-start(bf16[32,1536]{1,0:T(8,128)(2,1)S(1)} %first_pair.1.refs_0_), channel_id=1, source_target_pairs={{0,2},{1,3},{2,0},{3,1},{4,6},{5,7},{6,4},{7,5},{8,10},{9,11},{10,... | collective-permute-start | bytes 294920 | tf_op jit(solution)/shard_map/ppermute | solution.py:535
  7.1 6.6 %collective-permute-start.2 = (bf16[32,1536]{1,0:T(8,128)(2,1)S(1)}, bf16[32,1536]{1,0:T(8,128)(2,1)S(1)}, u32[]{:S(2)}, u32[]{:S(2)}) collective-permute-start(bf16[32,1536]{1,0:T(8,128)(2,1)S(1)} %first_pair.1.refs_0_), channel_id=1, source_target_pairs={{0,3},{1,0},{2,1},{3,2},{4,7},{5,4},{6,5},{7,6},{8,11},{9,8},{10,9... | collective-permute-start | bytes 294920 | tf_op jit(solution)/shard_map/ppermute | solution.py:535
  8.6 5.2 %copy-start = (s32[16,2]{0,1:T(2,128)S(1)}, s32[16,2]{0,1:T(2,128)}, u32[]{:S(2)}) copy-start(s32[16,2]{0,1:T(2,128)} %param.9) | copy-start | bytes 388
  8.6 5.2 %copy-start.1 = (bf16[16,2]{0,1:T(2,128)(2,1)S(1)}, bf16[16,2]{0,1:T(2,128)(2,1)}, u32[]{:S(2)}) copy-start(bf16[16,2]{0,1:T(2,128)(2,1)} %param.10) | copy-start | bytes 196
  13.9 11.6 %collective-permute-start.6 = (bf16[16,6272]{1,0:T(8,128)(2,1)S(1)}, bf16[16,6272]{1,0:T(8,128)(2,1)S(1)}, u32[]{:S(2)}, u32[]{:S(2)}) collective-permute-start(bf16[16,6272]{1,0:T(8,128)(2,1)S(1)} %get-tuple-element.41.refs_0_), channel_id=1, source_target_pairs={{0,16},{4,20},{8,24},{12,28},{16,0},{20,4},{24,8},{28,12},{1,17},{... | collective-permute-start | bytes 602120 | tf_op jit(solution)/shard_map/ppermute | solution.py:543
  15.5 10.8 %collective-permute-start.7 = (bf16[16,6272]{1,0:T(8,128)(2,1)S(1)}, bf16[16,6272]{1,0:T(8,128)(2,1)S(1)}, u32[]{:S(2)}, u32[]{:S(2)}) collective-permute-start(bf16[16,6272]{1,0:T(8,128)(2,1)S(1)} %get-tuple-element.41.refs_0_), channel_id=1, source_target_pairs={{0,4},{4,0},{8,12},{12,8},{16,20},{20,16},{24,28},{28,24},{1,5},{5... | collective-permute-start | bytes 602120 | tf_op jit(solution)/shard_map/ppermute | solution.py:543
  17.0 9.3 %collective-permute-start.8 = (bf16[16,6272]{1,0:T(8,128)(2,1)S(1)}, bf16[16,6272]{1,0:T(8,128)(2,1)S(1)}, u32[]{:S(2)}, u32[]{:S(2)}) collective-permute-start(bf16[16,6272]{1,0:T(8,128)(2,1)S(1)} %get-tuple-element.41.refs_0_), channel_id=1, source_target_pairs={{0,20},{4,16},{8,28},{12,24},{16,4},{20,0},{24,12},{28,8},{1,21},{... | collective-permute-start | bytes 602120 | tf_op jit(solution)/shard_map/ppermute | solution.py:543
  26.4 3.6 %collective-permute-start.9 = (bf16[64,6272]{1,0:T(8,128)(2,1)S(1)}, bf16[64,6272]{1,0:T(8,128)(2,1)S(1)}, u32[]{:S(2)}, u32[]{:S(2)}) collective-permute-start(bf16[64,6272]{1,0:T(8,128)(2,1)S(1)} %stacked.2.xp.near), channel_id=1, source_target_pairs={{0,8},{8,0},{16,24},{24,16},{1,9},{9,1},{17,25},{25,17},{2,10},{10... | collective-permute-start | bytes 2408456 | tf_op jit(solution)/shard_map/ppermute | solution.py:546
  26.4 13.5 %collective-permute-start.3 = (bf16[16,6144]{1,0:T(8,128)(2,1)S(1)}, bf16[16,6144]{1,0:T(8,128)(2,1)S(1)}, u32[]{:S(2)}, u32[]{:S(2)}) collective-permute-start(bf16[16,6144]{1,0:T(8,128)(2,1)S(1)} %get-tuple-element.40.refs_0_), channel_id=1, source_target_pairs={{0,16},{4,20},{8,24},{12,28},{16,0},{20,4},{24,8},{28,12},{1,17},{... | collective-permute-start | bytes 589832 | tf_op jit(solution)/shard_map/ppermute | solution.py:543
  27.7 12.3 %collective-permute-start.4 = (bf16[16,6144]{1,0:T(8,128)(2,1)S(1)}, bf16[16,6144]{1,0:T(8,128)(2,1)S(1)}, u32[]{:S(2)}, u32[]{:S(2)}) collective-permute-start(bf16[16,6144]{1,0:T(8,128)(2,1)S(1)} %get-tuple-element.40.refs_0_), channel_id=1, source_target_pairs={{0,4},{4,0},{8,12},{12,8},{16,20},{20,16},{24,28},{28,24},{1,5},{5... | collective-permute-start | bytes 589832 | tf_op jit(solution)/shard_map/ppermute | solution.py:543
  28.8 11.2 %collective-permute-start.5 = (bf16[16,6144]{1,0:T(8,128)(2,1)S(1)}, bf16[16,6144]{1,0:T(8,128)(2,1)S(1)}, u32[]{:S(2)}, u32[]{:S(2)}) collective-permute-start(bf16[16,6144]{1,0:T(8,128)(2,1)S(1)} %get-tuple-element.40.refs_0_), channel_id=1, source_target_pairs={{0,20},{4,16},{8,28},{12,24},{16,4},{20,0},{24,12},{28,8},{1,21},{... | collective-permute-start | bytes 589832 | tf_op jit(solution)/shard_map/ppermute | solution.py:543
  40.1 2.4 %collective-permute-start.10 = (bf16[64,6144]{1,0:T(8,128)(2,1)S(1)}, bf16[64,6144]{1,0:T(8,128)(2,1)S(1)}, u32[]{:S(2)}, u32[]{:S(2)}) collective-permute-start(bf16[64,6144]{1,0:T(8,128)(2,1)S(1)} %stacked.3.gp.near), channel_id=1, source_target_pairs={{0,8},{8,0},{16,24},{24,16},{1,9},{9,1},{17,25},{25,17},{2,10},{10... | collective-permute-start | bytes 2359304 | tf_op jit(solution)/shard_map/ppermute | solution.py:546
  48.5 2.4 %collective-permute-start.11 = (bf16[64,6272]{1,0:T(8,128)(2,1)S(1)}, bf16[64,6272]{1,0:T(8,128)(2,1)S(1)}, u32[]{:S(2)}, u32[]{:S(2)}) collective-permute-start(bf16[64,6272]{1,0:T(8,128)(2,1)S(1)} %get-tuple-element.57), channel_id=1, source_target_pairs={{0,8},{8,0},{16,24},{24,16},{1,9},{9,1},{17,25},{25,17},{2,10},{10... | collective-permute-start | bytes 2408456 | tf_op jit(solution)/shard_map/ppermute | solution.py:546
  51.3 12.5 %collective-permute-start.12 = (bf16[16,6272]{1,0:T(8,128)(2,1)S(1)}, bf16[16,6272]{1,0:T(8,128)(2,1)S(1)}, u32[]{:S(2)}, u32[]{:S(2)}) collective-permute-start(bf16[16,6272]{1,0:T(8,128)(2,1)S(1)} %get-tuple-element.59), channel_id=1, source_target_pairs={{0,16},{4,20},{8,24},{12,28},{16,0},{20,4},{24,8},{28,12},{1,17},{... | collective-permute-start | bytes 602120 | tf_op jit(solution)/shard_map/ppermute | solution.py:543
  52.6 11.2 %collective-permute-start.13 = (bf16[16,6272]{1,0:T(8,128)(2,1)S(1)}, bf16[16,6272]{1,0:T(8,128)(2,1)S(1)}, u32[]{:S(2)}, u32[]{:S(2)}) collective-permute-start(bf16[16,6272]{1,0:T(8,128)(2,1)S(1)} %get-tuple-element.60), channel_id=1, source_target_pairs={{0,4},{4,0},{8,12},{12,8},{16,20},{20,16},{24,28},{28,24},{1,5},{5... | collective-permute-start | bytes 602120 | tf_op jit(solution)/shard_map/ppermute | solution.py:543
  53.7 10.2 %collective-permute-start.14 = (bf16[16,6272]{1,0:T(8,128)(2,1)S(1)}, bf16[16,6272]{1,0:T(8,128)(2,1)S(1)}, u32[]{:S(2)}, u32[]{:S(2)}) collective-permute-start(bf16[16,6272]{1,0:T(8,128)(2,1)S(1)} %get-tuple-element.61), channel_id=1, source_target_pairs={{0,20},{4,16},{8,28},{12,24},{16,4},{20,0},{24,12},{28,8},{1,21},{... | collective-permute-start | bytes 602120 | tf_op jit(solution)/shard_map/ppermute | solution.py:543
  64.1 9.9 %collective-permute-start.15 = (bf16[16,1664]{1,0:T(8,128)(2,1)S(1)}, bf16[16,1664]{1,0:T(8,128)(2,1)S(1)}, u32[]{:S(2)}, u32[]{:S(2)}) collective-permute-start(bf16[16,1664]{1,0:T(8,128)(2,1)S(1)} %get-tuple-element.63), channel_id=1, source_target_pairs={{0,3},{1,0},{2,1},{3,2},{4,7},{5,4},{6,5},{7,6},{8,11},{9,8},{10,9... | collective-permute-start | bytes 159752 | tf_op jit(solution)/shard_map/ppermute | solution.py:535
  67.2 6.8 %collective-permute-start.16 = (bf16[16,1664]{1,0:T(8,128)(2,1)S(1)}, bf16[16,1664]{1,0:T(8,128)(2,1)S(1)}, u32[]{:S(2)}, u32[]{:S(2)}) collective-permute-start(bf16[16,1664]{1,0:T(8,128)(2,1)S(1)} %get-tuple-element.64), channel_id=1, source_target_pairs={{0,2},{1,3},{2,0},{3,1},{4,6},{5,7},{6,4},{7,5},{8,10},{9,11},{10,... | collective-permute-start | bytes 159752 | tf_op jit(solution)/shard_map/ppermute | solution.py:535
  68.2 5.9 %collective-permute-start.17 = (bf16[16,1664]{1,0:T(8,128)(2,1)S(1)}, bf16[16,1664]{1,0:T(8,128)(2,1)S(1)}, u32[]{:S(2)}, u32[]{:S(2)}) collective-permute-start(bf16[16,1664]{1,0:T(8,128)(2,1)S(1)} %get-tuple-element.65), channel_id=1, source_target_pairs={{0,1},{1,2},{2,3},{3,0},{4,5},{5,6},{6,7},{7,4},{8,9},{9,10},{10,1... | collective-permute-start | bytes 159752 | tf_op jit(solution)/shard_map/ppermute | solution.py:535

commit v5 on v4

--- a/solution.py
+++ b/solution.py
@@ -155,7 +155,7 @@
     wg, refs = refs[:pieces], refs[pieces:]
     gate, up, weight, *outs, buf, sems = refs
     hidden, width = wg[0].shape
-    size, chunks = whole_chunks(place[0], pieces, width * pieces, TURN_CHUNK)
+    size, chunks = whole_chunks(place[0], pieces, width * pieces)
     slots = buf.shape[0]
 
     def copy(j):
@@ -204,8 +204,8 @@
         [VMEM] * (3 + pieces),
         [out, out, shaped((2 * half, EXTRA), jnp.float32)] + [shaped((hidden, width))] * pieces,
         [
-            pltpu.VMEM((8, chunk_of(width, TURN_CHUNK), hidden), jnp.bfloat16),
-            pltpu.SemaphoreType.DMA((8,)),
+            pltpu.VMEM((4, chunk_of(width), hidden), jnp.bfloat16),
+            pltpu.SemaphoreType.DMA((4,)),
         ],
     )(place, near, far, pltpu.with_memory_space_constraint(w_up, pltpu.HBM), *turned_gate)
     return gate, up, weight, turned_up

time: 75.2 us -> 74.8 us (level)
  transfers between devices with their start and end apart: 18 -> 18, of which waited for: 5 -> 5; matrix products, arithmetic and copies ran while one was open for 0% -> 0% of each run, Pallas kernels for 52% -> 51%
where the time goes in v5:
time: 74.8 us; the launch traced here: 74.5 us
  Pallas kernels  46.9 us (63%)
  starting transfers between devices  22.2 us (30%)
  waiting for transfers between devices  4.52 us (6%)
  between operations  0.83 us (1%)
    pallas_call x3, Pallas kernels, weight_grads(): local_call(functools.partial(weight_kernel, pieces=pieces, jobs=[job[1:3]...  16.9 us
    pallas_call x2, Pallas kernels, turned(): local_call(shared, 'turned', 7 * len(kinds), 0, 0, [SMEM] + [HBM] * len(w...  12 us
    ppermute x6, starting transfers between devices, along(): return lax.ppermute(value, 'tensor', pairs)  11.2 us
    ppermute x9, starting transfers between devices, across(): return lax.ppermute(value, ('expert', 'seq'), pairs)  10.7 us
    pallas_call x1, Pallas kernels, gate_up(): local_call(functools.partial(gate_up_kernel, pieces=pieces), 'gate_up', 1...  9.46 us
    pallas_call x1, Pallas kernels, middle(): local_call(functools.partial(middle_kernel, pieces=pieces, experts=expert...  6.07 us
    ppermute x3, waiting for transfers between devices, swap(): return lax.ppermute(value, 'expert', [(e, e ^ 1) for e in range(experts)])  2.28 us
  transfers between devices with their start and end apart: 18, of which 5 were waited for; matrix products, arithmetic and copies ran while one was open for 0% of the time, Pallas kernels for 51%

profile of v5, /device:TPU:0, one launch (start us, length us, event | category | flops | bytes accessed | tf_op | source)
XLA Modules:
  0.0 74.5 jit_solution(13826616794258995077)
XLA Ops:
  0.6 0.8 %first_pair.1.refs_0_ = bf16[32,1536]{1,0:T(8,128)(2,1)S(1)} custom-call(bf16[16,1536]{1,0:T(8,128)(2,1)} %x.1, bf16[16,1536]{1,0:T(8,128)(2,1)} %g.1), custom_call_target="tpu_custom_call" | custom-call | bytes 196608 | tf_op jit(solution)/shard_map/first_pair/pallas_call | solution.py:369
  1.5 3.1 %collective-permute-start = (bf16[32,1536]{1,0:T(8,128)(2,1)S(1)}, bf16[32,1536]{1,0:T(8,128)(2,1)S(1)}, u32[]{:S(2)}, u32[]{:S(2)}) collective-permute-start(bf16[32,1536]{1,0:T(8,128)(2,1)S(1)} %first_pair.1.refs_0_), channel_id=1, source_target_pairs={{0,1},{1,2},{2,3},{3,0},{4,5},{5,6},{6,7},{7,4},{8,9},{9,10},{10,1... | collective-permute-start | bytes 294920 | tf_op jit(solution)/shard_map/ppermute | solution.py:535
  4.6 2.6 %collective-permute-start.1 = (bf16[32,1536]{1,0:T(8,128)(2,1)S(1)}, bf16[32,1536]{1,0:T(8,128)(2,1)S(1)}, u32[]{:S(2)}, u32[]{:S(2)}) collective-permute-start(bf16[32,1536]{1,0:T(8,128)(2,1)S(1)} %first_pair.1.refs_0_), channel_id=1, source_target_pairs={{0,2},{1,3},{2,0},{3,1},{4,6},{5,7},{6,4},{7,5},{8,10},{9,11},{10,... | collective-permute-start | bytes 294920 | tf_op jit(solution)/shard_map/ppermute | solution.py:535
  7.1 1.3 %collective-permute-start.2 = (bf16[32,1536]{1,0:T(8,128)(2,1)S(1)}, bf16[32,1536]{1,0:T(8,128)(2,1)S(1)}, u32[]{:S(2)}, u32[]{:S(2)}) collective-permute-start(bf16[32,1536]{1,0:T(8,128)(2,1)S(1)} %first_pair.1.refs_0_), channel_id=1, source_target_pairs={{0,3},{1,0},{2,1},{3,2},{4,7},{5,4},{6,5},{7,6},{8,11},{9,8},{10,9... | collective-permute-start | bytes 294920 | tf_op jit(solution)/shard_map/ppermute | solution.py:535
  8.6 3.9 %turned.2 = (bf16[1536,1024]{1,0:T(8,128)(2,1)S(1)}, bf16[1536,1024]{1,0:T(8,128)(2,1)S(1)}) custom-call(s32[2]{0:T(128)S(1)} %pad_add_fusion.place, bf16[1,1024,6144]{2,1,0:T(8,128)(2,1)} %refs_1_.1), custom_call_target="tpu_custom_call" | custom-call | tf_op jit(solution)/shard_map/turned/pallas_call | solution.py:132
  12.5 1.2 %collective-permute-done.1.refs_2_ = bf16[32,1536]{1,0:T(8,128)(2,1)S(1)} collective-permute-done((bf16[32,1536]{1,0:T(8,128)(2,1)S(1)}, bf16[32,1536]{1,0:T(8,128)(2,1)S(1)}, u32[]{:S(2)}, u32[]{:S(2)}) %collective-permute-start.1) | collective-permute-done | bytes 98336 | tf_op jit(solution)/shard_map/ppermute | solution.py:535
  13.9 1.6 %collective-permute-start.6 = (bf16[16,6272]{1,0:T(8,128)(2,1)S(1)}, bf16[16,6272]{1,0:T(8,128)(2,1)S(1)}, u32[]{:S(2)}, u32[]{:S(2)}) collective-permute-start(bf16[16,6272]{1,0:T(8,128)(2,1)S(1)} %get-tuple-element.41.refs_0_), channel_id=1, source_target_pairs={{0,16},{4,20},{8,24},{12,28},{16,0},{20,4},{24,8},{28,12},{1,17},{... | collective-permute-start | bytes 602120 | tf_op jit(solution)/shard_map/ppermute | solution.py:543
  15.5 1.5 %collective-permute-start.7 = (bf16[16,6272]{1,0:T(8,128)(2,1)S(1)}, bf16[16,6272]{1,0:T(8,128)(2,1)S(1)}, u32[]{:S(2)}, u32[]{:S(2)}) collective-permute-start(bf16[16,6272]{1,0:T(8,128)(2,1)S(1)} %get-tuple-element.41.refs_0_), channel_id=1, source_target_pairs={{0,4},{4,0},{8,12},{12,8},{16,20},{20,16},{24,28},{28,24},{1,5},{5... | collective-permute-start | bytes 602120 | tf_op jit(solution)/shard_map/ppermute | solution.py:543
  17.5 8.0 %turned.3 = (bf16[1024,1536]{1,0:T(8,128)(2,1)S(1)}, bf16[1024,1536]{1,0:T(8,128)(2,1)S(1)}, bf16[1024,1536]{1,0:T(8,128)(2,1)S(1)}, bf16[1024,1536]{1,0:T(8,128...) custom-call(s32[2]{0:T(128)S(1)} %pad_add_fusion.place, bf16[1,6144,1024]{2,1,0:T(8,128)(2,1)} %refs_0_.3, ...), custom_call_target="tpu_custom_call" | custom-call | tf_op jit(solution)/shard_map/turned/pallas_call | solution.py:132
  26.4 1.3 %collective-permute-start.3 = (bf16[16,6144]{1,0:T(8,128)(2,1)S(1)}, bf16[16,6144]{1,0:T(8,128)(2,1)S(1)}, u32[]{:S(2)}, u32[]{:S(2)}) collective-permute-start(bf16[16,6144]{1,0:T(8,128)(2,1)S(1)} %get-tuple-element.40.refs_0_), channel_id=1, source_target_pairs={{0,16},{4,20},{8,24},{12,28},{16,0},{20,4},{24,8},{28,12},{1,17},{... | collective-permute-start | bytes 589832 | tf_op jit(solution)/shard_map/ppermute | solution.py:543
  27.7 1.1 %collective-permute-start.4 = (bf16[16,6144]{1,0:T(8,128)(2,1)S(1)}, bf16[16,6144]{1,0:T(8,128)(2,1)S(1)}, u32[]{:S(2)}, u32[]{:S(2)}) collective-permute-start(bf16[16,6144]{1,0:T(8,128)(2,1)S(1)} %get-tuple-element.40.refs_0_), channel_id=1, source_target_pairs={{0,4},{4,0},{8,12},{12,8},{16,20},{20,16},{24,28},{28,24},{1,5},{5... | collective-permute-start | bytes 589832 | tf_op jit(solution)/shard_map/ppermute | solution.py:543
  28.8 1.2 %collective-permute-start.5 = (bf16[16,6144]{1,0:T(8,128)(2,1)S(1)}, bf16[16,6144]{1,0:T(8,128)(2,1)S(1)}, u32[]{:S(2)}, u32[]{:S(2)}) collective-permute-start(bf16[16,6144]{1,0:T(8,128)(2,1)S(1)} %get-tuple-element.40.refs_0_), channel_id=1, source_target_pairs={{0,20},{4,16},{8,28},{12,24},{16,4},{20,0},{24,12},{28,8},{1,21},{... | collective-permute-start | bytes 589832 | tf_op jit(solution)/shard_map/ppermute | solution.py:543
  30.0 9.5 %gate_up.1 = (f32[128,1024]{1,0:T(8,128)S(1)}, f32[128,1024]{1,0:T(8,128)S(1)}, f32[128,128]{1,0:T(8,128)S(1)}, bf16[1024,1536]{1,0:T(8,128)(2,1)S(1)}, bf16[102...) custom-call(s32[2]{0:T(128)S(1)} %pad_add_fusion.place, ...), custom_call_target="tpu_custom_call" | custom-call | tf_op jit(solution)/shard_map/gate_up/pallas_call | solution.py:197
  39.6 2.3 %collective-permute-done.10.go.far = bf16[64,6144]{1,0:T(8,128)(2,1)S(1)} collective-permute-done((bf16[64,6144]{1,0:T(8,128)(2,1)S(1)}, bf16[64,6144]{1,0:T(8,128)(2,1)S(1)}, u32[]{:S(2)}, u32[]{:S(2)}) %collective-permute-start.10) | collective-permute-done | bytes 786464 | tf_op jit(solution)/shard_map/ppermute | solution.py:546
  41.9 6.1 %middle.1 = (bf16[64,6272]{1,0:T(8,128)(2,1)S(1)}, bf16[64,6272]{1,0:T(8,128)(2,1)S(1)}, bf16[128,1024]{1,0:T(8,128)(2,1)S(1)}, bf16[128,1024]{1,0:T(8,128)(2,1)S(1)}, bf16[128,1024]{1,0:T(8,128)(2,1)S(1)}) custom-call(s32[2]{0:T(128)S(1)} %pad_add_fusion.place, bf16[64,6144]{1,0:T(8,128)(2,1)S(1)} %stacked.3.gp.near, ...), custom_call_target="tpu_custom_call" | custom-call | tf_op jit(solution)/shard_map/middle/pallas_call | solution.py:265
  48.2 2.2 %weight_grads.3.refs_2_ = bf16[1,6144,1024]{2,1,0:T(8,128)(2,1)} custom-call(s32[2]{0:T(128)S(1)} %pad_add_fusion.place, bf16[64,6272]{1,0:T(8,128)(2,1)S(1)} %stacked.2.xp.near, bf16[64,6272]{1,0:T(8,128)(2,1)S(1)} %collective-permute-done.9.xo.far, bf16[128,1024]{1,0:T(8,128)(2,1)S(1)} %get-tuple-element.68.refs_0_), custom_call_target="tpu_custom_call" | custom-call | flops 268435456 | bytes 2097152 | tf_op jit(solution)/shard_map/weight_grads/pallas_call | solution.py:308
  50.8 1.3 %collective-permute-start.12 = (bf16[16,6272]{1,0:T(8,128)(2,1)S(1)}, bf16[16,6272]{1,0:T(8,128)(2,1)S(1)}, u32[]{:S(2)}, u32[]{:S(2)}) collective-permute-start(bf16[16,6272]{1,0:T(8,128)(2,1)S(1)} %get-tuple-element.59), channel_id=1, source_target_pairs={{0,16},{4,20},{8,24},{12,28},{16,0},{20,4},{24,8},{28,12},{1,17},{... | collective-permute-start | bytes 602120 | tf_op jit(solution)/shard_map/ppermute | solution.py:543
  52.1 1.1 %collective-permute-start.13 = (bf16[16,6272]{1,0:T(8,128)(2,1)S(1)}, bf16[16,6272]{1,0:T(8,128)(2,1)S(1)}, u32[]{:S(2)}, u32[]{:S(2)}) collective-permute-start(bf16[16,6272]{1,0:T(8,128)(2,1)S(1)} %get-tuple-element.60), channel_id=1, source_target_pairs={{0,4},{4,0},{8,12},{12,8},{16,20},{20,16},{24,28},{28,24},{1,5},{5... | collective-permute-start | bytes 602120 | tf_op jit(solution)/shard_map/ppermute | solution.py:543
  53.2 1.2 %collective-permute-start.14 = (bf16[16,6272]{1,0:T(8,128)(2,1)S(1)}, bf16[16,6272]{1,0:T(8,128)(2,1)S(1)}, u32[]{:S(2)}, u32[]{:S(2)}) collective-permute-start(bf16[16,6272]{1,0:T(8,128)(2,1)S(1)} %get-tuple-element.61), channel_id=1, source_target_pairs={{0,20},{4,16},{8,28},{12,24},{16,4},{20,0},{24,12},{28,8},{1,21},{... | collective-permute-start | bytes 602120 | tf_op jit(solution)/shard_map/ppermute | solution.py:543
  54.4 8.9 %weight_grads.4 = (bf16[1,6144,1024]{2,1,0:T(8,128)(2,1)}, bf16[1,6144,1024]{2,1,0:T(8,128)(2,1)}) custom-call(s32[2]{0:T(128)S(1)} %pad_add_fusion.place, bf16[64,6272]{1,0:T(8,128)(2,1)S(1)} %stacked.2.xp.near, bf16[64,6272]{1,0:T(8,128)(2,1)S(1)} %collective-permute-done.9.xo.far, ...), custom_call_target="tpu_custom_call", output_to_operand_aliasing={{0}: (5, {})} | custom-call | flops 2952790016 | bytes 23068672 | tf_op jit(solution)/shard_map/weight_grads/pallas_call | solution.py:308
  63.6 3.2 %collective-permute-start.15 = (bf16[16,1664]{1,0:T(8,128)(2,1)S(1)}, bf16[16,1664]{1,0:T(8,128)(2,1)S(1)}, u32[]{:S(2)}, u32[]{:S(2)}) collective-permute-start(bf16[16,1664]{1,0:T(8,128)(2,1)S(1)} %get-tuple-element.63), channel_id=1, source_target_pairs={{0,3},{1,0},{2,1},{3,2},{4,7},{5,4},{6,5},{7,6},{8,11},{9,8},{10,9... | collective-permute-start | bytes 159752 | tf_op jit(solution)/shard_map/ppermute | solution.py:535
  66.7 1.0 %collective-permute-start.16 = (bf16[16,1664]{1,0:T(8,128)(2,1)S(1)}, bf16[16,1664]{1,0:T(8,128)(2,1)S(1)}, u32[]{:S(2)}, u32[]{:S(2)}) collective-permute-start(bf16[16,1664]{1,0:T(8,128)(2,1)S(1)} %get-tuple-element.64), channel_id=1, source_target_pairs={{0,2},{1,3},{2,0},{3,1},{4,6},{5,7},{6,4},{7,5},{8,10},{9,11},{10,... | collective-permute-start | bytes 159752 | tf_op jit(solution)/shard_map/ppermute | solution.py:535
  67.7 5.8 %weight_grads.5 = bf16[1,1024,6144]{2,1,0:T(8,128)(2,1)} custom-call(s32[2]{0:T(128)S(1)} %pad_add_fusion.place, bf16[64,6144]{1,0:T(8,128)(2,1)S(1)} %stacked.3.gp.near, bf16[64,6144]{1,0:T(8,128)(2,1)S(1)} %collective-permute-done.10.go.far, bf16[128,1024]{1,0:T(8,128)(2,1)S(1)} %get-tuple-element.72.refs_0_), custom_call_target="tpu_custom_call" | custom-call | flops 1610612736 | bytes 12582912 | tf_op jit(solution)/shard_map/weight_grads/pallas_call | solution.py:308
  73.7 0.9 %line_sums.1 = (bf16[16,1536]{1,0:T(8,128)(2,1)}, bf16[2,16]{1,0:T(2,128)(2,1)}) custom-call(bf16[16,1664]{1,0:T(8,128)(2,1)S(1)} %get-tuple-element.62.refs_0_, bf16[16,1664]{1,0:T(8,128)(2,1)S(1)} %collective-permute-done.15.refs_1_, bf16[16,1664]{1,0:T(8,128)(2,1)S(1)} %collective-permute-done.16.refs_2_, ...), custom_call_target="tpu_custom_call" | custom-call | bytes 212992 | tf_op jit(solution)/shard_map/line_sums/pallas_call | solution.py:511
  (31 shorter events, 2.8 us)
Async XLA Ops:
  1.5 11.0 %collective-permute-start = (bf16[32,1536]{1,0:T(8,128)(2,1)S(1)}, bf16[32,1536]{1,0:T(8,128)(2,1)S(1)}, u32[]{:S(2)}, u32[]{:S(2)}) collective-permute-start(bf16[32,1536]{1,0:T(8,128)(2,1)S(1)} %first_pair.1.refs_0_), channel_id=1, source_target_pairs={{0,1},{1,2},{2,3},{3,0},{4,5},{5,6},{6,7},{7,4},{8,9},{9,10},{10,1... | collective-permute-start | bytes 294920 | tf_op jit(solution)/shard_map/ppermute | solution.py:535
  4.6 9.2 %collective-permute-start.1 = (bf16[32,1536]{1,0:T(8,128)(2,1)S(1)}, bf16[32,1536]{1,0:T(8,128)(2,1)S(1)}, u32[]{:S(2)}, u32[]{:S(2)}) collective-permute-start(bf16[32,1536]{1,0:T(8,128)(2,1)S(1)} %first_pair.1.refs_0_), channel_id=1, source_target_pairs={{0,2},{1,3},{2,0},{3,1},{4,6},{5,7},{6,4},{7,5},{8,10},{9,11},{10,... | collective-permute-start | bytes 294920 | tf_op jit(solution)/shard_map/ppermute | solution.py:535
  7.1 6.6 %collective-permute-start.2 = (bf16[32,1536]{1,0:T(8,128)(2,1)S(1)}, bf16[32,1536]{1,0:T(8,128)(2,1)S(1)}, u32[]{:S(2)}, u32[]{:S(2)}) collective-permute-start(bf16[32,1536]{1,0:T(8,128)(2,1)S(1)} %first_pair.1.refs_0_), channel_id=1, source_target_pairs={{0,3},{1,0},{2,1},{3,2},{4,7},{5,4},{6,5},{7,6},{8,11},{9,8},{10,9... | collective-permute-start | bytes 294920 | tf_op jit(solution)/shard_map/ppermute | solution.py:535
  8.6 5.2 %copy-start = (s32[16,2]{0,1:T(2,128)S(1)}, s32[16,2]{0,1:T(2,128)}, u32[]{:S(2)}) copy-start(s32[16,2]{0,1:T(2,128)} %param.9) | copy-start | bytes 388
  8.6 5.2 %copy-start.1 = (bf16[16,2]{0,1:T(2,128)(2,1)S(1)}, bf16[16,2]{0,1:T(2,128)(2,1)}, u32[]{:S(2)}) copy-start(bf16[16,2]{0,1:T(2,128)(2,1)} %param.10) | copy-start | bytes 196
  13.9 11.6 %collective-permute-start.6 = (bf16[16,6272]{1,0:T(8,128)(2,1)S(1)}, bf16[16,6272]{1,0:T(8,128)(2,1)S(1)}, u32[]{:S(2)}, u32[]{:S(2)}) collective-permute-start(bf16[16,6272]{1,0:T(8,128)(2,1)S(1)} %get-tuple-element.41.refs_0_), channel_id=1, source_target_pairs={{0,16},{4,20},{8,24},{12,28},{16,0},{20,4},{24,8},{28,12},{1,17},{... | collective-permute-start | bytes 602120 | tf_op jit(solution)/shard_map/ppermute | solution.py:543
  15.5 10.8 %collective-permute-start.7 = (bf16[16,6272]{1,0:T(8,128)(2,1)S(1)}, bf16[16,6272]{1,0:T(8,128)(2,1)S(1)}, u32[]{:S(2)}, u32[]{:S(2)}) collective-permute-start(bf16[16,6272]{1,0:T(8,128)(2,1)S(1)} %get-tuple-element.41.refs_0_), channel_id=1, source_target_pairs={{0,4},{4,0},{8,12},{12,8},{16,20},{20,16},{24,28},{28,24},{1,5},{5... | collective-permute-start | bytes 602120 | tf_op jit(solution)/shard_map/ppermute | solution.py:543
  17.0 9.3 %collective-permute-start.8 = (bf16[16,6272]{1,0:T(8,128)(2,1)S(1)}, bf16[16,6272]{1,0:T(8,128)(2,1)S(1)}, u32[]{:S(2)}, u32[]{:S(2)}) collective-permute-start(bf16[16,6272]{1,0:T(8,128)(2,1)S(1)} %get-tuple-element.41.refs_0_), channel_id=1, source_target_pairs={{0,20},{4,16},{8,28},{12,24},{16,4},{20,0},{24,12},{28,8},{1,21},{... | collective-permute-start | bytes 602120 | tf_op jit(solution)/shard_map/ppermute | solution.py:543
  26.4 3.6 %collective-permute-start.9 = (bf16[64,6272]{1,0:T(8,128)(2,1)S(1)}, bf16[64,6272]{1,0:T(8,128)(2,1)S(1)}, u32[]{:S(2)}, u32[]{:S(2)}) collective-permute-start(bf16[64,6272]{1,0:T(8,128)(2,1)S(1)} %stacked.2.xp.near), channel_id=1, source_target_pairs={{0,8},{8,0},{16,24},{24,16},{1,9},{9,1},{17,25},{25,17},{2,10},{10... | collective-permute-start | bytes 2408456 | tf_op jit(solution)/shard_map/ppermute | solution.py:546
  26.4 13.0 %collective-permute-start.3 = (bf16[16,6144]{1,0:T(8,128)(2,1)S(1)}, bf16[16,6144]{1,0:T(8,128)(2,1)S(1)}, u32[]{:S(2)}, u32[]{:S(2)}) collective-permute-start(bf16[16,6144]{1,0:T(8,128)(2,1)S(1)} %get-tuple-element.40.refs_0_), channel_id=1, source_target_pairs={{0,16},{4,20},{8,24},{12,28},{16,0},{20,4},{24,8},{28,12},{1,17},{... | collective-permute-start | bytes 589832 | tf_op jit(solution)/shard_map/ppermute | solution.py:543
  27.7 11.7 %collective-permute-start.4 = (bf16[16,6144]{1,0:T(8,128)(2,1)S(1)}, bf16[16,6144]{1,0:T(8,128)(2,1)S(1)}, u32[]{:S(2)}, u32[]{:S(2)}) collective-permute-start(bf16[16,6144]{1,0:T(8,128)(2,1)S(1)} %get-tuple-element.40.refs_0_), channel_id=1, source_target_pairs={{0,4},{4,0},{8,12},{12,8},{16,20},{20,16},{24,28},{28,24},{1,5},{5... | collective-permute-start | bytes 589832 | tf_op jit(solution)/shard_map/ppermute | solution.py:543
  28.8 10.7 %collective-permute-start.5 = (bf16[16,6144]{1,0:T(8,128)(2,1)S(1)}, bf16[16,6144]{1,0:T(8,128)(2,1)S(1)}, u32[]{:S(2)}, u32[]{:S(2)}) collective-permute-start(bf16[16,6144]{1,0:T(8,128)(2,1)S(1)} %get-tuple-element.40.refs_0_), channel_id=1, source_target_pairs={{0,20},{4,16},{8,28},{12,24},{16,4},{20,0},{24,12},{28,8},{1,21},{... | collective-permute-start | bytes 589832 | tf_op jit(solution)/shard_map/ppermute | solution.py:543
  39.5 2.4 %collective-permute-start.10 = (bf16[64,6144]{1,0:T(8,128)(2,1)S(1)}, bf16[64,6144]{1,0:T(8,128)(2,1)S(1)}, u32[]{:S(2)}, u32[]{:S(2)}) collective-permute-start(bf16[64,6144]{1,0:T(8,128)(2,1)S(1)} %stacked.3.gp.near), channel_id=1, source_target_pairs={{0,8},{8,0},{16,24},{24,16},{1,9},{9,1},{17,25},{25,17},{2,10},{10... | collective-permute-start | bytes 2359304 | tf_op jit(solution)/shard_map/ppermute | solution.py:546
  48.0 2.4 %collective-permute-start.11 = (bf16[64,6272]{1,0:T(8,128)(2,1)S(1)}, bf16[64,6272]{1,0:T(8,128)(2,1)S(1)}, u32[]{:S(2)}, u32[]{:S(2)}) collective-permute-start(bf16[64,6272]{1,0:T(8,128)(2,1)S(1)} %get-tuple-element.57), channel_id=1, source_target_pairs={{0,8},{8,0},{16,24},{24,16},{1,9},{9,1},{17,25},{25,17},{2,10},{10... | collective-permute-start | bytes 2408456 | tf_op jit(solution)/shard_map/ppermute | solution.py:546
  50.8 12.5 %collective-permute-start.12 = (bf16[16,6272]{1,0:T(8,128)(2,1)S(1)}, bf16[16,6272]{1,0:T(8,128)(2,1)S(1)}, u32[]{:S(2)}, u32[]{:S(2)}) collective-permute-start(bf16[16,6272]{1,0:T(8,128)(2,1)S(1)} %get-tuple-element.59), channel_id=1, source_target_pairs={{0,16},{4,20},{8,24},{12,28},{16,0},{20,4},{24,8},{28,12},{1,17},{... | collective-permute-start | bytes 602120 | tf_op jit(solution)/shard_map/ppermute | solution.py:543
  52.1 11.2 %collective-permute-start.13 = (bf16[16,6272]{1,0:T(8,128)(2,1)S(1)}, bf16[16,6272]{1,0:T(8,128)(2,1)S(1)}, u32[]{:S(2)}, u32[]{:S(2)}) collective-permute-start(bf16[16,6272]{1,0:T(8,128)(2,1)S(1)} %get-tuple-element.60), channel_id=1, source_target_pairs={{0,4},{4,0},{8,12},{12,8},{16,20},{20,16},{24,28},{28,24},{1,5},{5... | collective-permute-start | bytes 602120 | tf_op jit(solution)/shard_map/ppermute | solution.py:543
  53.2 10.2 %collective-permute-start.14 = (bf16[16,6272]{1,0:T(8,128)(2,1)S(1)}, bf16[16,6272]{1,0:T(8,128)(2,1)S(1)}, u32[]{:S(2)}, u32[]{:S(2)}) collective-permute-start(bf16[16,6272]{1,0:T(8,128)(2,1)S(1)} %get-tuple-element.61), channel_id=1, source_target_pairs={{0,20},{4,16},{8,28},{12,24},{16,4},{20,0},{24,12},{28,8},{1,21},{... | collective-permute-start | bytes 602120 | tf_op jit(solution)/shard_map/ppermute | solution.py:543
  63.6 9.9 %collective-permute-start.15 = (bf16[16,1664]{1,0:T(8,128)(2,1)S(1)}, bf16[16,1664]{1,0:T(8,128)(2,1)S(1)}, u32[]{:S(2)}, u32[]{:S(2)}) collective-permute-start(bf16[16,1664]{1,0:T(8,128)(2,1)S(1)} %get-tuple-element.63), channel_id=1, source_target_pairs={{0,3},{1,0},{2,1},{3,2},{4,7},{5,4},{6,5},{7,6},{8,11},{9,8},{10,9... | collective-permute-start | bytes 159752 | tf_op jit(solution)/shard_map/ppermute | solution.py:535
  66.7 6.8 %collective-permute-start.16 = (bf16[16,1664]{1,0:T(8,128)(2,1)S(1)}, bf16[16,1664]{1,0:T(8,128)(2,1)S(1)}, u32[]{:S(2)}, u32[]{:S(2)}) collective-permute-start(bf16[16,1664]{1,0:T(8,128)(2,1)S(1)} %get-tuple-element.64), channel_id=1, source_target_pairs={{0,2},{1,3},{2,0},{3,1},{4,6},{5,7},{6,4},{7,5},{8,10},{9,11},{10,... | collective-permute-start | bytes 159752 | tf_op jit(solution)/shard_map/ppermute | solution.py:535
  67.7 5.9 %collective-permute-start.17 = (bf16[16,1664]{1,0:T(8,128)(2,1)S(1)}, bf16[16,1664]{1,0:T(8,128)(2,1)S(1)}, u32[]{:S(2)}, u32[]{:S(2)}) collective-permute-start(bf16[16,1664]{1,0:T(8,128)(2,1)S(1)} %get-tuple-element.65), channel_id=1, source_target_pairs={{0,1},{1,2},{2,3},{3,0},{4,5},{5,6},{6,7},{7,4},{8,9},{9,10},{10,1... | collective-permute-start | bytes 159752 | tf_op jit(solution)/shard_map/ppermute | solution.py:535
